TPU v7x, 512 devices: a whole 4x8x8 slice. The times are simulated.
512 devices in a mesh: dp: 8 (over y), ctx: 64 (over z, x, core).
Axes of the slice: x: 4, y: 8, z: 8, core: 2. Of those that a mesh axis runs over, the one named last changes fastest.
Arguments:
- queries: bfloat16 [8, 8192, 512], P('dp', 'ctx'), may hold values from -4 to 4
- keys: bfloat16 [8, 8192, 512], P('dp', 'ctx'), may hold values from -4 to 4
- values: bfloat16 [8, 8192, 512], P('dp', 'ctx'), may hold values from -6 to 6
- upstream: bfloat16 [8, 8192, 512], P('dp', 'ctx'), may hold values from -6 to 6
- query_map: bfloat16 [8, 64, 64], replicated, may hold values from -0.75 to 0.75
- key_map: bfloat16 [8, 64, 64], replicated, may hold values from -0.75 to 0.75
Outputs:
- grad_queries: bfloat16 [8, 8192, 512], P('dp', 'ctx')
- grad_keys: bfloat16 [8, 8192, 512], P('dp', 'ctx')
- grad_values: bfloat16 [8, 8192, 512], P('dp', 'ctx')
- grad_query_map: bfloat16 [8, 64, 64], replicated
- grad_key_map: bfloat16 [8, 64, 64], replicated
All inputs are finite; a program needn't handle non-finite values.
Results may differ from a plain program's by a relative error of at most 0.0015.
Values sent between devices are 32-bit elements; how exact they have to be, the bound alone decides.
No kernel may reach another device: no remote copies, remote signals or barrier semaphores. Data moves between devices by JAX's collectives and lax.ppermute only.
A program may use at most 64 MiB of HBM per device.

v0:
```python
import jax
import jax.numpy as jnp
from jax import lax
from jax.sharding import PartitionSpec as P


def entering(value, axis, combine, identity, reverse):
    count, index = (lax.axis_size(axis), lax.axis_index(axis))
    everything = jax.tree.map(lambda part: lax.all_gather(part, axis), value)
    start = jax.tree.map(
        lambda part, zero: jnp.broadcast_to(jnp.asarray(zero, part.dtype), part.shape),
        value,
        identity,
    )

    def hop(k, before):
        at = count - 1 - k if reverse else k
        reached = at > index if reverse else at < index
        new = combine(before, jax.tree.map(lambda part: part[at], everything))
        return jax.tree.map(lambda a, b: jnp.where(reached, a, b), new, before)

    return lax.fori_loop(0, count, hop, start)


def feature(z):
    up = jnp.exp(z)
    down = jnp.exp(-z)
    return jnp.concatenate(
        [up / jnp.sum(up, -1, keepdims=True), down / jnp.sum(down, -1, keepdims=True)], -1
    )


def feature_back(z, grad):
    width = z.shape[-1]
    up = jnp.exp(z)
    down = jnp.exp(-z)
    plus = up / jnp.sum(up, -1, keepdims=True)
    minus = down / jnp.sum(down, -1, keepdims=True)
    first = grad[..., :width]
    second = grad[..., width:]
    return plus * (first - jnp.sum(plus * first, -1, keepdims=True)) - minus * (
        second - jnp.sum(minus * second, -1, keepdims=True)
    )


def add_pair(earlier, later):
    return (earlier[0] + later[0], earlier[1] + later[1])


def per_device(queries, keys, values, upstream, query_map, key_map):
    hp = lax.Precision.HIGHEST
    heads = query_map.shape[0]
    width = query_map.shape[1]
    rows = queries.shape[1]
    q_heads = queries.reshape(rows, heads, width)
    k_heads = keys.reshape(rows, heads, width)
    zq = jnp.einsum("thd,hde->hte", q_heads, query_map, preferred_element_type=jnp.float32)
    zk = jnp.einsum("thd,hde->hte", k_heads, key_map, preferred_element_type=jnp.float32)
    qf = feature(zq)
    kf = feature(zk)
    vals = jnp.transpose(values.reshape(rows, heads, width), (1, 0, 2)).astype(jnp.float32)
    grads = jnp.transpose(upstream.reshape(rows, heads, width), (1, 0, 2)).astype(jnp.float32)
    feats = qf.shape[-1]
    local_kv = jnp.einsum("htf,hte->hfe", kf, vals, precision=hp)
    local_ks = jnp.sum(kf, 1)
    zero_pair = (
        jnp.zeros((heads, feats, width), jnp.float32),
        jnp.zeros((heads, feats), jnp.float32),
    )
    state, ksum = entering((local_kv, local_ks), "ctx", add_pair, zero_pair, False)
    mask = jnp.tril(jnp.ones((rows, rows), jnp.float32))
    scores = jnp.einsum("htf,hsf->hts", qf, kf, precision=hp) * mask
    numer = jnp.einsum("htf,hfe->hte", qf, state, precision=hp) + jnp.einsum(
        "hts,hse->hte", scores, vals, precision=hp
    )
    denom = jnp.einsum("htf,hf->ht", qf, ksum, precision=hp) + jnp.sum(scores, -1)
    attended = numer / denom[..., None]
    dnum = grads / denom[..., None]
    dden = -jnp.sum(grads * attended, -1) / denom
    local_ds = jnp.einsum("htf,hte->hfe", qf, dnum, precision=hp)
    local_dz = jnp.einsum("htf,ht->hf", qf, dden, precision=hp)
    later_ds, later_dz = entering((local_ds, local_dz), "ctx", add_pair, zero_pair, True)
    mixing = mask * (jnp.einsum("hte,hse->hts", dnum, vals, precision=hp) + dden[..., None])
    grad_qf = (
        jnp.einsum("hte,hfe->htf", dnum, state, precision=hp)
        + dden[..., None] * ksum[:, None, :]
        + jnp.einsum("hts,hsf->htf", mixing, kf, precision=hp)
    )
    grad_kf = (
        jnp.einsum("hts,htf->hsf", mixing, qf, precision=hp)
        + jnp.einsum("hse,hfe->hsf", vals, later_ds, precision=hp)
        + later_dz[:, None, :]
    )
    grad_v = jnp.einsum("hts,hte->hse", scores, dnum, precision=hp) + jnp.einsum(
        "hsf,hfe->hse", kf, later_ds, precision=hp
    )
    dzq = feature_back(zq, grad_qf)
    dzk = feature_back(zk, grad_kf)
    qmap = query_map.astype(jnp.float32)
    kmap = key_map.astype(jnp.float32)
    grad_q = jnp.einsum("hte,hde->thd", dzq, qmap, precision=hp).reshape(1, rows, heads * width)
    grad_k = jnp.einsum("hte,hde->thd", dzk, kmap, precision=hp).reshape(1, rows, heads * width)
    grad_vv = jnp.transpose(grad_v, (1, 0, 2)).reshape(1, rows, heads * width)
    gq = jnp.einsum("thd,hte->hde", q_heads.astype(jnp.float32), dzq, precision=hp)
    gk = jnp.einsum("thd,hte->hde", k_heads.astype(jnp.float32), dzk, precision=hp)
    total_q, total_k = lax.psum((gq, gk), ("dp", "ctx"))
    scale = float(rows * lax.axis_size("ctx") * lax.axis_size("dp")) ** (-0.5)
    return (
        grad_q.astype(jnp.bfloat16),
        grad_k.astype(jnp.bfloat16),
        grad_vv.astype(jnp.bfloat16),
        (total_q * scale).astype(jnp.bfloat16),
        (total_k * scale).astype(jnp.bfloat16),
    )


def solution(mesh):
    in_specs = (
        P("dp", "ctx", None),
        P("dp", "ctx", None),
        P("dp", "ctx", None),
        P("dp", "ctx", None),
        P(),
        P(),
    )
    out_specs = (P("dp", "ctx", None), P("dp", "ctx", None), P("dp", "ctx", None), P(), P())
    return jax.shard_map(
        per_device, mesh=mesh, in_specs=in_specs, out_specs=out_specs, check_vma=False
    )
```

profile of v0, /device:TPU:1, one launch (start us, length us, event | category | flops | bytes accessed | tf_op | source)
XLA Modules:
  0.0 779.8 jit_solution(2666392582592079177)
XLA Ops:
  7.2 1.1 copy.69
  8.3 1.1 copy.72
  9.4 1.0 copy.74
  10.4 1.2 exponential_reduce_fusion
  12.1 1.3 fusion.12
  13.5 1.0 copy.71
  14.7 55.0 %all-gather.1 = f32[512,128]{1,0:T(8,128)} all-gather(f32[8,128]{1,0:T(8,128)S(1)} %fusion.11), channel_id=3, replica_groups=mesh['dp'=8,'ctx'=64] {'ctx'}, dimensions={0}, use_global_device_ids=true | all-gather | bytes 266240 | tf_op jit(solution)/shard_map/all_gather | solution.py:9
  70.4 1.0 fusion.27
  71.4 54.1 %all-gather.7.cloned.1.call-done = f32[512,128,64]{1,2,0:T(8,128)} async-done(((f32[8,128,64]{1,2,0:T(8,128)}), f32[512,128,64]{1,2,0:T(8,128)}) %all-gather.7.cloned.1.call-update) | async-done | bytes 16777232 | tf_op jit(solution)/shard_map/all_gather | solution.py:9
  125.5 132.9 %while.34 = (s32[]{:T(128)}, f32[8,128,64]{2,1,0:T(8,128)S(1)}, f32[8,128]{1,0:T(8,128)S(1)}, s32[]{:T(128)}, f32[64,8,128,64]{2,3,1,0:T(8,128)}, /*index=5*/f32[64,8,128]{2,1,0:T(8,128)}, s32[]{:T(128)}, s32[]{:T(128)}) while((s32[]{:T(128)}, f32[8,128,64]{2,1,0:T(8,128)S(1)}, f32[8,128]{1,0:T(8,128)S(1)}, s32[]{:T(128)}, ...), condition=%wide.region_6.7_spmd.clone, body=%wide.region_5.6_spmd.clone.sunk | while | flops 199684 | bytes 1847419 | solution.py:22
  130.4 1.0 constant_dynamic-slice_fusion.4
  134.5 1.0 constant_dynamic-slice_fusion.4
  138.7 1.0 constant_dynamic-slice_fusion.4
  140.8 1.0 constant_dynamic-slice_fusion.4
  142.8 1.0 constant_dynamic-slice_fusion.4
  147.0 1.0 constant_dynamic-slice_fusion.4
  149.1 1.0 constant_dynamic-slice_fusion.4
  151.2 1.0 constant_dynamic-slice_fusion.4
  161.5 1.0 constant_dynamic-slice_fusion.4
  163.6 1.0 constant_dynamic-slice_fusion.4
  165.7 1.0 constant_dynamic-slice_fusion.4
  167.8 1.0 constant_dynamic-slice_fusion.4
  176.1 1.0 constant_dynamic-slice_fusion.4
  178.2 1.0 constant_dynamic-slice_fusion.4
  196.9 1.0 constant_dynamic-slice_fusion.4
  201.0 1.0 constant_dynamic-slice_fusion.4
  207.2 1.0 constant_dynamic-slice_fusion.4
  213.5 1.0 constant_dynamic-slice_fusion.4
  215.5 1.0 constant_dynamic-slice_fusion.4
  221.8 1.0 constant_dynamic-slice_fusion.4
  223.9 1.0 constant_dynamic-slice_fusion.4
  225.9 1.0 constant_dynamic-slice_fusion.4
  230.1 1.0 constant_dynamic-slice_fusion.4
  232.2 1.0 constant_dynamic-slice_fusion.4
  238.4 1.0 constant_dynamic-slice_fusion.4
  242.6 1.0 constant_dynamic-slice_fusion.4
  244.6 1.0 constant_dynamic-slice_fusion.4
  248.8 1.0 constant_dynamic-slice_fusion.4
  252.9 1.0 constant_dynamic-slice_fusion.4
  255.0 1.0 constant_dynamic-slice_fusion.4
  259.0 1.8 fusion.15
  260.9 1.0 fusion.16
  262.3 1.3 fusion.1
  267.0 45.9 %all-gather.3 = f32[512,128]{1,0:T(8,128)} all-gather(f32[8,128]{1,0:T(8,128)S(1)} %bitcast.99), channel_id=5, replica_groups=mesh['dp'=8,'ctx'=64] {'ctx'}, dimensions={0}, use_global_device_ids=true | all-gather | bytes 266240 | tf_op jit(solution)/shard_map/all_gather | solution.py:9
  312.8 1.9 convolution_bitcast_fusion.2
  314.8 48.8 %all-gather.9.cloned.1.call-done = f32[512,128,64]{1,2,0:T(8,128)} async-done(((f32[8,128,64]{1,2,0:T(8,128)}), f32[512,128,64]{1,2,0:T(8,128)}) %all-gather.9.cloned.1.call-update) | async-done | bytes 16777232 | tf_op jit(solution)/shard_map/all_gather | solution.py:9
  363.6 133.2 %while.35 = (s32[]{:T(128)}, f32[8,128,64]{2,1,0:T(8,128)S(1)}, f32[8,128]{1,0:T(8,128)S(1)}, s32[]{:T(128)}, f32[64,8,128,64]{2,3,1,0:T(8,128)}, /*index=5*/f32...) while((s32[]{:T(128)}, f32[8,128,64]{2,1,0:T(8,128)S(1)}, ...), condition=%wide.region_12.13_spmd.clone, body=%wide.region_11.12_spmd.clone.sunk | while | flops 199688 | bytes 1847481 | solution.py:22
  364.3 1.0 constant_dynamic-slice_fusion.5
  376.8 1.0 constant_dynamic-slice_fusion.5
  378.9 1.0 constant_dynamic-slice_fusion.5
  383.0 1.0 constant_dynamic-slice_fusion.5
  393.4 1.0 constant_dynamic-slice_fusion.5
  395.5 1.0 constant_dynamic-slice_fusion.5
  397.6 1.0 constant_dynamic-slice_fusion.5
  399.7 1.0 constant_dynamic-slice_fusion.5
  401.8 1.0 constant_dynamic-slice_fusion.5
  496.8 1.0 fusion.10
  498.2 1.1 fusion.4
  500.1 2.2 fusion
  502.5 1.0 convolution_bitcast_fusion.1
  503.5 1.2 convolution_convert_fusion
  505.5 264.3 %all-reduce.3.cloned.1.call-done = (f32[8,64,64]{1,2,0:T(8,128)}, f32[8,64,64]{1,2,0:T(8,128)}) async-done(((f32[8,64,64]{1,2,0:T(8,128)}, f32[8,64,64]{1,2,0:T(8,128)}), (f32[8,64,64]{1,2,0:T(8,128)}, f32[8,64,64]{1,2,0:T(8,128)})) %all-reduce.3.cloned.1.call-update) | async-done | bytes 262160 | tf_op jit(solution)/shard_map/psum | solution.py:106
  769.8 1.0 multiply_convert_fusion.1
  771.5 1.0 multiply_convert_fusion
  (513 shorter events, 232.4 us)
Async XLA Ops:
  7.2 4.4 copy-start
  7.2 118.4 %all-gather.7.cloned.1.call-start = ((), (), s32[]{:S(2)}) async-start(), calls=%async_computation | async-start | bytes 17039360 | tf_op jit(solution)/shard_map/all_gather | solution.py:9
  8.3 3.6 copy-start.2
  13.4 350.2 %all-gather.9.cloned.1.call-start = ((), (), s32[]{:S(2)}) async-start(), calls=%async_computation.1 | async-start | bytes 17039360 | tf_op jit(solution)/shard_map/all_gather | solution.py:9
  69.8 0.6 copy-start.3
  260.8 508.9 %all-reduce.3.cloned.1.call-start = ((), (), s32[]{:S(2)}) async-start(), calls=%async_computation.2 | async-start | bytes 1048576 | tf_op jit(solution)/shard_map/psum | solution.py:106
  263.6 1.4 copy-start.1
Sparse Core Ops, SparseCore 0:
  13.6 111.9 all-gather.6
  261.0 102.6 all-gather.8
  503.7 266.0 all-reduce.2
where the time goes:
time: 788 us; the launch traced here: 780 us
  waiting for transfers between devices  367 us (47%)
  local copies, waits for them, and re-layouts  158 us (20%)
  other arithmetic  114 us (14%)
  blocking collectives  101 us (13%)
  matrix products  20.1 us (3%)
  between operations  14 us (2%)
    psum x1, waiting for transfers between devices, per_device(): total_q, total_k = lax.psum((gq, gk), ('dp', 'ctx'))  264 us
    dynamic_slice x256, local copies, waits for them, and re-layouts, hop(): new = combine(before, jax.tree.map(lambda part: part[at], everything))  149 us
    select_n x256, other arithmetic, hop(): return jax.tree.map(lambda a, b: jnp.where(reached, a, b), new, before)  111 us
    all_gather x2, waiting for transfers between devices, entering(): everything = jax.tree.map(lambda part: lax.all_gather(part, axis), value)  103 us
    all_gather x2, blocking collectives, entering(): everything = jax.tree.map(lambda part: lax.all_gather(part, axis), value)  101 us
  transfers between devices with their start and end apart: 3, of which 3 were waited for; matrix products, arithmetic and copies ran while one was open for 2% of the time, Pallas kernels for 0%

commit v1 on v0

v1 whole, which is shorter than its diff:
```python
import functools

import jax
import jax.numpy as jnp
import numpy as np
from jax import lax
from jax.experimental import pallas as pl
from jax.experimental.pallas import tpu as pltpu
from jax.sharding import Mesh, PartitionSpec as P

F32 = jnp.float32
BF16 = jnp.bfloat16
CTX = ("z", "x", "core")
CHIPS = ("z", "x")
LANES = 128
HALF = 64
TOK = 128
PAIRS = 4


def nn(a, b):
    return lax.dot_general(a, b, (((1,), (0,)), ((), ())), preferred_element_type=F32)


def nt(a, b):
    return lax.dot_general(a, b, (((1,), (1,)), ((), ())), preferred_element_type=F32)


def split(x):
    hi = x.astype(BF16)
    return hi, (x - hi.astype(F32)).astype(BF16)


def both(op, a, w):
    rows = a[0].shape[0]
    out = op(jnp.concatenate(a, 0), w)
    return out[:rows] + out[rows:]


def three(op, a, b):
    return both(op, a, b[0]) + op(a[0], b[1])


def iota(shape, dim):
    return lax.broadcasted_iota(jnp.int32, shape, dim)


def low_lane(shape):
    return lax.rem(iota(shape, 1), LANES) < HALF


def diagonal(shape):
    return (lax.rem(iota(shape, 0), LANES) < HALF) == low_lane(shape)


def swap(x):
    return jnp.concatenate([x[HALF:], x[:HALF]], 0)


def pack(d):
    return jnp.where(diagonal((LANES, LANES)), d[:, :LANES], swap(d[:, LANES:]))


def unpack(x):
    diag = diagonal((LANES, LANES))
    return jnp.concatenate([jnp.where(diag, x, 0.0), jnp.where(diag, swap(x), 0.0)], 1)


def stacked(x):
    low = low_lane(x.shape)
    zero = jnp.zeros_like(x)
    return jnp.concatenate([jnp.where(low, x, zero), jnp.where(low, zero, x)], 0)


def side_by_side(x):
    return jnp.concatenate([x[:TOK], x[TOK:]], 1)


def block_ones():
    return jnp.where(diagonal((LANES, LANES)), 1.0, 0.0).astype(BF16)


def head_sum(x):
    return both(nn, split(x), block_ones())


def block_maps(maps_ref):
    twice = jnp.where(
        iota((HALF, LANES), 0) == lax.rem(iota((HALF, LANES), 1), HALF), 1.0, 0.0
    ).astype(BF16)
    wide = nn(maps_ref[...], twice)
    return jnp.where(diagonal(wide.shape), wide, 0.0).astype(BF16)


def cols(p, width=LANES):
    return slice(p * width, (p + 1) * width)


def softmaxes(z):
    low = low_lane(z.shape)
    inf = jnp.inf
    top = jnp.where(
        low,
        jnp.max(jnp.where(low, z, -inf), 1, keepdims=True),
        jnp.max(jnp.where(low, -inf, z), 1, keepdims=True),
    )
    bottom = jnp.where(
        low,
        jnp.min(jnp.where(low, z, inf), 1, keepdims=True),
        jnp.min(jnp.where(low, inf, z), 1, keepdims=True),
    )
    up = jnp.exp(z - top)
    down = jnp.exp(bottom - z)
    return up / head_sum(up), down / head_sum(down)


def chip_index(axis_sizes):
    return lax.axis_index("z") * axis_sizes["x"] + lax.axis_index("x"), lax.axis_index("core")


def features_kernel(q, k, v, qmap, kmap, send, kv, qh, ql, kh, kl):
    wq = block_maps(qmap)
    wk = block_maps(kmap)
    sums_p, sums_m = [], []
    chips = send.shape[0]
    for p in range(PAIRS):
        c = cols(p)
        pk, mk = softmaxes(nn(k[:, c], wk[c]))
        sums_p.append(jnp.sum(pk, 0, keepdims=True))
        sums_m.append(jnp.sum(mk, 0, keepdims=True))
        hi, lo = split(jnp.concatenate([pk, mk], 1))
        kh[:, cols(p, 2 * LANES)] = hi
        kl[:, cols(p, 2 * LANES)] = lo
        vt = v[:, c].T
        kv[c, :] = pack(nn(vt, hi) + nn(vt, lo))
    send[:, : 4 * LANES // chips, :] = kv[...].reshape(chips, 4 * LANES // chips, LANES)
    sums = jnp.concatenate(sums_p + sums_m, 0)
    send[:, 4 * LANES // chips :, :] = jnp.broadcast_to(sums[None], (chips, 8, LANES))
    for p in range(PAIRS):
        c = cols(p)
        pq, mq = softmaxes(nn(q[:, c], wq[c]))
        hi, lo = split(jnp.concatenate([pq, mq], 1))
        qh[:, cols(p, 2 * LANES)] = hi
        ql[:, cols(p, 2 * LANES)] = lo


def local_kernel(v, qh, ql, kh, kl, num, den, sth, stl):
    row = lax.rem(iota((2 * TOK, TOK), 0), TOK)
    lane = iota((2 * TOK, TOK), 1)
    for p in range(PAIRS):
        w = cols(p, 2 * LANES)
        q2 = (qh[:, w], ql[:, w])
        k2 = (kh[:, w], kl[:, w])
        scores = three(nt, (stacked(q2[0]), stacked(q2[1])), k2)
        scores = side_by_side(jnp.where(lane <= row, scores, 0.0))
        v2 = stacked(v[:, cols(p)])
        ones = stacked(jnp.ones((TOK, LANES), BF16))
        out = both(nn, split(scores), jnp.concatenate([v2, ones], 1))
        num[:, cols(p)] = out[:, :LANES]
        den[:, cols(p)] = out[:, LANES:]
        back = three(nt, (stacked(k2[0]), stacked(k2[1])), q2)
        hi, lo = split(side_by_side(jnp.where(lane >= row, back, 0.0)))
        sth[:, w] = hi
        stl[:, w] = lo


def second_kernel(sizes, got, g, qh, ql, denl, send, den, dn, ds, ksum):
    chip, core = chip_index(sizes)
    chips = send.shape[0]
    rows = 4 * LANES // chips
    part = rows // 2
    start = pl.multiple_of(core * part, part)
    acc = jnp.zeros((8, LANES), F32)
    run = jnp.zeros((part, LANES), F32)
    for m in range(chips):
        send[m, :part, :] = run
        run = run + (got[0, m, pl.ds(start, part), :] + got[1, m, pl.ds(start, part), :])
        zero = got[0, m, rows:, :]
        one = got[1, m, rows:, :]
        acc = acc + jnp.where(
            m < chip, zero + one, jnp.where((m == chip) & (core == 1), zero, 0.0)
        )
    ksum[...] = acc
    diag = diagonal((LANES, 2 * LANES))
    for p in range(PAIRS):
        c = cols(p)
        w = cols(p, 2 * LANES)
        q2 = (qh[:, w], ql[:, w])
        sums = jnp.concatenate([acc[p : p + 1], acc[p + 4 : p + 5]], 1)
        sums = jnp.where(diag, jnp.broadcast_to(sums, (LANES, 2 * LANES)), 0.0)
        d = denl[:, c] + three(nt, q2, split(sums))
        den[:, c] = d
        scaled = g[:, c].astype(F32) / d
        dn[:, c] = scaled
        ds[c, :] = pack(three(nn, split(scaled.T), q2))
    send[:, part:, :] = ds[...].reshape(chips, rows, LANES)


def gathered(got, part):
    return jnp.stack([got[0, :, :part, :], got[1, :, :part, :]], 1).reshape(4 * LANES, LANES)


def third_kernel(sizes, got, kvs, g, qh, ql, numl, den, send, dd, state):
    _, core = chip_index(sizes)
    chips = send.shape[0]
    rows = 4 * LANES // chips
    part = rows // 2
    start = pl.multiple_of(part + core * part, part)
    run = jnp.zeros((part, LANES), F32)
    for m in reversed(range(chips)):
        send[m, :part, :] = run
        run = run + (got[0, m, pl.ds(start, part), :] + got[1, m, pl.ds(start, part), :])
    whole = gathered(got, part) + jnp.where(core == 1, kvs[0], 0.0)
    state[...] = whole
    sums_p, sums_m = [], []
    for p in range(PAIRS):
        c = cols(p)
        w = cols(p, 2 * LANES)
        q2 = (qh[:, w], ql[:, w])
        numer = numl[:, c] + three(nt, q2, split(unpack(whole[c])))
        d = den[:, c]
        dden = -head_sum(g[:, c].astype(F32) * (numer / d)) / d
        dd[:, c] = dden
        full = q2[0].astype(F32) + q2[1].astype(F32)
        sums_p.append(jnp.sum(full[:, :LANES] * dden, 0, keepdims=True))
        sums_m.append(jnp.sum(full[:, LANES:] * dden, 0, keepdims=True))
    sums = jnp.concatenate(sums_p + sums_m, 0)
    send[:, part:, :] = jnp.broadcast_to(sums[None], (chips, 8, LANES))


def feature_back(f2, grad):
    full = f2[0].astype(F32) + f2[1].astype(F32)
    plus, minus = full[:, :LANES], full[:, LANES:]
    first, second = grad[:, :LANES], grad[:, LANES:]
    return plus * (first - head_sum(plus * first)) - minus * (second - head_sum(minus * second))


def one_hot_lane(shape):
    return lax.rem(iota(shape, 1), HALF) == 0


def fourth_kernel(
    q, v, qmap, qh, ql, kh, kl, sth, stl, dn, dd, state, ksum, gq_out, gq_map, gkl, gvl
):
    wq = block_maps(qmap)
    row = lax.rem(iota((2 * TOK, TOK), 0), TOK)
    lane = iota((2 * TOK, TOK), 1)
    hot = one_hot_lane((TOK, LANES))
    for p in range(PAIRS):
        c = cols(p)
        w = cols(p, 2 * LANES)
        q2 = (qh[:, w], ql[:, w])
        k2 = (kh[:, w], kl[:, w])
        v2 = v[:, c]
        scaled = dn[:, c]
        dden = dd[:, c]
        s2 = split(scaled)
        wide = split(jnp.concatenate([scaled, jnp.where(hot, dden, 0.0)], 1))
        ones = jnp.ones((TOK, LANES), BF16)
        mixing = both(
            nt, (stacked(wide[0]), stacked(wide[1])), jnp.concatenate([v2, ones], 1)
        )
        mixing = split(side_by_side(jnp.where(lane <= row, mixing, 0.0)))
        grad = three(nn, mixing, (stacked(k2[0]), stacked(k2[1])))
        grad = grad + three(nn, s2, split(unpack(state[c, :])))
        grad = grad + jnp.concatenate(
            [dden * ksum[p : p + 1, :], dden * ksum[p + 4 : p + 5, :]], 1
        )
        dzq = feature_back(q2, grad)
        z2 = split(dzq)
        gq_out[:, c] = both(nt, z2, wq[c]).astype(BF16)
        qt = q[:, c].T
        gq_map[c, :] = nn(qt, z2[0]) + nn(qt, z2[1])
        vwide = stacked(jnp.concatenate([v2, jnp.where(hot, 1.0, 0.0).astype(BF16)], 1))
        back = nt(vwide, wide[0]) + nt(vwide, wide[1])
        back = split(side_by_side(jnp.where(lane >= row, back, 0.0)))
        gkl[:, w] = three(nn, back, (stacked(q2[0]), stacked(q2[1])))
        gvl[:, c] = three(nn, (sth[:, w], stl[:, w]), (stacked(s2[0]), stacked(s2[1])))


def fifth_kernel(sizes, got, dss, k, v, kh, kl, gkl, gq_map, send, dz, later):
    chip, core = chip_index(sizes)
    chips = send.shape[0]
    rows = 4 * LANES // chips
    part = rows // 2
    acc = jnp.zeros((8, LANES), F32)
    for m in range(chips):
        zero = got[0, m, part:, :]
        one = got[1, m, part:, :]
        acc = acc + jnp.where(
            m > chip, zero + one, jnp.where((m == chip) & (core == 0), one, 0.0)
        )
    whole = gathered(got, part) + jnp.where(core == 0, dss[1], 0.0)
    later[...] = whole
    out = []
    for p in range(PAIRS):
        c = cols(p)
        w = cols(p, 2 * LANES)
        k2 = (kh[:, w], kl[:, w])
        v2 = v[:, c]
        sums = jnp.concatenate([acc[p : p + 1], acc[p + 4 : p + 5]], 1)
        grad = gkl[:, w] + sums + nn(
            jnp.concatenate([v2, v2], 1), jnp.concatenate(split(unpack(whole[c])), 0)
        )
        dzk = feature_back(k2, grad)
        dz[:, c] = dzk
        z2 = split(dzk)
        kt = k[:, c].T
        out.append(
            pack(jnp.concatenate([gq_map[c, :], nn(kt, z2[0]) + nn(kt, z2[1])], 1))
        )
    send[...] = jnp.concatenate(out, 0).reshape(chips, rows, LANES)


def sixth_kernel(kmap, kh, kl, gvl, dz, later, gk_out, gv_out):
    wk = block_maps(kmap)
    for p in range(PAIRS):
        c = cols(p)
        w = cols(p, 2 * LANES)
        gk_out[:, c] = both(nt, split(dz[:, c]), wk[c]).astype(BF16)
        grad = gvl[:, c] + three(nt, (kh[:, w], kl[:, w]), split(unpack(later[c, :])))
        gv_out[:, c] = grad.astype(BF16)


def sum_kernel(got, send):
    total = got[0]
    for m in range(1, got.shape[0]):
        total = total + got[m]
    send[...] = jnp.broadcast_to(total[None], send.shape)


def last_kernel(scale, got, gq, gk):
    for p in range(PAIRS):
        x = got[cols(p), :] * scale
        y = pltpu.roll(x, HALF, 1)
        gq[2 * p] = x[:HALF, :HALF].astype(BF16)
        gq[2 * p + 1] = y[HALF:, :HALF].astype(BF16)
        gk[2 * p] = x[HALF:, :HALF].astype(BF16)
        gk[2 * p + 1] = y[:HALF, :HALF].astype(BF16)


def call(kernel, outs, *args, flops=10**8):
    shapes = [jax.ShapeDtypeStruct(shape, dtype) for shape, dtype in outs]
    moved = sum(a.size * a.dtype.itemsize for a in (*args, *shapes))
    return pl.pallas_call(
        kernel,
        out_shape=shapes,
        in_specs=[pl.BlockSpec(memory_space=pltpu.VMEM)] * len(args),
        out_specs=[pl.BlockSpec(memory_space=pltpu.VMEM)] * len(outs),
        compiler_params=pltpu.CompilerParams(vmem_limit_bytes=48 * 2**20),
        cost_estimate=pl.CostEstimate(flops=flops, bytes_accessed=moved, transcendentals=0),
    )(*args)


def per_device(sizes, queries, keys, values, upstream, query_map, key_map):
    chips = sizes["z"] * sizes["x"]
    rows = 4 * LANES // chips
    part = rows // 2
    q, k, v, g = (a.reshape(TOK, 4 * LANES) for a in (queries, keys, values, upstream))
    qmap = query_map.reshape(8 * HALF, HALF)
    kmap = key_map.reshape(8 * HALF, HALF)
    feats = ((TOK, 8 * LANES), BF16)
    flat = ((TOK, 4 * LANES), F32)
    small = ((TOK, 4 * LANES), BF16)
    square = ((4 * LANES, LANES), F32)

    def exchange(a):
        return lax.all_gather(lax.all_to_all(a, CHIPS, 0, 0), "core")

    send, kv, qh, ql, kh, kl = call(
        features_kernel,
        [((chips, rows + 8, LANES), F32), square, feats, feats, feats, feats],
        q, k, v, qmap, kmap,
    )
    got = exchange(send)
    kvs = lax.all_gather(kv, "core")
    numl, denl, sth, stl = call(
        local_kernel, [flat, flat, feats, feats], v, qh, ql, kh, kl, flops=10**9
    )
    send, den, dn, ds, ksum = call(
        functools.partial(second_kernel, sizes),
        [((chips, part + rows, LANES), F32), flat, flat, square, ((8, LANES), F32)],
        got, g, qh, ql, denl,
    )
    got = exchange(send)
    dss = lax.all_gather(ds, "core")
    send, dd, state = call(
        functools.partial(third_kernel, sizes),
        [((chips, part + 8, LANES), F32), flat, square],
        got, kvs, g, qh, ql, numl, den,
    )
    got = exchange(send)
    grad_q, gq_map, gkl, gvl = call(
        fourth_kernel,
        [small, square, ((TOK, 8 * LANES), F32), flat],
        q, v, qmap, qh, ql, kh, kl, sth, stl, dn, dd, state, ksum,
        flops=10**9,
    )
    send, dz, later = call(
        functools.partial(fifth_kernel, sizes),
        [((chips, rows, LANES), F32), flat, square],
        got, dss, k, v, kh, kl, gkl, gq_map,
    )
    got = lax.all_to_all(send, CHIPS, 0, 0)
    grad_k, grad_v = call(
        sixth_kernel, [small, small], kmap, kh, kl, gvl, dz, later, flops=10**9
    )
    others = sizes["dp"] * sizes["core"]
    (send,) = call(sum_kernel, [((others, rows, LANES), F32)], got)
    got = lax.all_to_all(send, ("dp", "core"), 0, 0)
    (send,) = call(sum_kernel, [((chips, rows, LANES), F32)], got)
    got = lax.all_to_all(send, CHIPS, 0, 0)
    scale = float(TOK * chips * others) ** (-0.5)
    heads = ((8, HALF, HALF), BF16)
    total_q, total_k = call(
        functools.partial(last_kernel, scale), [heads, heads], got.reshape(4 * LANES, LANES)
    )
    shape = queries.shape
    return grad_q.reshape(shape), grad_k.reshape(shape), grad_v.reshape(shape), total_q, total_k


def physical(mesh):
    dp, ctx = mesh.devices.shape
    x = 4 if ctx % 8 == 0 and ctx > 8 else 2
    sizes = {"dp": dp, "z": ctx // (2 * x), "x": x, "core": 2}
    return Mesh(mesh.devices.reshape(tuple(sizes.values())), tuple(sizes)), sizes


def solution(mesh):
    inner, sizes = physical(mesh)
    tokens = P("dp", CTX, None)
    return jax.shard_map(
        functools.partial(per_device, sizes),
        mesh=inner,
        in_specs=(tokens,) * 4 + (P(), P()),
        out_specs=(tokens,) * 3 + (P(), P()),
        check_vma=False,
    )
```

time: 788 us -> 142 us (0.18)
  waiting for transfers between devices: 367 us -> 38.4 us
  local copies, waits for them, and re-layouts: 158 us -> 7.61 us
  other arithmetic: 114 us -> 0 us
  blocking collectives: 101 us -> 51.6 us
  starting transfers between devices: 0.12 us -> 27 us
  matrix products: 20.1 us -> 0 us
  Pallas kernels: 0 us -> 16.1 us
  between operations: 14 us -> 0.79 us
    psum x1 -> x0, waiting for transfers between devices: 264 us -> none  [per_device(): total_q, total_k = lax.psum((gq, gk), ('dp', 'ctx'))]
    dynamic_slice x256 -> x0, local copies, waits for them, and re-layouts: 149 us -> none  [hop(): new = combine(before, jax.tree.map(lambda part: part[at], everything))]
    select_n x257 -> x0, other arithmetic: 111 us -> none  [the longest x256 111 us: hop(): return jax.tree.map(lambda a, b: jnp.where(reached, a, b), new, before)]
    all_gather x2 -> x0, waiting for transfers between devices: 103 us -> none  [entering(): everything = jax.tree.map(lambda part: lax.all_gather(part, axis), value)]
    all_gather x2 -> x5, blocking collectives: 101 us -> 17.1 us  [the longest x3 12.6 us: exchange(): return lax.all_gather(lax.all_to_all(a, CHIPS, 0, 0), 'core')]
    all_to_all x0 -> x4, waiting for transfers between devices: none -> 38.4 us  [the longest x3 26.9 us: exchange(): return lax.all_gather(lax.all_to_all(a, CHIPS, 0, 0), 'core')]
    all_to_all x0 -> x2, blocking collectives: none -> 34.5 us  [the longest x1 18.4 us: per_device(): got = lax.all_to_all(send, ('dp', 'core'), 0, 0)]
    all_to_all x0 -> x4, starting transfers between devices: none -> 27 us  [the longest x3 23 us: exchange(): return lax.all_gather(lax.all_to_all(a, CHIPS, 0, 0), 'core')]
  transfers between devices with their start and end apart: 3 -> 4, of which waited for: 3 -> 4; matrix products, arithmetic and copies ran while one was open for 2% -> 0% of each run, Pallas kernels for 0% -> 5%
where the time goes in v1:
time: 142 us
  blocking collectives  51.6 us (36%)
  waiting for transfers between devices  38.4 us (27%)
  starting transfers between devices  27 us (19%)
  Pallas kernels  16.1 us (11%)
  local copies, waits for them, and re-layouts  7.61 us (5%)
    all_to_all x3, waiting for transfers between devices, exchange(): return lax.all_gather(lax.all_to_all(a, CHIPS, 0, 0), 'core')  26.9 us
    all_to_all x3, starting transfers between devices, exchange(): return lax.all_gather(lax.all_to_all(a, CHIPS, 0, 0), 'core')  23 us
    all_to_all x1, blocking collectives, per_device(): got = lax.all_to_all(send, ('dp', 'core'), 0, 0)  18.4 us
    all_to_all x1, blocking collectives, per_device(): got = lax.all_to_all(send, CHIPS, 0, 0)  16.1 us
    pallas_call x10, Pallas kernels, call(): pl.pallas_call(kernel, out_shape=shapes, in_specs=[pl.BlockSpec(memory_sp...  16.1 us
    all_gather x3, blocking collectives, exchange(): return lax.all_gather(lax.all_to_all(a, CHIPS, 0, 0), 'core')  12.6 us
    all_to_all x1, waiting for transfers between devices, per_device(): got = lax.all_to_all(send, CHIPS, 0, 0)  11.6 us
    unnamed x38, local copies, waits for them, and re-layouts  7.61 us
  transfers between devices with their start and end apart: 4, of which 4 were waited for; matrix products, arithmetic and copies ran while one was open for 0% of the time, Pallas kernels for 5%

profile of v1, /device:TPU:1, one launch (start us, length us, event | category | flops | bytes accessed | tf_op | source)
XLA Modules:
  0.0 141.5 jit_solution(3492742215224088072)
XLA Ops:
  0.6 0.0 copy-start
  0.6 0.9 copy-done
  1.5 0.0 copy-start.2
  1.5 0.9 copy-done.2
  2.4 0.0 copy-start.5
  2.4 0.9 copy-done.5
  3.3 0.0 copy-start.7
  3.3 0.9 copy-done.7
  4.3 0.0 copy-start.9
  4.3 0.9 copy-done.9
  5.2 2.7 %shard_map.101 = (f32[32,24,128]{2,1,0:T(8,128)}, f32[512,128]{1,0:T(8,128)S(1)}, bf16[128,1024]{1,0:T(8,128)(2,1)S(1)}, bf16[128,1024]{1,0:T(8,128)(2,1)S(1)}, ...) custom-call(bf16[128,512]{1,0:T(8,128)(2,1)S(1)} %bitcast.29, bf16[128,512]{1,0:T(8,128)(2,1)S(1)} %bitcast.24, ...), custom_call_target="tpu_custom_call" | custom-call | flops 100000000 | bytes 2228224 | tf_op jit(solution)/shard_map/pallas_call | solution.py:345
  7.8 0.0 copy-start.1
  7.8 13.8 %all-to-all-start = ((f32[32,24,128]{2,1,0:T(8,128)}), f32[32,24,128]{2,1,0:T(8,128)S(1)}, u32[]{:S(2)}, u32[]{:S(2)}) async-start(f32[32,24,128]{2,1,0:T(8,128)} %get-tuple-element.40), calls=%async_computation | async-start | bytes 786432 | tf_op jit(solution)/shard_map/all_to_all | solution.py:368
  21.7 0.0 copy-done.1
  21.7 1.6 %shard_map.102 = (f32[128,512]{1,0:T(8,128)S(1)}, f32[128,512]{1,0:T(8,128)S(1)}, bf16[128,1024]{1,0:T(8,128)(2,1)S(1)}, bf16[128,1024]{1,0:T(8,128)(2,1)S(1)}) custom-call(bf16[128,512]{1,0:T(8,128)(2,1)S(1)} %bitcast.21, bf16[128,1024]{1,0:T(8,128)(2,1)S(1)} %get-tuple-element.34.qh, bf16[128,1024]{1,0:T(8,128)(2,1)S(1)} %get-tuple-element.35.ql, ...), custom_call_target="tpu_custom_call" | custom-call | flops 1000000000 | bytes 2228224 | tf_op jit(solution)/shard_map/pallas_call | solution.py:345
  23.3 0.0 copy-start.15
  23.3 0.7 copy-done.15
  24.0 0.0 copy-start.13
  24.0 0.0 copy-start.4
  24.0 11.5 %all-to-all-done = f32[32,24,128]{2,1,0:T(8,128)S(1)} async-done(((f32[32,24,128]{2,1,0:T(8,128)}), f32[32,24,128]{2,1,0:T(8,128)S(1)}, u32[]{:S(2)}, u32[]{:S(2)}) %all-to-all-start) | async-done | bytes 393248 | tf_op jit(solution)/shard_map/all_to_all | solution.py:368
  35.5 4.5 %all-gather = f32[64,24,128]{2,1,0:T(8,128)S(1)} all-gather(f32[32,24,128]{2,1,0:T(8,128)S(1)} %all-to-all-done), channel_id=2, replica_groups=mesh['dp'=8,'z'=8,'x'=4,'core'=2] {'core'}, dimensions={0}, use_global_device_ids=true | all-gather | bytes 1179648 | tf_op jit(solution)/shard_map/all_gather | solution.py:368
  40.0 0.0 copy-done.13
  40.0 0.0 copy-done.4
  40.0 1.7 %shard_map.103 = (f32[32,24,128]{2,1,0:T(8,128)}, f32[128,512]{1,0:T(8,128)S(1)}, f32[128,512]{1,0:T(8,128)S(1)}, f32[512,128]{1,0:T(8,128)S(1)}, f32[8,128]{1,0:T(8,128)S(1)}) custom-call(f32[2,32,24,128]{3,2,1,0:T(8,128)S(1)} %bitcast.16, bf16[128,512]{1,0:T(8,128)(2,1)S(1)} %bitcast.26, bf16[128,1024]{1,0:T(8,128)(2,1)S(1)} %get-tuple-element.34.qh, ...), custom_call_target="tpu_custom_call" | custom-call | flops 100000000 | bytes 2887680 | tf_op jit(solution)/shard_map/pallas_call | solution.py:345
  41.6 4.6 %all-to-all-start.1 = ((f32[32,24,128]{2,1,0:T(8,128)}), f32[32,24,128]{2,1,0:T(8,128)}, u32[]{:S(2)}, u32[]{:S(2)}) async-start(f32[32,24,128]{2,1,0:T(8,128)} %get-tuple-element.43), calls=%async_computation.1 | async-start | bytes 786432 | tf_op jit(solution)/shard_map/all_to_all | solution.py:368
  46.2 2.2 %all-gather.2 = f32[1024,128]{1,0:T(8,128)S(1)} all-gather(f32[512,128]{1,0:T(8,128)S(1)} %get-tuple-element.44), channel_id=4, replica_groups=mesh['dp'=8,'z'=8,'x'=4,'core'=2] {'core'}, dimensions={0}, use_global_device_ids=true | all-gather | bytes 786432 | tf_op jit(solution)/shard_map/all_gather | solution.py:376
  48.4 12.2 %all-to-all-done.1 = f32[32,24,128]{2,1,0:T(8,128)} async-done(((f32[32,24,128]{2,1,0:T(8,128)}), f32[32,24,128]{2,1,0:T(8,128)}, u32[]{:S(2)}, u32[]{:S(2)}) %all-to-all-start.1) | async-done | bytes 393248 | tf_op jit(solution)/shard_map/all_to_all | solution.py:368
  60.7 4.0 %all-gather.1 = f32[64,24,128]{2,1,0:T(8,128)S(1)} all-gather(f32[32,24,128]{2,1,0:T(8,128)} %all-to-all-done.1), channel_id=3, replica_groups=mesh['dp'=8,'z'=8,'x'=4,'core'=2] {'core'}, dimensions={0}, use_global_device_ids=true | all-gather | bytes 1179648 | tf_op jit(solution)/shard_map/all_gather | solution.py:368
  64.7 1.6 %shard_map.104 = (f32[32,16,128]{2,1,0:T(8,128)}, f32[128,512]{1,0:T(8,128)S(1)}, f32[512,128]{1,0:T(8,128)S(1)}) custom-call(f32[2,32,24,128]{3,2,1,0:T(8,128)S(1)} %bitcast.15, f32[2,512,128]{2,1,0:T(8,128)S(1)} %bitcast.18, bf16[128,512]{1,0:T(8,128)(2,1)S(1)} %bitcast.27, bf16[128,1024]{1,0:T(8,128)(2,1)S(1)} %get-tuple-element.34.qh, ...), custom_call_target="tpu_custom_call" | custom-call | flops 100000000 | bytes 3276800 | tf_op jit(solution)/shard_map/pallas_call | solution.py:345
  66.3 0.0 copy-start.11
  66.3 0.7 copy-done.11
  67.0 4.6 %all-to-all-start.2 = ((f32[32,16,128]{2,1,0:T(8,128)}), f32[32,16,128]{2,1,0:T(8,128)}, u32[]{:S(2)}, u32[]{:S(2)}) async-start(f32[32,16,128]{2,1,0:T(8,128)} %get-tuple-element.52), calls=%async_computation.2 | async-start | bytes 524288 | tf_op jit(solution)/shard_map/all_to_all | solution.py:368
  71.6 0.0 copy-start.6
  71.6 0.0 copy-start.8
  71.6 0.0 copy-start.12
  71.6 0.0 copy-start.14
  71.6 2.3 %all-gather.4 = f32[1024,128]{1,0:T(8,128)S(1)} all-gather(f32[512,128]{1,0:T(8,128)S(1)} %get-tuple-element.53), channel_id=6, replica_groups=mesh['dp'=8,'z'=8,'x'=4,'core'=2] {'core'}, dimensions={0}, use_global_device_ids=true | all-gather | bytes 786432 | tf_op jit(solution)/shard_map/all_gather | solution.py:386
  73.9 0.0 copy-done.6
  73.9 0.0 copy-done.8
  73.9 0.0 copy-done.12
  74.0 0.0 copy-done.14
  74.0 0.0 copy-start.16
  74.0 0.9 copy-done.16
  74.9 4.7 %shard_map.105 = (bf16[128,512]{1,0:T(8,128)(2,1)}, f32[512,128]{1,0:T(8,128)S(1)}, f32[128,1024]{1,0:T(8,128)S(1)}, f32[128,512]{1,0:T(8,128)S(1)}) custom-call(bf16[128,512]{1,0:T(8,128)(2,1)S(1)} %bitcast.30, bf16[128,512]{1,0:T(8,128)(2,1)S(1)} %bitcast.22, bf16[512,64]{1,0:T(8,128)(2,1)S(1)} %bitcast.32, bf16[128,1024]{1,0:T(8,128)(2,1)S(1)} %get-tuple-element.34.qh, ...), custom_call_target="tpu_custom_call" | custom-call | flops 1000000000 | bytes 3870720 | tf_op jit(solution)/shard_map/pallas_call | solution.py:345
  79.6 0.0 copy-start.17
  79.6 0.7 copy-done.17
  80.3 0.0 copy-start.3
  80.3 3.1 %all-to-all-done.2 = f32[32,16,128]{2,1,0:T(8,128)} async-done(((f32[32,16,128]{2,1,0:T(8,128)}), f32[32,16,128]{2,1,0:T(8,128)}, u32[]{:S(2)}, u32[]{:S(2)}) %all-to-all-start.2) | async-done | bytes 262176 | tf_op jit(solution)/shard_map/all_to_all | solution.py:368
  83.4 4.1 %all-gather.3 = f32[64,16,128]{2,1,0:T(8,128)S(1)} all-gather(f32[32,16,128]{2,1,0:T(8,128)} %all-to-all-done.2), channel_id=5, replica_groups=mesh['dp'=8,'z'=8,'x'=4,'core'=2] {'core'}, dimensions={0}, use_global_device_ids=true | all-gather | bytes 786432 | tf_op jit(solution)/shard_map/all_gather | solution.py:368
  87.5 0.0 copy-done.3
  87.5 1.1 shard_map.106
  88.6 16.1 %all_to_all.30.got = f32[32,16,128]{2,1,0:T(8,128)S(1)} all-to-all(f32[32,16,128]{2,1,0:T(8,128)S(1)} %get-tuple-element.60), channel_id=1, replica_groups=mesh['dp'=8,'z'=8,'x'=4,'core'=2] {'z','x'}, dimensions={0} | all-to-all | bytes 524288 | tf_op jit(solution)/shard_map/all_to_all | solution.py:404
  104.8 18.4 %all_to_all.31.got = f32[16,16,128]{2,1,0:T(8,128)S(1)} all-to-all(f32[16,16,128]{2,1,0:T(8,128)S(1)} %shard_map.108), channel_id=1, replica_groups=mesh['dp'=8,'z'=8,'x'=4,'core'=2] {'dp','core'}, dimensions={0} | all-to-all | bytes 262144 | tf_op jit(solution)/shard_map/all_to_all | solution.py:410
  123.2 0.7 shard_map.109
  123.9 0.0 copy-start.10
  123.9 0.0 copy-start.18
  123.9 4.0 %all-to-all-start.5 = ((f32[32,16,128]{2,1,0:T(8,128)}), f32[32,16,128]{2,1,0:T(8,128)S(1)}, u32[]{:S(2)}, u32[]{:S(2)}) async-start(f32[32,16,128]{2,1,0:T(8,128)} %shard_map.109), calls=%async_computation.5 | async-start | bytes 524288 | tf_op jit(solution)/shard_map/all_to_all | solution.py:412
  127.9 0.0 copy-done.10
  127.9 0.0 copy-done.18
  127.9 1.3 shard_map.107
  129.2 11.6 %all-to-all-done.5 = f32[32,16,128]{2,1,0:T(8,128)S(1)} async-done(((f32[32,16,128]{2,1,0:T(8,128)}), f32[32,16,128]{2,1,0:T(8,128)S(1)}, u32[]{:S(2)}, u32[]{:S(2)}) %all-to-all-start.5) | async-done | bytes 262176 | tf_op jit(solution)/shard_map/all_to_all | solution.py:412
  140.7 0.8 shard_map.110
  (1 shorter events, 0.0 us)
Async XLA Ops:
  0.6 0.9 copy-start
  1.5 0.9 copy-start.2
  2.4 0.9 copy-start.5
  3.3 0.9 copy-start.7
  4.3 0.9 copy-start.9
  7.8 13.9 %copy-start.1 = (bf16[1,128,512]{2,1,0:T(8,128)(2,1)S(1)}, bf16[1,128,512]{2,1,0:T(8,128)(2,1)}, u32[]{:S(2)}) copy-start(bf16[1,128,512]{2,1,0:T(8,128)(2,1)} %param.8) | copy-start | bytes 393220
  7.8 27.7 %all-to-all-start = ((f32[32,24,128]{2,1,0:T(8,128)}), f32[32,24,128]{2,1,0:T(8,128)S(1)}, u32[]{:S(2)}, u32[]{:S(2)}) async-start(f32[32,24,128]{2,1,0:T(8,128)} %get-tuple-element.40), calls=%async_computation | async-start | bytes 786432 | tf_op jit(solution)/shard_map/all_to_all | solution.py:368
  23.3 0.7 copy-start.15
  24.0 16.0 %copy-start.13 = (bf16[128,1024]{1,0:T(8,128)(2,1)}, bf16[128,1024]{1,0:T(8,128)(2,1)S(1)}, u32[]{:S(2)}) copy-start(bf16[128,1024]{1,0:T(8,128)(2,1)S(1)} %get-tuple-element.38.sth) | copy-start | bytes 786436
  24.0 16.0 %copy-start.4 = (bf16[1,128,512]{2,1,0:T(8,128)(2,1)S(1)}, bf16[1,128,512]{2,1,0:T(8,128)(2,1)}, u32[]{:S(2)}) copy-start(bf16[1,128,512]{2,1,0:T(8,128)(2,1)} %param.9) | copy-start | bytes 393220
  41.6 19.0 %all-to-all-start.1 = ((f32[32,24,128]{2,1,0:T(8,128)}), f32[32,24,128]{2,1,0:T(8,128)}, u32[]{:S(2)}, u32[]{:S(2)}) async-start(f32[32,24,128]{2,1,0:T(8,128)} %get-tuple-element.43), calls=%async_computation.1 | async-start | bytes 786432 | tf_op jit(solution)/shard_map/all_to_all | solution.py:368
  66.3 0.7 copy-start.11
  67.0 16.4 %all-to-all-start.2 = ((f32[32,16,128]{2,1,0:T(8,128)}), f32[32,16,128]{2,1,0:T(8,128)}, u32[]{:S(2)}, u32[]{:S(2)}) async-start(f32[32,16,128]{2,1,0:T(8,128)} %get-tuple-element.52), calls=%async_computation.2 | async-start | bytes 524288 | tf_op jit(solution)/shard_map/all_to_all | solution.py:368
  71.6 2.4 %copy-start.6 = (bf16[1,128,512]{2,1,0:T(8,128)(2,1)S(1)}, bf16[1,128,512]{2,1,0:T(8,128)(2,1)}, u32[]{:S(2)}) copy-start(bf16[1,128,512]{2,1,0:T(8,128)(2,1)} %param.6) | copy-start | bytes 393220
  71.6 2.4 %copy-start.8 = (bf16[8,64,64]{2,1,0:T(8,128)(2,1)S(1)}, bf16[8,64,64]{2,1,0:T(8,128)(2,1)}, u32[]{:S(2)}) copy-start(bf16[8,64,64]{2,1,0:T(8,128)(2,1)} %param.10) | copy-start | bytes 196612
  71.6 2.3 %copy-start.12 = (f32[512,128]{1,0:T(8,128)S(1)}, f32[512,128]{1,0:T(8,128)}, u32[]{:S(2)}) copy-start(f32[512,128]{1,0:T(8,128)} %copy-done.11) | copy-start | bytes 786436
  71.6 2.3 %copy-start.14 = (bf16[128,1024]{1,0:T(8,128)(2,1)S(1)}, bf16[128,1024]{1,0:T(8,128)(2,1)}, u32[]{:S(2)}) copy-start(bf16[128,1024]{1,0:T(8,128)(2,1)} %copy-done.13) | copy-start | bytes 786436
  74.0 1.0 copy-start.16
  79.6 0.7 copy-start.17
  80.3 7.2 %copy-start.3 = (bf16[1,128,512]{2,1,0:T(8,128)(2,1)S(1)}, bf16[1,128,512]{2,1,0:T(8,128)(2,1)}, u32[]{:S(2)}) copy-start(bf16[1,128,512]{2,1,0:T(8,128)(2,1)} %param.7) | copy-start | bytes 393220
  123.9 4.0 %copy-start.10 = (bf16[8,64,64]{2,1,0:T(8,128)(2,1)S(1)}, bf16[8,64,64]{2,1,0:T(8,128)(2,1)}, u32[]{:S(2)}) copy-start(bf16[8,64,64]{2,1,0:T(8,128)(2,1)} %param.11) | copy-start | bytes 196612
  123.9 4.0 %copy-start.18 = (f32[128,512]{1,0:T(8,128)S(1)}, f32[128,512]{1,0:T(8,128)}, u32[]{:S(2)}) copy-start(f32[128,512]{1,0:T(8,128)} %copy-done.17) | copy-start | bytes 786436
  123.9 16.8 %all-to-all-start.5 = ((f32[32,16,128]{2,1,0:T(8,128)}), f32[32,16,128]{2,1,0:T(8,128)S(1)}, u32[]{:S(2)}, u32[]{:S(2)}) async-start(f32[32,16,128]{2,1,0:T(8,128)} %shard_map.109), calls=%async_computation.5 | async-start | bytes 524288 | tf_op jit(solution)/shard_map/all_to_all | solution.py:412

commit v2 on v1

v2 whole, which is shorter than its diff:
```python
import functools

import jax
import jax.numpy as jnp
import numpy as np
from jax import lax
from jax.experimental import pallas as pl
from jax.experimental.pallas import tpu as pltpu
from jax.sharding import Mesh, PartitionSpec as P

F32 = jnp.float32
BF16 = jnp.bfloat16
CTX = ("z", "x", "core")
CHIPS = ("z", "x")
LANES = 128
HALF = 64
TOK = 128
BLOCK = 256
PAIRS = 2
WIDE = PAIRS * LANES


def nn(a, b):
    return lax.dot_general(a, b, (((1,), (0,)), ((), ())), preferred_element_type=F32)


def nt(a, b):
    return lax.dot_general(a, b, (((1,), (1,)), ((), ())), preferred_element_type=F32)


def split(x):
    hi = x.astype(BF16)
    return hi, (x - hi.astype(F32)).astype(BF16)


def both(op, a, w):
    rows = a[0].shape[0]
    out = op(jnp.concatenate(a, 0), w)
    return out[:rows] + out[rows:]


def three(op, a, b):
    return both(op, a, b[0]) + op(a[0], b[1])


def iota(shape, dim):
    return lax.broadcasted_iota(jnp.int32, shape, dim)


def low_lane(shape):
    return lax.rem(iota(shape, 1), LANES) < HALF


def diagonal(shape):
    return (lax.rem(iota(shape, 0), LANES) < HALF) == low_lane(shape)


def swap(x):
    return jnp.concatenate([x[HALF:], x[:HALF]], 0)


def pack(d):
    return jnp.where(diagonal((LANES, LANES)), d[:, :LANES], swap(d[:, LANES:]))


def unpack(x):
    diag = diagonal((LANES, LANES))
    return jnp.concatenate([jnp.where(diag, x, 0.0), jnp.where(diag, swap(x), 0.0)], 1)


def stacked(x):
    low = low_lane(x.shape)
    zero = jnp.zeros_like(x)
    return jnp.concatenate([jnp.where(low, x, zero), jnp.where(low, zero, x)], 0)


def side_by_side(x):
    return jnp.concatenate([x[:BLOCK], x[BLOCK:]], 1)


def block_ones():
    return jnp.where(diagonal((LANES, LANES)), 1.0, 0.0).astype(BF16)


def head_sum(x):
    return both(nn, split(x), block_ones())


def block_maps(maps_ref):
    twice = jnp.where(
        iota((HALF, LANES), 0) == lax.rem(iota((HALF, LANES), 1), HALF), 1.0, 0.0
    ).astype(BF16)
    wide = nn(maps_ref[...], twice)
    return jnp.where(diagonal(wide.shape), wide, 0.0).astype(BF16)


def cols(p, width=LANES):
    return slice(p * width, (p + 1) * width)


def softmaxes(z):
    low = low_lane(z.shape)
    inf = jnp.inf
    top = jnp.where(
        low,
        jnp.max(jnp.where(low, z, -inf), 1, keepdims=True),
        jnp.max(jnp.where(low, -inf, z), 1, keepdims=True),
    )
    bottom = jnp.where(
        low,
        jnp.min(jnp.where(low, z, inf), 1, keepdims=True),
        jnp.min(jnp.where(low, inf, z), 1, keepdims=True),
    )
    up = jnp.exp(z - top)
    down = jnp.exp(bottom - z)
    return up / head_sum(up), down / head_sum(down)


def core():
    return lax.axis_index("core")


def chip(sizes):
    return lax.axis_index("z") * sizes["x"] + lax.axis_index("x")


def causal(rows):
    return iota((rows, BLOCK), 1) <= lax.rem(iota((rows, BLOCK), 0), BLOCK)


def causal_back(rows):
    return iota((rows, BLOCK), 1) >= lax.rem(iota((rows, BLOCK), 0), BLOCK)


def start_kernel(a, b, maps, send, own, wide, other, few, sems):
    mine = pl.ds(pl.multiple_of(core() * WIDE, WIDE), WIDE)
    theirs = pl.ds(pl.multiple_of((1 - core()) * WIDE, WIDE), WIDE)
    copies = []
    for i, ref in enumerate((a, b)):
        here = pl.ds(i * WIDE, WIDE)
        copies.append(pltpu.make_async_copy(ref.at[:, theirs], other.at[:, here], sems.at[2 * i]))
        copies.append(pltpu.make_async_copy(ref.at[:, mine], own.at[:, here], sems.at[2 * i + 1]))
    copies.append(pltpu.make_async_copy(maps.at[mine, :], few, sems.at[4]))
    for copy in copies:
        copy.start()
    copies[4].wait()
    wide[...] = block_maps(few)
    for copy in copies[:4]:
        copy.wait()
    send[...] = other[...].astype(F32)


def assemble(own, got, first, second):
    here = pl.ds(pl.multiple_of(core() * TOK, TOK), TOK)
    there = pl.ds(pl.multiple_of((1 - core()) * TOK, TOK), TOK)
    for i, ref in enumerate((first, second)):
        lanes = slice(i * WIDE, (i + 1) * WIDE)
        ref[here, :] = own[:, lanes]
        ref[there, :] = got[1 - core(), :, lanes].astype(BF16)


def keys_kernel(own, got, wk, send, k, v, kh, kl):
    assemble(own, got, k, v)
    chips = send.shape[0]
    rows = WIDE // chips
    state, sums_p, sums_m = [], [], []
    for p in range(PAIRS):
        c = cols(p)
        pk, mk = softmaxes(nn(k[:, c], wk[c]))
        sums_p.append(jnp.sum(pk, 0, keepdims=True))
        sums_m.append(jnp.sum(mk, 0, keepdims=True))
        hi, lo = split(jnp.concatenate([pk, mk], 1))
        kh[:, cols(p, 2 * LANES)] = hi
        kl[:, cols(p, 2 * LANES)] = lo
        vt = v[:, c].T
        state.append(pack(nn(vt, hi) + nn(vt, lo)))
    send[:, :rows, :] = jnp.concatenate(state, 0).reshape(chips, rows, LANES)
    sums = jnp.concatenate(sums_p + sums_m + [jnp.zeros((4, LANES), F32)], 0)
    send[:, rows:, :] = jnp.broadcast_to(sums[None], (chips, 8, LANES))


def queries_kernel(own, got, wq, v, kh, kl, q, g, qh, ql, num, den, sth, stl, cumk):
    assemble(own, got, q, g)
    mask = causal(2 * BLOCK)
    back_mask = causal_back(2 * BLOCK)
    tri = jnp.where(causal(BLOCK), 1.0, 0.0).astype(BF16)
    for p in range(PAIRS):
        c = cols(p)
        w = cols(p, 2 * LANES)
        pq, mq = softmaxes(nn(q[:, c], wq[c]))
        q2 = split(jnp.concatenate([pq, mq], 1))
        qh[:, w], ql[:, w] = q2
        k2 = (kh[:, w], kl[:, w])
        cumk[:, w] = nn(tri, k2[0]) + nn(tri, k2[1])
        scores = three(nt, (stacked(q2[0]), stacked(q2[1])), k2)
        scores = side_by_side(jnp.where(mask, scores, 0.0))
        v2 = stacked(v[:, c])
        ones = stacked(jnp.ones((BLOCK, LANES), BF16))
        out = both(nn, split(scores), jnp.concatenate([v2, ones], 1))
        num[:, c] = out[:, :LANES]
        den[:, c] = out[:, LANES:]
        back = three(nt, (stacked(k2[0]), stacked(k2[1])), q2)
        hi, lo = split(side_by_side(jnp.where(back_mask, back, 0.0)))
        both_heads = cols(p, 2 * BLOCK)
        sth[:, both_heads] = hi
        stl[:, both_heads] = lo


def second_kernel(sizes, got, g, qh, ql, denl, send, den, dn, ksum):
    chips = send.shape[0]
    rows = WIDE // chips
    me = chip(sizes)
    acc = jnp.zeros((8, LANES), F32)
    run = jnp.zeros((rows, LANES), F32)
    for m in range(chips):
        send[m, :rows, :] = run
        run = run + got[m, :rows, :]
        acc = acc + jnp.where(m < me, got[m, rows:, :], 0.0)
    ksum[...] = acc
    diag = diagonal((LANES, 2 * LANES))
    out = []
    for p in range(PAIRS):
        c = cols(p)
        w = cols(p, 2 * LANES)
        q2 = (qh[:, w], ql[:, w])
        sums = jnp.concatenate([acc[p : p + 1], acc[p + PAIRS : p + PAIRS + 1]], 1)
        sums = jnp.where(diag, jnp.broadcast_to(sums, (LANES, 2 * LANES)), 0.0)
        d = denl[:, c] + three(nt, q2, split(sums))
        den[:, c] = d
        scaled = g[:, c].astype(F32) / d
        dn[:, c] = scaled
        out.append(pack(three(nn, split(scaled.T), q2)))
    send[:, rows:, :] = jnp.concatenate(out, 0).reshape(chips, rows, LANES)


def local_kernel(v, qh, ql, kh, kl, sth, stl, dn, gql, gkl, gvl):
    mask = causal(2 * BLOCK)
    back_mask = causal_back(2 * BLOCK)
    for p in range(PAIRS):
        c = cols(p)
        w = cols(p, 2 * LANES)
        both_heads = cols(p, 2 * BLOCK)
        q2 = (qh[:, w], ql[:, w])
        k2 = (kh[:, w], kl[:, w])
        v2 = v[:, c]
        s2 = split(dn[:, c])
        d2 = (stacked(s2[0]), stacked(s2[1]))
        mixing = split(side_by_side(jnp.where(mask, both(nt, d2, v2), 0.0)))
        gql[:, w] = three(nn, mixing, (stacked(k2[0]), stacked(k2[1])))
        vv = stacked(v2)
        back = jnp.where(back_mask, nt(vv, s2[0]) + nt(vv, s2[1]), 0.0)
        back = split(side_by_side(back))
        gkl[:, w] = three(nn, back, (stacked(q2[0]), stacked(q2[1])))
        gvl[:, c] = three(nn, (sth[:, both_heads], stl[:, both_heads]), d2)


def third_kernel(got, g, qh, ql, numl, den, send, dd):
    chips = send.shape[0]
    rows = WIDE // chips
    run = jnp.zeros((rows, LANES), F32)
    for m in reversed(range(chips)):
        send[m, :rows, :] = run
        run = run + got[m, rows:, :]
    state = got[:, :rows, :].reshape(WIDE, LANES)
    sums_p, sums_m = [], []
    for p in range(PAIRS):
        c = cols(p)
        w = cols(p, 2 * LANES)
        q2 = (qh[:, w], ql[:, w])
        numer = numl[:, c] + three(nt, q2, split(unpack(state[c])))
        d = den[:, c]
        dden = -head_sum(g[:, c].astype(F32) * (numer / d)) / d
        dd[:, c] = dden
        full = q2[0].astype(F32) + q2[1].astype(F32)
        sums_p.append(jnp.sum(full[:, :LANES] * dden, 0, keepdims=True))
        sums_m.append(jnp.sum(full[:, LANES:] * dden, 0, keepdims=True))
    sums = jnp.concatenate(sums_p + sums_m + [jnp.zeros((4, LANES), F32)], 0)
    send[:, rows:, :] = jnp.broadcast_to(sums[None], (chips, 8, LANES))


def feature_back(f2, grad):
    full = f2[0].astype(F32) + f2[1].astype(F32)
    plus, minus = full[:, :LANES], full[:, LANES:]
    first, second = grad[:, :LANES], grad[:, LANES:]
    return plus * (first - head_sum(plus * first)) - minus * (second - head_sum(minus * second))


def twice(x):
    return jnp.concatenate([x, x], 1)


def fourth_kernel(got, q, wq, qh, ql, dn, dd, ksum, cumk, gql, gkl, whole, gq_map, gk_all):
    rows = WIDE // got.shape[0]
    state = got[:, :rows, :].reshape(WIDE, LANES)
    tri = jnp.where(causal_back(BLOCK), 1.0, 0.0).astype(BF16)
    for p in range(PAIRS):
        c = cols(p)
        w = cols(p, 2 * LANES)
        q2 = (qh[:, w], ql[:, w])
        dden = twice(dd[:, c])
        sums = jnp.concatenate([ksum[p : p + 1, :], ksum[p + PAIRS : p + PAIRS + 1, :]], 1)
        grad = gql[:, w] + three(nn, split(dn[:, c]), split(unpack(state[c])))
        grad = grad + dden * (sums + cumk[:, w])
        dzq = feature_back(q2, grad)
        z2 = split(dzq)
        whole[:, c] = both(nt, z2, wq[c])
        qt = q[:, c].T
        gq_map[c, :] = nn(qt, z2[0]) + nn(qt, z2[1])
        later = split((q2[0].astype(F32) + q2[1].astype(F32)) * dden)
        gk_all[:, w] = gkl[:, w] + nn(tri, later[0]) + nn(tri, later[1])


def fifth_kernel(sizes, got, k, v, kh, kl, gkl, gq_map, send, dz):
    chips = send.shape[0]
    rows = WIDE // chips
    me = chip(sizes)
    acc = jnp.zeros((8, LANES), F32)
    for m in range(chips):
        acc = acc + jnp.where(m > me, got[m, rows:, :], 0.0)
    later = got[:, :rows, :].reshape(WIDE, LANES)
    out = []
    for p in range(PAIRS):
        c = cols(p)
        w = cols(p, 2 * LANES)
        k2 = (kh[:, w], kl[:, w])
        sums = jnp.concatenate([acc[p : p + 1], acc[p + PAIRS : p + PAIRS + 1]], 1)
        grad = gkl[:, w] + sums + nn(
            twice(v[:, c]), jnp.concatenate(split(unpack(later[c])), 0)
        )
        dzk = feature_back(k2, grad)
        dz[:, c] = dzk
        z2 = split(dzk)
        kt = k[:, c].T
        out.append(
            pack(jnp.concatenate([gq_map[c, :], nn(kt, z2[0]) + nn(kt, z2[1])], 1))
        )
    send[...] = jnp.concatenate(out, 0).reshape(chips, rows, LANES)


def sixth_kernel(got, wk, kh, kl, gvl, dz, whole):
    rows = WIDE // got.shape[0]
    later = got[:, :rows, :].reshape(WIDE, LANES)
    for p in range(PAIRS):
        c = cols(p)
        w = cols(p, 2 * LANES)
        whole[:, c] = both(nt, split(dz[:, c]), wk[c])
        grad = gvl[:, c] + three(nt, (kh[:, w], kl[:, w]), split(unpack(later[c])))
        whole[:, WIDE + p * LANES : WIDE + (p + 1) * LANES] = grad


def theirs_kernel(whole, send):
    send[...] = whole[pl.ds(pl.multiple_of((1 - core()) * TOK, TOK), TOK), :]


def finish_kernel(whole, got, *outs):
    own = whole[pl.ds(pl.multiple_of(core() * TOK, TOK), TOK), :]
    other = got[1 - core()]
    first = core() == 0
    for i, out in enumerate(outs):
        lanes = slice(i * WIDE, (i + 1) * WIDE)
        a, b = own[:, lanes], other[:, lanes]
        out[:, :WIDE] = jnp.where(first, a, b).astype(BF16)
        out[:, WIDE:] = jnp.where(first, b, a).astype(BF16)


def sum_kernel(got, send):
    total = got[0]
    for m in range(1, got.shape[0]):
        total = total + got[m]
    send[...] = jnp.broadcast_to(total[None], send.shape)


def last_kernel(scale, got, gq, gk):
    for p in range(2 * PAIRS):
        x = got[cols(p), :] * scale
        y = pltpu.roll(x, HALF, 1)
        gq[2 * p] = x[:HALF, :HALF].astype(BF16)
        gq[2 * p + 1] = y[HALF:, :HALF].astype(BF16)
        gk[2 * p] = x[HALF:, :HALF].astype(BF16)
        gk[2 * p + 1] = y[:HALF, :HALF].astype(BF16)


def call(kernel, outs, *args, flops=10**8, space=pltpu.VMEM, scratch=(), room=32):
    shapes = [jax.ShapeDtypeStruct(shape, dtype) for shape, dtype in outs]
    moved = sum(a.size * a.dtype.itemsize for a in (*args, *shapes))
    return pl.pallas_call(
        kernel,
        out_shape=shapes,
        in_specs=[pl.BlockSpec(memory_space=space)] * len(args),
        out_specs=[pl.BlockSpec(memory_space=pltpu.VMEM)] * len(outs),
        scratch_shapes=scratch,
        compiler_params=pltpu.CompilerParams(vmem_limit_bytes=room * 2**20),
        cost_estimate=pl.CostEstimate(flops=flops, bytes_accessed=moved, transcendentals=0),
    )(*args)


def per_device(sizes, queries, keys, values, upstream, query_map, key_map):
    chips = sizes["z"] * sizes["x"]
    rows = WIDE // chips
    q, k, v, g = (a.reshape(TOK, 2 * WIDE) for a in (queries, keys, values, upstream))
    qmap = query_map.reshape(2 * WIDE, HALF)
    kmap = key_map.reshape(2 * WIDE, HALF)
    feats = ((BLOCK, 2 * WIDE), BF16)
    feats32 = ((BLOCK, 2 * WIDE), F32)
    flat = ((BLOCK, WIDE), F32)
    small = ((BLOCK, WIDE), BF16)
    scores = ((BLOCK, 2 * PAIRS * BLOCK), BF16)
    sums = ((8, LANES), F32)

    def across(a):
        return lax.all_gather(a, "core")

    def exchange(a):
        return lax.all_to_all(a, CHIPS, 0, 0)

    def start(a, b, maps, room):
        send, own, wide = call(
            start_kernel,
            [((TOK, 2 * WIDE), F32), ((TOK, 2 * WIDE), BF16), ((WIDE, LANES), BF16)],
            a, b, maps,
            space=pl.ANY,
            room=room,
            scratch=[
                pltpu.VMEM((TOK, 2 * WIDE), BF16),
                pltpu.VMEM((WIDE, HALF), BF16),
                pltpu.SemaphoreType.DMA((5,)),
            ],
        )
        return own, across(send), wide

    def finish(whole, count):
        (send,) = call(theirs_kernel, [((TOK, count * WIDE), F32)], whole)
        out = [((TOK, 2 * WIDE), BF16)] * count
        return call(finish_kernel, out, whole, across(send))

    own, got, wk = start(k, v, kmap, 60)
    send, k2, v2, kh, kl = call(
        keys_kernel, [((chips, rows + 8, LANES), F32), small, small, feats, feats], own, got, wk
    )
    first = exchange(send)
    own, got, wq = start(q, g, qmap, 32)
    q2, g2, qh, ql, numl, denl, sth, stl, cumk = call(
        queries_kernel,
        [small, small, feats, feats, flat, flat, scores, scores, feats32],
        own, got, wq, v2, kh, kl,
        flops=10**9,
    )
    send, den, dn, ksum = call(
        functools.partial(second_kernel, sizes),
        [((chips, 2 * rows, LANES), F32), flat, flat, sums],
        first, g2, qh, ql, denl,
    )
    second = exchange(send)
    gql, gkl, gvl = call(
        local_kernel, [feats32, feats32, flat], v2, qh, ql, kh, kl, sth, stl, dn, flops=10**9
    )
    send, dd = call(
        third_kernel,
        [((chips, rows + 8, LANES), F32), flat],
        second, g2, qh, ql, numl, den,
    )
    third = exchange(send)
    whole, gq_map, gkl = call(
        fourth_kernel,
        [flat, ((WIDE, LANES), F32), feats32],
        second, q2, wq, qh, ql, dn, dd, ksum, cumk, gql, gkl,
        flops=10**9,
    )
    (grad_q,) = finish(whole, 1)
    send, dz = call(
        functools.partial(fifth_kernel, sizes),
        [((chips, rows, LANES), F32), flat],
        third, k2, v2, kh, kl, gkl, gq_map,
    )
    got = exchange(send)
    (whole,) = call(
        sixth_kernel, [((BLOCK, 2 * WIDE), F32)], third, wk, kh, kl, gvl, dz, flops=10**9
    )
    grad_k, grad_v = finish(whole, 2)
    (send,) = call(sum_kernel, [((sizes["dp"], rows, LANES), F32)], got)
    got = lax.all_to_all(send, "dp", 0, 0)
    (send,) = call(sum_kernel, [((chips, rows, LANES), F32)], got)
    got = across(exchange(send))
    scale = float(BLOCK * chips * sizes["dp"]) ** (-0.5)
    heads = ((8, HALF, HALF), BF16)
    total_q, total_k = call(
        functools.partial(last_kernel, scale), [heads, heads], got.reshape(2 * WIDE, LANES)
    )
    shape = queries.shape
    return grad_q.reshape(shape), grad_k.reshape(shape), grad_v.reshape(shape), total_q, total_k


def physical(mesh):
    dp, ctx = mesh.devices.shape
    x = 4 if ctx % 8 == 0 and ctx > 8 else 2
    sizes = {"dp": dp, "z": ctx // (2 * x), "x": x, "core": 2}
    return Mesh(mesh.devices.reshape(tuple(sizes.values())), tuple(sizes)), sizes


def solution(mesh):
    inner, sizes = physical(mesh)
    tokens = P("dp", CTX, None)
    return jax.shard_map(
        functools.partial(per_device, sizes),
        mesh=inner,
        in_specs=(tokens,) * 4 + (P(), P()),
        out_specs=(tokens,) * 3 + (P(), P()),
        check_vma=False,
    )
```

time: 142 us -> 120 us (0.85)
  waiting for transfers between devices: 38.4 us -> 15.4 us
  blocking collectives: 51.6 us -> 58 us
  starting transfers between devices: 27 us -> 23.1 us
  local copies, waits for them, and re-layouts: 7.61 us -> 4.53 us
  Pallas kernels: 16.1 us -> 17.8 us
    all_to_all x4, waiting for transfers between devices: 38.4 us -> 15.4 us  [the longest x3 8.51 us: exchange(): return lax.all_to_all(a, CHIPS, 0, 0)]
    all_gather x5, blocking collectives: 17.1 us -> 26.2 us  [across(): return lax.all_gather(a, 'core')]
    all_to_all x4, starting transfers between devices: 27 us -> 23.1 us  [the longest x3 16.2 us: exchange(): return lax.all_to_all(a, CHIPS, 0, 0)]
    unnamed x38 -> x26, local copies, waits for them, and re-layouts: 7.61 us -> 4.53 us
    all_to_all x2, blocking collectives: 34.5 us -> 31.8 us  [exchange(): return lax.all_to_all(a, CHIPS, 0, 0)]
    pallas_call x10 -> x17, Pallas kernels: 16.1 us -> 17.8 us  [call(): pl.pallas_call(kernel, out_shape=shapes, in_specs=[pl.BlockSpec(memory_sp...]
  transfers between devices with their start and end apart: 4 -> 4, of which waited for: 4 -> 3; matrix products, arithmetic and copies ran while one was open for 0% -> 0% of each run, Pallas kernels for 5% -> 7%
where the time goes in v2:
time: 120 us
  blocking collectives  58 us (48%)
  starting transfers between devices  23.1 us (19%)
  Pallas kernels  17.8 us (15%)
  waiting for transfers between devices  15.4 us (13%)
  local copies, waits for them, and re-layouts  4.53 us (4%)
    all_to_all x2, blocking collectives, exchange(): return lax.all_to_all(a, CHIPS, 0, 0)  31.8 us
    all_gather x5, blocking collectives, across(): return lax.all_gather(a, 'core')  26.2 us
    pallas_call x17, Pallas kernels, call(): pl.pallas_call(kernel, out_shape=shapes, in_specs=[pl.BlockSpec(memory_sp...  17.8 us
    all_to_all x3, starting transfers between devices, exchange(): return lax.all_to_all(a, CHIPS, 0, 0)  16.2 us
    all_to_all x3, waiting for transfers between devices, exchange(): return lax.all_to_all(a, CHIPS, 0, 0)  8.51 us
    all_to_all x1, waiting for transfers between devices, per_device(): got = lax.all_to_all(send, 'dp', 0, 0)  6.86 us
    all_to_all x1, starting transfers between devices, per_device(): got = lax.all_to_all(send, 'dp', 0, 0)  6.82 us
    unnamed x26, local copies, waits for them, and re-layouts  4.53 us
  transfers between devices with their start and end apart: 4, of which 3 were waited for; matrix products, arithmetic and copies ran while one was open for 0% of the time, Pallas kernels for 7%

profile of v2, /device:TPU:1, one launch (start us, length us, event | category | flops | bytes accessed | tf_op | source)
XLA Modules:
  0.0 119.6 jit_solution(1158140185839930666)
XLA Ops:
  0.6 1.9 %shard_map.101 = (f32[128,512]{1,0:T(8,128)}, bf16[128,512]{1,0:T(8,128)(2,1)}, bf16[256,128]{1,0:T(8,128)(2,1)}) custom-call(bf16[128,512]{1,0:T(8,128)(2,1)} %bitcast.22, bf16[128,512]{1,0:T(8,128)(2,1)} %bitcast.23, bf16[512,64]{1,0:T(8,128)(2,1)} %bitcast.24), custom_call_target="tpu_custom_call" | custom-call | flops 100000000 | bytes 786432 | tf_op jit(solution)/shard_map/pallas_call | solution.py:386
  2.6 0.0 copy-start.3
  2.6 0.0 copy-start.4
  2.6 9.0 %all-gather = f32[256,512]{1,0:T(8,128)S(1)} all-gather(f32[128,512]{1,0:T(8,128)} %get-tuple-element.44), channel_id=2, replica_groups=mesh['dp'=8,'z'=8,'x'=4,'core'=2] {'core'}, dimensions={0}, use_global_device_ids=true | all-gather | bytes 786432 | tf_op jit(solution)/shard_map/all_gather | solution.py:411
  11.6 0.0 copy-done.3
  11.6 0.0 copy-done.4
  11.6 1.9 %shard_map.102 = (f32[32,16,128]{2,1,0:T(8,128)}, bf16[256,256]{1,0:T(8,128)(2,1)S(1)}, bf16[256,256]{1,0:T(8,128)(2,1)S(1)}, bf16[256,512]{1,0:T(8,128)(2,1)S(1)}, bf16[256,512]{1,0:T(8,128)(2,1)S(1)}) custom-call(bf16[128,512]{1,0:T(8,128)(2,1)S(1)} %copy-done.3, f32[2,128,512]{2,1,0:T(8,128)S(1)} %bitcast.14, bf16[256,128]{1,0:T(8,128)(2,1)S(1)} %copy-done.4), custom_call_target="tpu_custom_call" | custom-call | flops 100000000 | bytes 1769472 | tf_op jit(solution)/shard_map/pallas_call | solution.py:386
  13.5 0.0 copy-start
  13.5 0.0 copy-start.1
  13.5 0.0 copy-start.2
  13.5 7.6 %all-to-all-start = ((f32[32,16,128]{2,1,0:T(8,128)}), f32[32,16,128]{2,1,0:T(8,128)S(1)}, u32[]{:S(2)}, u32[]{:S(2)}) async-start(f32[32,16,128]{2,1,0:T(8,128)} %get-tuple-element.46), calls=%async_computation | async-start | bytes 524288 | tf_op jit(solution)/shard_map/all_to_all | solution.py:414
  21.2 0.0 copy-done
  21.2 0.0 copy-done.1
  21.2 0.0 copy-done.2
  21.2 0.3 shard_map.103
  21.5 2.5 %all-gather.1 = f32[256,512]{1,0:T(8,128)S(1)} all-gather(f32[128,512]{1,0:T(8,128)S(1)} %get-tuple-element.48), channel_id=3, replica_groups=mesh['dp'=8,'z'=8,'x'=4,'core'=2] {'core'}, dimensions={0}, use_global_device_ids=true | all-gather | bytes 786432 | tf_op jit(solution)/shard_map/all_gather | solution.py:411
  24.0 2.8 %shard_map.104 = (bf16[256,256]{1,0:T(8,128)(2,1)S(1)}, bf16[256,256]{1,0:T(8,128)(2,1)S(1)}, bf16[256,512]{1,0:T(8,128)(2,1)S(1)}, bf16[256,512]{1,0:T(8,128)(2...) custom-call(bf16[128,512]{1,0:T(8,128)(2,1)S(1)} %get-tuple-element., ...), custom_call_target="tpu_custom_call" | custom-call | flops 1000000000 | bytes 4259840 | tf_op jit(solution)/shard_map/pallas_call | solution.py:386
  26.8 0.0 copy-start.5
  26.8 0.8 copy-done.5
  27.6 0.0 copy-start.7
  27.6 0.8 copy-done.7
  28.4 0.0 copy-start.9
  28.4 0.8 copy-done.9
  29.2 3.5 %all-to-all-done.got = f32[32,16,128]{2,1,0:T(8,128)S(1)} async-done(((f32[32,16,128]{2,1,0:T(8,128)}), f32[32,16,128]{2,1,0:T(8,128)S(1)}, u32[]{:S(2)}, u32[]{:S(2)}) %all-to-all-start) | async-done | bytes 262176 | tf_op jit(solution)/shard_map/all_to_all | solution.py:414
  32.7 1.0 shard_map.105
  33.7 17.4 %all_to_all.30.got = f32[32,16,128]{2,1,0:T(8,128)S(1)} all-to-all(f32[32,16,128]{2,1,0:T(8,128)S(1)} %get-tuple-element.57), channel_id=1, replica_groups=mesh['dp'=8,'z'=8,'x'=4,'core'=2] {'z','x'}, dimensions={0} | all-to-all | bytes 524288 | tf_op jit(solution)/shard_map/all_to_all | solution.py:414
  51.1 1.4 %shard_map.106 = (f32[32,16,128]{2,1,0:T(8,128)}, f32[256,256]{1,0:T(8,128)S(1)}) custom-call(f32[32,16,128]{2,1,0:T(8,128)S(1)} %all_to_all.30.got, bf16[256,256]{1,0:T(8,128)(2,1)S(1)} %get-tuple-element.53.g, bf16[256,512]{1,0:T(8,128)(2,1)S(1)} %get-tuple-element.54.qh, bf16[256,512]{1,0:T(8,128)(2,1)S(1)} %get-tuple-element.55.ql, ...), custom_call_target="tpu_custom_call" | custom-call | flops 100000000 | bytes 1966080 | tf_op jit(solution)/shard_map/pallas_call | solution.py:386
  52.5 0.0 copy-start.8
  52.5 4.7 %all-to-all-start.2 = ((f32[32,16,128]{2,1,0:T(8,128)}), f32[32,16,128]{2,1,0:T(8,128)S(1)}, u32[]{:S(2)}, u32[]{:S(2)}) async-start(f32[32,16,128]{2,1,0:T(8,128)} %get-tuple-element.70), calls=%async_computation.2 | async-start | bytes 524288 | tf_op jit(solution)/shard_map/all_to_all | solution.py:414
  57.3 0.0 copy-done.8
  57.3 0.0 copy-start.10
  57.3 1.0 copy-done.10
  58.3 0.0 copy-start.6
  58.3 2.2 %shard_map.107 = (f32[256,512]{1,0:T(8,128)S(1)}, f32[256,512]{1,0:T(8,128)S(1)}, f32[256,256]{1,0:T(8,128)S(1)}) custom-call(bf16[256,256]{1,0:T(8,128)(2,1)S(1)} %get-tuple-element.50.v, bf16[256,512]{1,0:T(8,128)(2,1)S(1)} %get-tuple-element.54.qh, bf16[256,512]{1,0:T(8,128)(2,1)S(1)} %get-tuple-element.55.ql, bf16[256,512]{1,0:T(8,128)(2,1)S(1)} %get-tuple-element.51.kh, ...), custom_call_target="tpu_custom_call" | custom-call | flops 1000000000 | bytes 3801088 | tf_op jit(solution)/shard_map/pallas_call | solution.py:386
  60.5 0.0 copy-start.11
  60.5 0.7 copy-done.11
  61.2 0.0 copy-done.6
  61.2 1.4 %shard_map.108 = (f32[256,256]{1,0:T(8,128)S(1)}, f32[256,128]{1,0:T(8,128)S(1)}, f32[256,512]{1,0:T(8,128)S(1)}) custom-call(f32[32,16,128]{2,1,0:T(8,128)S(1)} %all_to_all.30.got, bf16[256,256]{1,0:T(8,128)(2,1)S(1)} %get-tuple-element.58.q, bf16[256,128]{1,0:T(8,128)(2,1)S(1)} %get-tuple-element.49.wq, bf16[256,512]{1,0:T(8,128)(2,1)S(1)} %get-tuple-element.54.qh, ...), custom_call_target="tpu_custom_call" | custom-call | flops 1000000000 | bytes 4001792 | tf_op jit(solution)/shard_map/pallas_call | solution.py:386
  62.7 5.0 %all-to-all-done.2.got = f32[32,16,128]{2,1,0:T(8,128)S(1)} async-done(((f32[32,16,128]{2,1,0:T(8,128)}), f32[32,16,128]{2,1,0:T(8,128)S(1)}, u32[]{:S(2)}, u32[]{:S(2)}) %all-to-all-start.2) | async-done | bytes 262176 | tf_op jit(solution)/shard_map/all_to_all | solution.py:414
  67.7 0.9 shard_map.111
  68.6 14.4 %all_to_all.31.got = f32[32,8,128]{2,1,0:T(8,128)S(1)} all-to-all(f32[32,8,128]{2,1,0:T(8,128)S(1)} %get-tuple-element.78), channel_id=1, replica_groups=mesh['dp'=8,'z'=8,'x'=4,'core'=2] {'z','x'}, dimensions={0} | all-to-all | bytes 262144 | tf_op jit(solution)/shard_map/all_to_all | solution.py:414
  83.0 0.6 shard_map.115
  83.7 6.8 %all-to-all-start.4 = ((f32[8,8,128]{2,1,0:T(8,128)}), f32[8,8,128]{2,1,0:T(8,128)S(1)}, u32[]{:S(2)}, u32[]{:S(2)}) async-start(f32[8,8,128]{2,1,0:T(8,128)} %shard_map.115), calls=%async_computation.4 | async-start | bytes 65536 | tf_op jit(solution)/shard_map/all_to_all | solution.py:481
  90.5 6.9 %all-to-all-done.4.got = f32[8,8,128]{2,1,0:T(8,128)S(1)} async-done(((f32[8,8,128]{2,1,0:T(8,128)}), f32[8,8,128]{2,1,0:T(8,128)S(1)}, u32[]{:S(2)}, u32[]{:S(2)}) %all-to-all-start.4) | async-done | bytes 32800 | tf_op jit(solution)/shard_map/all_to_all | solution.py:481
  97.3 0.7 shard_map.116
  98.0 3.9 %all-to-all-start.5 = ((f32[32,8,128]{2,1,0:T(8,128)}), f32[32,8,128]{2,1,0:T(8,128)S(1)}, u32[]{:S(2)}, u32[]{:S(2)}) async-start(f32[32,8,128]{2,1,0:T(8,128)} %shard_map.116), calls=%async_computation.5 | async-start | bytes 262144 | tf_op jit(solution)/shard_map/all_to_all | solution.py:414
  101.9 6.4 %all-gather.2 = f32[256,256]{1,0:T(8,128)S(1)} all-gather(f32[128,256]{1,0:T(8,128)S(1)} %shard_map.109), channel_id=4, replica_groups=mesh['dp'=8,'z'=8,'x'=4,'core'=2] {'core'}, dimensions={0}, use_global_device_ids=true | all-gather | bytes 393216 | tf_op jit(solution)/shard_map/all_gather | solution.py:411
  108.2 0.0 copy-start.12
  108.2 0.7 shard_map.110
  108.9 0.3 copy-done.12
  109.2 0.4 shard_map.112.whole
  109.7 2.2 %all-gather.3 = f32[256,512]{1,0:T(8,128)S(1)} all-gather(f32[128,512]{1,0:T(8,128)S(1)} %shard_map.113), channel_id=5, replica_groups=mesh['dp'=8,'z'=8,'x'=4,'core'=2] {'core'}, dimensions={0}, use_global_device_ids=true | all-gather | bytes 786432 | tf_op jit(solution)/shard_map/all_gather | solution.py:411
  111.9 0.7 shard_map.114
  112.6 0.0 all-to-all-done.5
  112.6 6.1 %all-gather.4 = f32[64,8,128]{2,1,0:T(8,128)S(1)} all-gather(f32[32,8,128]{2,1,0:T(8,128)S(1)} %all-to-all-done.5), channel_id=6, replica_groups=mesh['dp'=8,'z'=8,'x'=4,'core'=2] {'core'}, dimensions={0}, use_global_device_ids=true | all-gather | bytes 393216 | tf_op jit(solution)/shard_map/all_gather | solution.py:411
  118.8 0.8 shard_map.117
  (2 shorter events, 0.0 us)
Async XLA Ops:
  2.6 9.1 %copy-start.3 = (bf16[128,512]{1,0:T(8,128)(2,1)S(1)}, bf16[128,512]{1,0:T(8,128)(2,1)}, u32[]{:S(2)}) copy-start(bf16[128,512]{1,0:T(8,128)(2,1)} %get-tuple-element.43.own) | copy-start | bytes 393220
  2.6 9.0 %copy-start.4 = (bf16[256,128]{1,0:T(8,128)(2,1)S(1)}, bf16[256,128]{1,0:T(8,128)(2,1)}, u32[]{:S(2)}) copy-start(bf16[256,128]{1,0:T(8,128)(2,1)} %get-tuple-element.45.wk) | copy-start | bytes 196612
  13.5 7.7 %copy-start = (bf16[1,128,512]{2,1,0:T(8,128)(2,1)S(1)}, bf16[1,128,512]{2,1,0:T(8,128)(2,1)}, u32[]{:S(2)}) copy-start(bf16[1,128,512]{2,1,0:T(8,128)(2,1)} %param.6) | copy-start | bytes 393220
  13.5 7.7 %copy-start.1 = (bf16[1,128,512]{2,1,0:T(8,128)(2,1)S(1)}, bf16[1,128,512]{2,1,0:T(8,128)(2,1)}, u32[]{:S(2)}) copy-start(bf16[1,128,512]{2,1,0:T(8,128)(2,1)} %param.9) | copy-start | bytes 393220
  13.5 7.7 %copy-start.2 = (bf16[8,64,64]{2,1,0:T(8,128)(2,1)S(1)}, bf16[8,64,64]{2,1,0:T(8,128)(2,1)}, u32[]{:S(2)}) copy-start(bf16[8,64,64]{2,1,0:T(8,128)(2,1)} %param.10) | copy-start | bytes 196612
  13.5 19.2 %all-to-all-start = ((f32[32,16,128]{2,1,0:T(8,128)}), f32[32,16,128]{2,1,0:T(8,128)S(1)}, u32[]{:S(2)}, u32[]{:S(2)}) async-start(f32[32,16,128]{2,1,0:T(8,128)} %get-tuple-element.46), calls=%async_computation | async-start | bytes 524288 | tf_op jit(solution)/shard_map/all_to_all | solution.py:414
  26.8 0.8 copy-start.5
  27.6 0.8 copy-start.7
  28.4 0.8 copy-start.9
  52.5 4.7 %copy-start.8 = (bf16[256,1024]{1,0:T(8,128)(2,1)S(1)}, bf16[256,1024]{1,0:T(8,128)(2,1)}, u32[]{:S(2)}) copy-start(bf16[256,1024]{1,0:T(8,128)(2,1)} %copy-done.7) | copy-start | bytes 1572868
  52.5 15.2 %all-to-all-start.2 = ((f32[32,16,128]{2,1,0:T(8,128)}), f32[32,16,128]{2,1,0:T(8,128)S(1)}, u32[]{:S(2)}, u32[]{:S(2)}) async-start(f32[32,16,128]{2,1,0:T(8,128)} %get-tuple-element.70), calls=%async_computation.2 | async-start | bytes 524288 | tf_op jit(solution)/shard_map/all_to_all | solution.py:414
  57.3 1.0 copy-start.10
  58.3 2.9 %copy-start.6 = (f32[256,512]{1,0:T(8,128)S(1)}, f32[256,512]{1,0:T(8,128)}, u32[]{:S(2)}) copy-start(f32[256,512]{1,0:T(8,128)} %copy-done.5) | copy-start | bytes 1572868
  60.5 0.7 copy-start.11
  83.7 13.7 %all-to-all-start.4 = ((f32[8,8,128]{2,1,0:T(8,128)}), f32[8,8,128]{2,1,0:T(8,128)S(1)}, u32[]{:S(2)}, u32[]{:S(2)}) async-start(f32[8,8,128]{2,1,0:T(8,128)} %shard_map.115), calls=%async_computation.4 | async-start | bytes 65536 | tf_op jit(solution)/shard_map/all_to_all | solution.py:481
  98.0 14.6 %all-to-all-start.5 = ((f32[32,8,128]{2,1,0:T(8,128)}), f32[32,8,128]{2,1,0:T(8,128)S(1)}, u32[]{:S(2)}, u32[]{:S(2)}) async-start(f32[32,8,128]{2,1,0:T(8,128)} %shard_map.116), calls=%async_computation.5 | async-start | bytes 262144 | tf_op jit(solution)/shard_map/all_to_all | solution.py:414
  108.2 1.0 copy-start.12

commit v3 on v2

--- a/solution.py
+++ b/solution.py
@@ -179,11 +179,9 @@
     send[:, rows:, :] = jnp.broadcast_to(sums[None], (chips, 8, LANES))
 
 
-def queries_kernel(own, got, wq, v, kh, kl, q, g, qh, ql, num, den, sth, stl, cumk):
+def queries_kernel(own, got, wq, v, kh, kl, q, g, qh, ql, num, den):
     assemble(own, got, q, g)
     mask = causal(2 * BLOCK)
-    back_mask = causal_back(2 * BLOCK)
-    tri = jnp.where(causal(BLOCK), 1.0, 0.0).astype(BF16)
     for p in range(PAIRS):
         c = cols(p)
         w = cols(p, 2 * LANES)
@@ -191,7 +189,6 @@
         q2 = split(jnp.concatenate([pq, mq], 1))
         qh[:, w], ql[:, w] = q2
         k2 = (kh[:, w], kl[:, w])
-        cumk[:, w] = nn(tri, k2[0]) + nn(tri, k2[1])
         scores = three(nt, (stacked(q2[0]), stacked(q2[1])), k2)
         scores = side_by_side(jnp.where(mask, scores, 0.0))
         v2 = stacked(v[:, c])
@@ -199,11 +196,6 @@
         out = both(nn, split(scores), jnp.concatenate([v2, ones], 1))
         num[:, c] = out[:, :LANES]
         den[:, c] = out[:, LANES:]
-        back = three(nt, (stacked(k2[0]), stacked(k2[1])), q2)
-        hi, lo = split(side_by_side(jnp.where(back_mask, back, 0.0)))
-        both_heads = cols(p, 2 * BLOCK)
-        sth[:, both_heads] = hi
-        stl[:, both_heads] = lo
 
 
 def second_kernel(sizes, got, g, qh, ql, denl, send, den, dn, ksum):
@@ -233,13 +225,13 @@
     send[:, rows:, :] = jnp.concatenate(out, 0).reshape(chips, rows, LANES)
 
 
-def local_kernel(v, qh, ql, kh, kl, sth, stl, dn, gql, gkl, gvl):
+def local_kernel(v, qh, ql, kh, kl, dn, gql, gvl, token):
+    token[...] = jnp.zeros_like(token)
     mask = causal(2 * BLOCK)
     back_mask = causal_back(2 * BLOCK)
     for p in range(PAIRS):
         c = cols(p)
         w = cols(p, 2 * LANES)
-        both_heads = cols(p, 2 * BLOCK)
         q2 = (qh[:, w], ql[:, w])
         k2 = (kh[:, w], kl[:, w])
         v2 = v[:, c]
@@ -247,14 +239,12 @@
         d2 = (stacked(s2[0]), stacked(s2[1]))
         mixing = split(side_by_side(jnp.where(mask, both(nt, d2, v2), 0.0)))
         gql[:, w] = three(nn, mixing, (stacked(k2[0]), stacked(k2[1])))
-        vv = stacked(v2)
-        back = jnp.where(back_mask, nt(vv, s2[0]) + nt(vv, s2[1]), 0.0)
-        back = split(side_by_side(back))
-        gkl[:, w] = three(nn, back, (stacked(q2[0]), stacked(q2[1])))
-        gvl[:, c] = three(nn, (sth[:, both_heads], stl[:, both_heads]), d2)
-
-
-def third_kernel(got, g, qh, ql, numl, den, send, dd):
+        scores = three(nt, (stacked(k2[0]), stacked(k2[1])), q2)
+        scores = split(side_by_side(jnp.where(back_mask, scores, 0.0)))
+        gvl[:, c] = three(nn, scores, d2)
+
+
+def third_kernel(got, g, qh, ql, numl, den, _, send, dd):
     chips = send.shape[0]
     rows = WIDE // chips
     run = jnp.zeros((rows, LANES), F32)
@@ -289,28 +279,35 @@
     return jnp.concatenate([x, x], 1)
 
 
-def fourth_kernel(got, q, wq, qh, ql, dn, dd, ksum, cumk, gql, gkl, whole, gq_map, gk_all):
+def fourth_kernel(got, q, v, wq, qh, ql, kh, kl, dn, dd, ksum, gql, whole, gq_map, gk_all):
     rows = WIDE // got.shape[0]
     state = got[:, :rows, :].reshape(WIDE, LANES)
-    tri = jnp.where(causal_back(BLOCK), 1.0, 0.0).astype(BF16)
+    tri = jnp.where(causal(BLOCK), 1.0, 0.0).astype(BF16)
+    tri_back = jnp.where(causal_back(BLOCK), 1.0, 0.0).astype(BF16)
+    back_mask = causal_back(2 * BLOCK)
     for p in range(PAIRS):
         c = cols(p)
         w = cols(p, 2 * LANES)
         q2 = (qh[:, w], ql[:, w])
         dden = twice(dd[:, c])
         sums = jnp.concatenate([ksum[p : p + 1, :], ksum[p + PAIRS : p + PAIRS + 1, :]], 1)
-        grad = gql[:, w] + three(nn, split(dn[:, c]), split(unpack(state[c])))
-        grad = grad + dden * (sums + cumk[:, w])
+        s2 = split(dn[:, c])
+        grad = gql[:, w] + three(nn, s2, split(unpack(state[c])))
+        grad = grad + dden * (sums + (nn(tri, kh[:, w]) + nn(tri, kl[:, w])))
         dzq = feature_back(q2, grad)
         z2 = split(dzq)
         whole[:, c] = both(nt, z2, wq[c])
         qt = q[:, c].T
         gq_map[c, :] = nn(qt, z2[0]) + nn(qt, z2[1])
         later = split((q2[0].astype(F32) + q2[1].astype(F32)) * dden)
-        gk_all[:, w] = gkl[:, w] + nn(tri, later[0]) + nn(tri, later[1])
-
-
-def fifth_kernel(sizes, got, k, v, kh, kl, gkl, gq_map, send, dz):
+        vv = stacked(v[:, c])
+        back = jnp.where(back_mask, nt(vv, s2[0]) + nt(vv, s2[1]), 0.0)
+        back = split(side_by_side(back))
+        gk = three(nn, back, (stacked(q2[0]), stacked(q2[1])))
+        gk_all[:, w] = gk + (nn(tri_back, later[0]) + nn(tri_back, later[1]))
+
+
+def fifth_kernel(sizes, got, k, v, kh, kl, gkl, gq_map, _, send, dz):
     chips = send.shape[0]
     rows = WIDE // chips
     me = chip(sizes)
@@ -337,7 +334,7 @@
     send[...] = jnp.concatenate(out, 0).reshape(chips, rows, LANES)
 
 
-def sixth_kernel(got, wk, kh, kl, gvl, dz, whole):
+def sixth_kernel(got, wk, kh, kl, gvl, dz, _, whole):
     rows = WIDE // got.shape[0]
     later = got[:, :rows, :].reshape(WIDE, LANES)
     for p in range(PAIRS):
@@ -353,6 +350,8 @@
 
 
 def finish_kernel(whole, got, *outs):
+    *outs, token = outs
+    token[...] = jnp.zeros_like(token)
     own = whole[pl.ds(pl.multiple_of(core() * TOK, TOK), TOK), :]
     other = got[1 - core()]
     first = core() == 0
@@ -363,7 +362,8 @@
         out[:, WIDE:] = jnp.where(first, b, a).astype(BF16)
 
 
-def sum_kernel(got, send):
+def sum_kernel(got, *rest):
+    send = rest[-1]
     total = got[0]
     for m in range(1, got.shape[0]):
         total = total + got[m]
@@ -389,7 +389,7 @@
         in_specs=[pl.BlockSpec(memory_space=space)] * len(args),
         out_specs=[pl.BlockSpec(memory_space=pltpu.VMEM)] * len(outs),
         scratch_shapes=scratch,
-        compiler_params=pltpu.CompilerParams(vmem_limit_bytes=room * 2**20),
+        compiler_params=pltpu.CompilerParams(vmem_limit_bytes=int(room * 2**20)),
         cost_estimate=pl.CostEstimate(flops=flops, bytes_accessed=moved, transcendentals=0),
     )(*args)
 
@@ -404,7 +404,6 @@
     feats32 = ((BLOCK, 2 * WIDE), F32)
     flat = ((BLOCK, WIDE), F32)
     small = ((BLOCK, WIDE), BF16)
-    scores = ((BLOCK, 2 * PAIRS * BLOCK), BF16)
     sums = ((8, LANES), F32)
 
     def across(a):
@@ -430,7 +429,7 @@
 
     def finish(whole, count):
         (send,) = call(theirs_kernel, [((TOK, count * WIDE), F32)], whole)
-        out = [((TOK, 2 * WIDE), BF16)] * count
+        out = [((TOK, 2 * WIDE), BF16)] * count + [sums]
         return call(finish_kernel, out, whole, across(send))
 
     own, got, wk = start(k, v, kmap, 60)
@@ -439,9 +438,9 @@
     )
     first = exchange(send)
     own, got, wq = start(q, g, qmap, 32)
-    q2, g2, qh, ql, numl, denl, sth, stl, cumk = call(
+    q2, g2, qh, ql, numl, denl = call(
         queries_kernel,
-        [small, small, feats, feats, flat, flat, scores, scores, feats32],
+        [small, small, feats, feats, flat, flat],
         own, got, wq, v2, kh, kl,
         flops=10**9,
     )
@@ -451,35 +450,38 @@
         first, g2, qh, ql, denl,
     )
     second = exchange(send)
-    gql, gkl, gvl = call(
-        local_kernel, [feats32, feats32, flat], v2, qh, ql, kh, kl, sth, stl, dn, flops=10**9
+    gql, gvl, token = call(
+        local_kernel, [feats32, flat, sums], v2, qh, ql, kh, kl, dn, flops=10**9
     )
     send, dd = call(
         third_kernel,
         [((chips, rows + 8, LANES), F32), flat],
-        second, g2, qh, ql, numl, den,
+        second, g2, qh, ql, numl, den, token,
     )
     third = exchange(send)
     whole, gq_map, gkl = call(
         fourth_kernel,
         [flat, ((WIDE, LANES), F32), feats32],
-        second, q2, wq, qh, ql, dn, dd, ksum, cumk, gql, gkl,
+        second, q2, v2, wq, qh, ql, kh, kl, dn, dd, ksum, gql,
         flops=10**9,
     )
-    (grad_q,) = finish(whole, 1)
+    grad_q, token = finish(whole, 1)
     send, dz = call(
         functools.partial(fifth_kernel, sizes),
         [((chips, rows, LANES), F32), flat],
-        third, k2, v2, kh, kl, gkl, gq_map,
+        third, k2, v2, kh, kl, gkl, gq_map, token,
     )
     got = exchange(send)
+    (send,) = call(sum_kernel, [((sizes["dp"], rows, LANES), F32)], got)
     (whole,) = call(
-        sixth_kernel, [((BLOCK, 2 * WIDE), F32)], third, wk, kh, kl, gvl, dz, flops=10**9
-    )
-    grad_k, grad_v = finish(whole, 2)
-    (send,) = call(sum_kernel, [((sizes["dp"], rows, LANES), F32)], got)
+        sixth_kernel,
+        [((BLOCK, 2 * WIDE), F32)],
+        third, wk, kh, kl, gvl, dz, send,
+        flops=10**9,
+    )
+    grad_k, grad_v, token = finish(whole, 2)
     got = lax.all_to_all(send, "dp", 0, 0)
-    (send,) = call(sum_kernel, [((chips, rows, LANES), F32)], got)
+    (send,) = call(sum_kernel, [((chips, rows, LANES), F32)], got, token)
     got = across(exchange(send))
     scale = float(BLOCK * chips * sizes["dp"]) ** (-0.5)
     heads = ((8, HALF, HALF), BF16)

time: 120 us -> 118 us (0.983)
  blocking collectives: 58 us -> 54.5 us
  local copies, waits for them, and re-layouts: 4.53 us -> 2.58 us
  Pallas kernels: 17.8 us -> 19.2 us
    all_to_all x3, waiting for transfers between devices: 8.51 us -> 15.8 us  [exchange(): return lax.all_to_all(a, CHIPS, 0, 0)]
    all_to_all x1, waiting for transfers between devices: 6.86 us -> 0.7 us  [per_device(): got = lax.all_to_all(send, 'dp', 0, 0)]
    all_to_all x2, blocking collectives: 31.8 us -> 29.4 us  [exchange(): return lax.all_to_all(a, CHIPS, 0, 0)]
    unnamed x26 -> x18, local copies, waits for them, and re-layouts: 4.53 us -> 2.58 us
    pallas_call x17, Pallas kernels: 17.8 us -> 19.2 us  [call(): pl.pallas_call(kernel, out_shape=shapes, in_specs=[pl.BlockSpec(memory_sp...]
  transfers between devices with their start and end apart: 4 -> 4, of which waited for: 3 -> 4; matrix products, arithmetic and copies ran while one was open for 0% -> 0% of each run, Pallas kernels for 7% -> 8%
where the time goes in v3:
time: 118 us
  blocking collectives  54.5 us (46%)
  starting transfers between devices  24.2 us (21%)
  Pallas kernels  19.2 us (16%)
  waiting for transfers between devices  16.5 us (14%)
  local copies, waits for them, and re-layouts  2.58 us (2%)
    all_to_all x2, blocking collectives, exchange(): return lax.all_to_all(a, CHIPS, 0, 0)  29.4 us
    all_gather x5, blocking collectives, across(): return lax.all_gather(a, 'core')  25.1 us
    pallas_call x17, Pallas kernels, call(): pl.pallas_call(kernel, out_shape=shapes, in_specs=[pl.BlockSpec(memory_sp...  19.2 us
    all_to_all x3, starting transfers between devices, exchange(): return lax.all_to_all(a, CHIPS, 0, 0)  17.4 us
    all_to_all x3, waiting for transfers between devices, exchange(): return lax.all_to_all(a, CHIPS, 0, 0)  15.8 us
    all_to_all x1, starting transfers between devices, per_device(): got = lax.all_to_all(send, 'dp', 0, 0)  6.82 us
    unnamed x18, local copies, waits for them, and re-layouts  2.58 us
  transfers between devices with their start and end apart: 4, of which 4 were waited for; matrix products, arithmetic and copies ran while one was open for 0% of the time, Pallas kernels for 8%

profile of v3, /device:TPU:1, one launch (start us, length us, event | category | flops | bytes accessed | tf_op | source)
XLA Modules:
  0.0 117.8 jit_solution(9457024897913918172)
XLA Ops:
  0.6 1.9 %shard_map.101 = (f32[128,512]{1,0:T(8,128)}, bf16[128,512]{1,0:T(8,128)(2,1)}, bf16[256,128]{1,0:T(8,128)(2,1)}) custom-call(bf16[128,512]{1,0:T(8,128)(2,1)} %bitcast.22, bf16[128,512]{1,0:T(8,128)(2,1)} %bitcast.23, bf16[512,64]{1,0:T(8,128)(2,1)} %bitcast.24), custom_call_target="tpu_custom_call" | custom-call | flops 100000000 | bytes 786432 | tf_op jit(solution)/shard_map/pallas_call | solution.py:386
  2.6 0.0 copy-start.3
  2.6 0.0 copy-start.4
  2.6 9.0 %all-gather = f32[256,512]{1,0:T(8,128)S(1)} all-gather(f32[128,512]{1,0:T(8,128)} %get-tuple-element.44), channel_id=2, replica_groups=mesh['dp'=8,'z'=8,'x'=4,'core'=2] {'core'}, dimensions={0}, use_global_device_ids=true | all-gather | bytes 786432 | tf_op jit(solution)/shard_map/all_gather | solution.py:410
  11.6 0.0 copy-done.3
  11.6 0.0 copy-done.4
  11.6 1.9 %shard_map.102 = (f32[32,16,128]{2,1,0:T(8,128)}, bf16[256,256]{1,0:T(8,128)(2,1)S(1)}, bf16[256,256]{1,0:T(8,128)(2,1)S(1)}, bf16[256,512]{1,0:T(8,128)(2,1)S(1)}, bf16[256,512]{1,0:T(8,128)(2,1)S(1)}) custom-call(bf16[128,512]{1,0:T(8,128)(2,1)S(1)} %copy-done.3, f32[2,128,512]{2,1,0:T(8,128)S(1)} %bitcast.14, bf16[256,128]{1,0:T(8,128)(2,1)S(1)} %copy-done.4), custom_call_target="tpu_custom_call" | custom-call | flops 100000000 | bytes 1769472 | tf_op jit(solution)/shard_map/pallas_call | solution.py:386
  13.5 0.0 copy-start
  13.5 0.0 copy-start.1
  13.5 0.0 copy-start.2
  13.5 7.6 %all-to-all-start = ((f32[32,16,128]{2,1,0:T(8,128)}), f32[32,16,128]{2,1,0:T(8,128)S(1)}, u32[]{:S(2)}, u32[]{:S(2)}) async-start(f32[32,16,128]{2,1,0:T(8,128)} %get-tuple-element.46), calls=%async_computation | async-start | bytes 524288 | tf_op jit(solution)/shard_map/all_to_all | solution.py:413
  21.2 0.0 copy-done
  21.2 0.0 copy-done.1
  21.2 0.0 copy-done.2
  21.2 0.3 shard_map.103
  21.5 2.5 %all-gather.1 = f32[256,512]{1,0:T(8,128)S(1)} all-gather(f32[128,512]{1,0:T(8,128)S(1)} %get-tuple-element.48), channel_id=3, replica_groups=mesh['dp'=8,'z'=8,'x'=4,'core'=2] {'core'}, dimensions={0}, use_global_device_ids=true | all-gather | bytes 786432 | tf_op jit(solution)/shard_map/all_gather | solution.py:410
  24.0 2.4 %shard_map.104 = (bf16[256,256]{1,0:T(8,128)(2,1)S(1)}, bf16[256,256]{1,0:T(8,128)(2,1)S(1)}, bf16[256,512]{1,0:T(8,128)(2,1)S(1)}, bf16[256,512]{1,0:T(8,128)(2...) custom-call(bf16[128,512]{1,0:T(8,128)(2,1)S(1)} %get-tuple-element.47.own, f32[2,128,512]{2,1,0:T(8,128)S(1)} %bitcast.17, ...), custom_call_target="tpu_custom_call" | custom-call | flops 1000000000 | bytes 2686976 | tf_op jit(solution)/shard_map/pallas_call | solution.py:386
  26.4 6.3 %all-to-all-done.got = f32[32,16,128]{2,1,0:T(8,128)S(1)} async-done(((f32[32,16,128]{2,1,0:T(8,128)}), f32[32,16,128]{2,1,0:T(8,128)S(1)}, u32[]{:S(2)}, u32[]{:S(2)}) %all-to-all-start) | async-done | bytes 262176 | tf_op jit(solution)/shard_map/all_to_all | solution.py:413
  32.7 1.7 %shard_map.105 = (f32[32,16,128]{2,1,0:T(8,128)}, f32[256,256]{1,0:T(8,128)S(1)}, f32[256,256]{1,0:T(8,128)S(1)}, f32[8,128]{1,0:T(8,128)S(1)}) custom-call(f32[32,16,128]{2,1,0:T(8,128)S(1)} %all-to-all-done.got, bf16[256,256]{1,0:T(8,128)(2,1)S(1)} %get-tuple-element.53.g, bf16[256,512]{1,0:T(8,128)(2,1)S(1)} %get-tuple-element.54.qh, ...), custom_call_target="tpu_custom_call" | custom-call | flops 100000000 | bytes 1970176 | tf_op jit(solution)/shard_map/pallas_call | solution.py:386
  34.4 4.6 %all-to-all-start.1 = ((f32[32,16,128]{2,1,0:T(8,128)}), f32[32,16,128]{2,1,0:T(8,128)S(1)}, u32[]{:S(2)}, u32[]{:S(2)}) async-start(f32[32,16,128]{2,1,0:T(8,128)} %get-tuple-element.57), calls=%async_computation.1 | async-start | bytes 524288 | tf_op jit(solution)/shard_map/all_to_all | solution.py:413
  39.0 1.9 %shard_map.106 = (f32[256,512]{1,0:T(8,128)S(1)}, f32[256,256]{1,0:T(8,128)S(1)}, f32[8,128]{1,0:T(8,128)S(1)}) custom-call(bf16[256,256]{1,0:T(8,128)(2,1)S(1)} %get-tuple-element.50.v, bf16[256,512]{1,0:T(8,128)(2,1)S(1)} %get-tuple-element.54.qh, bf16[256,512]{1,0:T(8,128)(2,1)S(1)} %get-tuple-element.55.ql, bf16[256,512]{1,0:T(8,128)(2,1)S(1)} %get-tuple-element.51.kh, ...), custom_call_target="tpu_custom_call" | custom-call | flops 1000000000 | bytes 2232320 | tf_op jit(solution)/shard_map/pallas_call | solution.py:386
  40.9 0.0 copy-start.5
  41.0 0.8 copy-done.5
  41.8 0.0 copy-start.7
  41.8 0.7 copy-done.7
  42.5 7.1 %all-to-all-done.1.got = f32[32,16,128]{2,1,0:T(8,128)S(1)} async-done(((f32[32,16,128]{2,1,0:T(8,128)}), f32[32,16,128]{2,1,0:T(8,128)S(1)}, u32[]{:S(2)}, u32[]{:S(2)}) %all-to-all-start.1) | async-done | bytes 262176 | tf_op jit(solution)/shard_map/all_to_all | solution.py:413
  49.5 1.4 %shard_map.107 = (f32[32,16,128]{2,1,0:T(8,128)}, f32[256,256]{1,0:T(8,128)S(1)}) custom-call(f32[32,16,128]{2,1,0:T(8,128)S(1)} %all-to-all-done.1.got, bf16[256,256]{1,0:T(8,128)(2,1)S(1)} %get-tuple-element.53.g, bf16[256,512]{1,0:T(8,128)(2,1)S(1)} %get-tuple-element.54.qh, bf16[256,512]{1,0:T(8,128)(2,1)S(1)} %get-tuple-element.55.ql, ...), custom_call_target="tpu_custom_call" | custom-call | flops 100000000 | bytes 1970176 | tf_op jit(solution)/shard_map/pallas_call | solution.py:386
  51.0 5.2 %all-to-all-start.2 = ((f32[32,16,128]{2,1,0:T(8,128)}), f32[32,16,128]{2,1,0:T(8,128)S(1)}, u32[]{:S(2)}, u32[]{:S(2)}) async-start(f32[32,16,128]{2,1,0:T(8,128)} %get-tuple-element.68), calls=%async_computation.2 | async-start | bytes 524288 | tf_op jit(solution)/shard_map/all_to_all | solution.py:413
  56.1 0.0 copy-start.6
  56.2 1.0 copy-done.6
  57.2 2.6 %shard_map.108 = (f32[256,256]{1,0:T(8,128)S(1)}, f32[256,128]{1,0:T(8,128)S(1)}, f32[256,512]{1,0:T(8,128)S(1)}) custom-call(f32[32,16,128]{2,1,0:T(8,128)S(1)} %all-to-all-done.1.got, bf16[256,256]{1,0:T(8,128)(2,1)S(1)} %get-tuple-element.58.q, bf16[256,256]{1,0:T(8,128)(2,1)S(1)} %get-tuple-element.50.v, bf16[256,128]{1,0:T(8,128)(2,1)S(1)} %get-tuple-element.49.wq, ...), custom_call_target="tpu_custom_call" | custom-call | flops 1000000000 | bytes 3608576 | tf_op jit(solution)/shard_map/pallas_call | solution.py:386
  59.8 3.7 %all-gather.2 = f32[256,256]{1,0:T(8,128)S(1)} all-gather(f32[128,256]{1,0:T(8,128)S(1)} %shard_map.109), channel_id=4, replica_groups=mesh['dp'=8,'z'=8,'x'=4,'core'=2] {'core'}, dimensions={0}, use_global_device_ids=true | all-gather | bytes 393216 | tf_op jit(solution)/shard_map/all_gather | solution.py:410
  63.5 0.7 shard_map.110
  64.2 2.4 %all-to-all-done.2.got = f32[32,16,128]{2,1,0:T(8,128)S(1)} async-done(((f32[32,16,128]{2,1,0:T(8,128)}), f32[32,16,128]{2,1,0:T(8,128)S(1)}, u32[]{:S(2)}, u32[]{:S(2)}) %all-to-all-start.2) | async-done | bytes 262176 | tf_op jit(solution)/shard_map/all_to_all | solution.py:413
  66.5 0.9 shard_map.111
  67.5 16.3 %all_to_all.30.got = f32[32,8,128]{2,1,0:T(8,128)S(1)} all-to-all(f32[32,8,128]{2,1,0:T(8,128)S(1)} %get-tuple-element.75), channel_id=1, replica_groups=mesh['dp'=8,'z'=8,'x'=4,'core'=2] {'z','x'}, dimensions={0} | all-to-all | bytes 262144 | tf_op jit(solution)/shard_map/all_to_all | solution.py:413
  83.7 0.0 copy-start.8
  83.7 0.6 shard_map.112._
  84.4 6.8 %all-to-all-start.4 = ((f32[8,8,128]{2,1,0:T(8,128)}), f32[8,8,128]{2,1,0:T(8,128)S(1)}, u32[]{:S(2)}, u32[]{:S(2)}) async-start(f32[8,8,128]{2,1,0:T(8,128)} %shard_map.112._), calls=%async_computation.4 | async-start | bytes 65536 | tf_op jit(solution)/shard_map/all_to_all | solution.py:483
  91.2 0.0 copy-done.8
  91.2 1.2 %shard_map.113.whole = f32[256,512]{1,0:T(8,128)S(1)} custom-call(f32[32,16,128]{2,1,0:T(8,128)S(1)} %all-to-all-done.2.got, bf16[256,128]{1,0:T(8,128)(2,1)S(1)} %copy-done.4, bf16[256,512]{1,0:T(8,128)(2,1)S(1)} %get-tuple-element.51.kh, bf16[256,512]{1,0:T(8,128)(2,1)S(1)} %get-tuple-element.52.kl, f32[256,256]{1,0:T(8,128)S(1)} %copy-done.8, ...), custom_call_target="tpu_custom_call" | custom-call | flops 1000000000 | bytes 1933312 | tf_op jit(solution)/shard_map/pallas_call | solution.py:386
  92.5 4.2 %all-gather.3 = f32[256,512]{1,0:T(8,128)S(1)} all-gather(f32[128,512]{1,0:T(8,128)S(1)} %shard_map.114), channel_id=5, replica_groups=mesh['dp'=8,'z'=8,'x'=4,'core'=2] {'core'}, dimensions={0}, use_global_device_ids=true | all-gather | bytes 786432 | tf_op jit(solution)/shard_map/all_gather | solution.py:410
  96.6 0.7 shard_map.115
  97.4 0.7 all-to-all-done.4.got
  98.1 13.1 %all_to_all.31 = f32[32,8,128]{2,1,0:T(8,128)S(1)} all-to-all(f32[32,8,128]{2,1,0:T(8,128)S(1)} %shard_map.116), channel_id=1, replica_groups=mesh['dp'=8,'z'=8,'x'=4,'core'=2] {'z','x'}, dimensions={0} | all-to-all | bytes 262144 | tf_op jit(solution)/shard_map/all_to_all | solution.py:413
  111.2 5.7 %all-gather.4 = f32[64,8,128]{2,1,0:T(8,128)S(1)} all-gather(f32[32,8,128]{2,1,0:T(8,128)S(1)} %all_to_all.31), channel_id=6, replica_groups=mesh['dp'=8,'z'=8,'x'=4,'core'=2] {'core'}, dimensions={0}, use_global_device_ids=true | all-gather | bytes 393216 | tf_op jit(solution)/shard_map/all_gather | solution.py:410
  117.0 0.8 shard_map.117
  (3 shorter events, 0.1 us)
Async XLA Ops:
  2.6 9.1 %copy-start.3 = (bf16[128,512]{1,0:T(8,128)(2,1)S(1)}, bf16[128,512]{1,0:T(8,128)(2,1)}, u32[]{:S(2)}) copy-start(bf16[128,512]{1,0:T(8,128)(2,1)} %get-tuple-element.43.own) | copy-start | bytes 393220
  2.6 9.0 %copy-start.4 = (bf16[256,128]{1,0:T(8,128)(2,1)S(1)}, bf16[256,128]{1,0:T(8,128)(2,1)}, u32[]{:S(2)}) copy-start(bf16[256,128]{1,0:T(8,128)(2,1)} %get-tuple-element.45.wk) | copy-start | bytes 196612
  13.5 7.7 %copy-start = (bf16[1,128,512]{2,1,0:T(8,128)(2,1)S(1)}, bf16[1,128,512]{2,1,0:T(8,128)(2,1)}, u32[]{:S(2)}) copy-start(bf16[1,128,512]{2,1,0:T(8,128)(2,1)} %param.6) | copy-start | bytes 393220
  13.5 7.7 %copy-start.1 = (bf16[1,128,512]{2,1,0:T(8,128)(2,1)S(1)}, bf16[1,128,512]{2,1,0:T(8,128)(2,1)}, u32[]{:S(2)}) copy-start(bf16[1,128,512]{2,1,0:T(8,128)(2,1)} %param.9) | copy-start | bytes 393220
  13.5 7.7 %copy-start.2 = (bf16[8,64,64]{2,1,0:T(8,128)(2,1)S(1)}, bf16[8,64,64]{2,1,0:T(8,128)(2,1)}, u32[]{:S(2)}) copy-start(bf16[8,64,64]{2,1,0:T(8,128)(2,1)} %param.10) | copy-start | bytes 196612
  13.5 19.2 %all-to-all-start = ((f32[32,16,128]{2,1,0:T(8,128)}), f32[32,16,128]{2,1,0:T(8,128)S(1)}, u32[]{:S(2)}, u32[]{:S(2)}) async-start(f32[32,16,128]{2,1,0:T(8,128)} %get-tuple-element.46), calls=%async_computation | async-start | bytes 524288 | tf_op jit(solution)/shard_map/all_to_all | solution.py:413
  34.4 15.1 %all-to-all-start.1 = ((f32[32,16,128]{2,1,0:T(8,128)}), f32[32,16,128]{2,1,0:T(8,128)S(1)}, u32[]{:S(2)}, u32[]{:S(2)}) async-start(f32[32,16,128]{2,1,0:T(8,128)} %get-tuple-element.57), calls=%async_computation.1 | async-start | bytes 524288 | tf_op jit(solution)/shard_map/all_to_all | solution.py:413
  40.9 0.8 copy-start.5
  41.8 0.7 copy-start.7
  51.0 15.6 %all-to-all-start.2 = ((f32[32,16,128]{2,1,0:T(8,128)}), f32[32,16,128]{2,1,0:T(8,128)S(1)}, u32[]{:S(2)}, u32[]{:S(2)}) async-start(f32[32,16,128]{2,1,0:T(8,128)} %get-tuple-element.68), calls=%async_computation.2 | async-start | bytes 524288 | tf_op jit(solution)/shard_map/all_to_all | solution.py:413
  56.1 1.0 copy-start.6
  83.7 7.5 %copy-start.8 = (f32[256,256]{1,0:T(8,128)S(1)}, f32[256,256]{1,0:T(8,128)}, u32[]{:S(2)}) copy-start(f32[256,256]{1,0:T(8,128)} %copy-done.7) | copy-start | bytes 786436
  84.4 13.7 %all-to-all-start.4 = ((f32[8,8,128]{2,1,0:T(8,128)}), f32[8,8,128]{2,1,0:T(8,128)S(1)}, u32[]{:S(2)}, u32[]{:S(2)}) async-start(f32[8,8,128]{2,1,0:T(8,128)} %shard_map.112._), calls=%async_computation.4 | async-start | bytes 65536 | tf_op jit(solution)/shard_map/all_to_all | solution.py:483

commit v4 on v3

--- a/solution.py
+++ b/solution.py
@@ -334,7 +334,7 @@
     send[...] = jnp.concatenate(out, 0).reshape(chips, rows, LANES)
 
 
-def sixth_kernel(got, wk, kh, kl, gvl, dz, _, whole):
+def sixth_kernel(got, wk, kh, kl, gvl, dz, whole):
     rows = WIDE // got.shape[0]
     later = got[:, :rows, :].reshape(WIDE, LANES)
     for p in range(PAIRS):
@@ -370,9 +370,18 @@
     send[...] = jnp.broadcast_to(total[None], send.shape)
 
 
+def sum_cores_kernel(got, send):
+    acc = [got[0], got[1]]
+    for m in range(2, got.shape[0]):
+        acc[m % 2] = acc[m % 2] + got[m]
+    send[...] = jnp.broadcast_to(jnp.concatenate(acc, 0)[None], send.shape)
+
+
 def last_kernel(scale, got, gq, gk):
+    rows = got.shape[1] // 2
+    cores = [got[:, :rows, :].reshape(WIDE, LANES), got[:, rows:, :].reshape(WIDE, LANES)]
     for p in range(2 * PAIRS):
-        x = got[cols(p), :] * scale
+        x = cores[p // PAIRS][cols(p % PAIRS), :] * scale
         y = pltpu.roll(x, HALF, 1)
         gq[2 * p] = x[:HALF, :HALF].astype(BF16)
         gq[2 * p + 1] = y[HALF:, :HALF].astype(BF16)
@@ -472,21 +481,19 @@
         third, k2, v2, kh, kl, gkl, gq_map, token,
     )
     got = exchange(send)
-    (send,) = call(sum_kernel, [((sizes["dp"], rows, LANES), F32)], got)
     (whole,) = call(
-        sixth_kernel,
-        [((BLOCK, 2 * WIDE), F32)],
-        third, wk, kh, kl, gvl, dz, send,
-        flops=10**9,
+        sixth_kernel, [((BLOCK, 2 * WIDE), F32)], third, wk, kh, kl, gvl, dz, flops=10**9
     )
     grad_k, grad_v, token = finish(whole, 2)
-    got = lax.all_to_all(send, "dp", 0, 0)
-    (send,) = call(sum_kernel, [((chips, rows, LANES), F32)], got, token)
-    got = across(exchange(send))
+    others = sizes["dp"] * sizes["core"]
+    (send,) = call(sum_kernel, [((others, rows, LANES), F32)], got, token)
+    got = lax.all_to_all(send, ("dp", "core"), 0, 0)
+    (send,) = call(sum_cores_kernel, [((chips, 2 * rows, LANES), F32)], got)
+    got = exchange(send)
     scale = float(BLOCK * chips * sizes["dp"]) ** (-0.5)
     heads = ((8, HALF, HALF), BF16)
     total_q, total_k = call(
-        functools.partial(last_kernel, scale), [heads, heads], got.reshape(2 * WIDE, LANES)
+        functools.partial(last_kernel, scale), [heads, heads], got
     )
     shape = queries.shape
     return grad_q.reshape(shape), grad_k.reshape(shape), grad_v.reshape(shape), total_q, total_k

time: 118 us -> 118 us (level)
  blocking collectives: 54.5 us -> 49.3 us
  waiting for transfers between devices: 16.5 us -> 21.5 us
    all_to_all x0 -> x1, blocking collectives: none -> 16.8 us  [per_device(): got = lax.all_to_all(send, ('dp', 'core'), 0, 0)]
    all_to_all x2 -> x1, blocking collectives: 29.4 us -> 14.8 us  [exchange(): return lax.all_to_all(a, CHIPS, 0, 0)]
    all_gather x5 -> x4, blocking collectives: 25.1 us -> 17.7 us  [across(): return lax.all_gather(a, 'core')]
    all_to_all x3 -> x4, starting transfers between devices: 17.4 us -> 24.7 us  [exchange(): return lax.all_to_all(a, CHIPS, 0, 0)]
    all_to_all x1 -> x0, starting transfers between devices: 6.82 us -> none  [per_device(): got = lax.all_to_all(send, 'dp', 0, 0)]
    all_to_all x3 -> x4, waiting for transfers between devices: 15.8 us -> 21.5 us  [exchange(): return lax.all_to_all(a, CHIPS, 0, 0)]
where the time goes in v4:
time: 118 us; the launch traced here: 117 us
  blocking collectives  49.3 us (42%)
  starting transfers between devices  24.7 us (21%)
  waiting for transfers between devices  21.5 us (18%)
  Pallas kernels  18.4 us (16%)
  local copies, waits for them, and re-layouts  2.58 us (2%)
    all_to_all x4, starting transfers between devices, exchange(): return lax.all_to_all(a, CHIPS, 0, 0)  24.7 us
    all_to_all x4, waiting for transfers between devices, exchange(): return lax.all_to_all(a, CHIPS, 0, 0)  21.5 us
    pallas_call x17, Pallas kernels, call(): pl.pallas_call(kernel, out_shape=shapes, in_specs=[pl.BlockSpec(memory_sp...  18.4 us
    all_gather x4, blocking collectives, across(): return lax.all_gather(a, 'core')  17.7 us
    all_to_all x1, blocking collectives, per_device(): got = lax.all_to_all(send, ('dp', 'core'), 0, 0)  16.8 us
    all_to_all x1, blocking collectives, exchange(): return lax.all_to_all(a, CHIPS, 0, 0)  14.8 us
    unnamed x18, local copies, waits for them, and re-layouts  2.58 us
  transfers between devices with their start and end apart: 4, of which 4 were waited for; matrix products, arithmetic and copies ran while one was open for 0% of the time, Pallas kernels for 8%

profile of v4, /device:TPU:1, one launch (start us, length us, event | category | flops | bytes accessed | tf_op | source)
XLA Modules:
  0.0 117.2 jit_solution(15131366828870266015)
XLA Ops:
  0.6 1.9 %shard_map.101 = (f32[128,512]{1,0:T(8,128)}, bf16[128,512]{1,0:T(8,128)(2,1)}, bf16[256,128]{1,0:T(8,128)(2,1)}) custom-call(bf16[128,512]{1,0:T(8,128)(2,1)} %bitcast.20, bf16[128,512]{1,0:T(8,128)(2,1)} %bitcast.21, bf16[512,64]{1,0:T(8,128)(2,1)} %bitcast.22), custom_call_target="tpu_custom_call" | custom-call | flops 100000000 | bytes 786432 | tf_op jit(solution)/shard_map/pallas_call | solution.py:395
  2.6 0.0 copy-start.3
  2.6 0.0 copy-start.4
  2.6 9.0 %all-gather = f32[256,512]{1,0:T(8,128)S(1)} all-gather(f32[128,512]{1,0:T(8,128)} %get-tuple-element.44), channel_id=2, replica_groups=mesh['dp'=8,'z'=8,'x'=4,'core'=2] {'core'}, dimensions={0}, use_global_device_ids=true | all-gather | bytes 786432 | tf_op jit(solution)/shard_map/all_gather | solution.py:419
  11.6 0.0 copy-done.3
  11.6 0.0 copy-done.4
  11.6 1.9 %shard_map.102 = (f32[32,16,128]{2,1,0:T(8,128)}, bf16[256,256]{1,0:T(8,128)(2,1)S(1)}, bf16[256,256]{1,0:T(8,128)(2,1)S(1)}, bf16[256,512]{1,0:T(8,128)(2,1)S(1)}, bf16[256,512]{1,0:T(8,128)(2,1)S(1)}) custom-call(bf16[128,512]{1,0:T(8,128)(2,1)S(1)} %copy-done.3, f32[2,128,512]{2,1,0:T(8,128)S(1)} %bitcast.13, bf16[256,128]{1,0:T(8,128)(2,1)S(1)} %copy-done.4), custom_call_target="tpu_custom_call" | custom-call | flops 100000000 | bytes 1769472 | tf_op jit(solution)/shard_map/pallas_call | solution.py:395
  13.5 0.0 copy-start
  13.5 0.0 copy-start.1
  13.5 0.0 copy-start.2
  13.5 7.6 %all-to-all-start = ((f32[32,16,128]{2,1,0:T(8,128)}), f32[32,16,128]{2,1,0:T(8,128)S(1)}, u32[]{:S(2)}, u32[]{:S(2)}) async-start(f32[32,16,128]{2,1,0:T(8,128)} %get-tuple-element.46), calls=%async_computation | async-start | bytes 524288 | tf_op jit(solution)/shard_map/all_to_all | solution.py:422
  21.2 0.0 copy-done
  21.2 0.0 copy-done.1
  21.2 0.0 copy-done.2
  21.2 0.3 shard_map.103
  21.5 2.5 %all-gather.1 = f32[256,512]{1,0:T(8,128)S(1)} all-gather(f32[128,512]{1,0:T(8,128)S(1)} %get-tuple-element.48), channel_id=3, replica_groups=mesh['dp'=8,'z'=8,'x'=4,'core'=2] {'core'}, dimensions={0}, use_global_device_ids=true | all-gather | bytes 786432 | tf_op jit(solution)/shard_map/all_gather | solution.py:419
  24.0 2.4 %shard_map.104 = (bf16[256,256]{1,0:T(8,128)(2,1)S(1)}, bf16[256,256]{1,0:T(8,128)(2,1)S(1)}, bf16[256,512]{1,0:T(8,128)(2,1)S(1)}, bf16[256,512]{1,0:T(8,128)(2...) custom-call(bf16[128,512]{1,0:T(8,128)(2,1)S(1)} %get-tuple-element.47.own, f32[2,128,512]{2,1,0:T(8,128)S(1)} %bitcast.16, ...), custom_call_target="tpu_custom_call" | custom-call | flops 1000000000 | bytes 2686976 | tf_op jit(solution)/shard_map/pallas_call | solution.py:395
  26.4 6.3 %all-to-all-done.got = f32[32,16,128]{2,1,0:T(8,128)S(1)} async-done(((f32[32,16,128]{2,1,0:T(8,128)}), f32[32,16,128]{2,1,0:T(8,128)S(1)}, u32[]{:S(2)}, u32[]{:S(2)}) %all-to-all-start) | async-done | bytes 262176 | tf_op jit(solution)/shard_map/all_to_all | solution.py:422
  32.7 1.7 %shard_map.105 = (f32[32,16,128]{2,1,0:T(8,128)}, f32[256,256]{1,0:T(8,128)S(1)}, f32[256,256]{1,0:T(8,128)S(1)}, f32[8,128]{1,0:T(8,128)S(1)}) custom-call(f32[32,16,128]{2,1,0:T(8,128)S(1)} %all-to-all-done.got, bf16[256,256]{1,0:T(8,128)(2,1)S(1)} %get-tuple-element.53.g, bf16[256,512]{1,0:T(8,128)(2,1)S(1)} %get-tuple-element.54.qh, ...), custom_call_target="tpu_custom_call" | custom-call | flops 100000000 | bytes 1970176 | tf_op jit(solution)/shard_map/pallas_call | solution.py:395
  34.4 4.6 %all-to-all-start.1 = ((f32[32,16,128]{2,1,0:T(8,128)}), f32[32,16,128]{2,1,0:T(8,128)S(1)}, u32[]{:S(2)}, u32[]{:S(2)}) async-start(f32[32,16,128]{2,1,0:T(8,128)} %get-tuple-element.57), calls=%async_computation.1 | async-start | bytes 524288 | tf_op jit(solution)/shard_map/all_to_all | solution.py:422
  39.0 1.9 %shard_map.106 = (f32[256,512]{1,0:T(8,128)S(1)}, f32[256,256]{1,0:T(8,128)S(1)}, f32[8,128]{1,0:T(8,128)S(1)}) custom-call(bf16[256,256]{1,0:T(8,128)(2,1)S(1)} %get-tuple-element.50.v, bf16[256,512]{1,0:T(8,128)(2,1)S(1)} %get-tuple-element.54.qh, bf16[256,512]{1,0:T(8,128)(2,1)S(1)} %get-tuple-element.55.ql, bf16[256,512]{1,0:T(8,128)(2,1)S(1)} %get-tuple-element.51.kh, ...), custom_call_target="tpu_custom_call" | custom-call | flops 1000000000 | bytes 2232320 | tf_op jit(solution)/shard_map/pallas_call | solution.py:395
  40.9 0.0 copy-start.5
  41.0 0.8 copy-done.5
  41.8 0.0 copy-start.7
  41.8 0.7 copy-done.7
  42.5 7.1 %all-to-all-done.1.got = f32[32,16,128]{2,1,0:T(8,128)S(1)} async-done(((f32[32,16,128]{2,1,0:T(8,128)}), f32[32,16,128]{2,1,0:T(8,128)S(1)}, u32[]{:S(2)}, u32[]{:S(2)}) %all-to-all-start.1) | async-done | bytes 262176 | tf_op jit(solution)/shard_map/all_to_all | solution.py:422
  49.5 1.4 %shard_map.107 = (f32[32,16,128]{2,1,0:T(8,128)}, f32[256,256]{1,0:T(8,128)S(1)}) custom-call(f32[32,16,128]{2,1,0:T(8,128)S(1)} %all-to-all-done.1.got, bf16[256,256]{1,0:T(8,128)(2,1)S(1)} %get-tuple-element.53.g, bf16[256,512]{1,0:T(8,128)(2,1)S(1)} %get-tuple-element.54.qh, bf16[256,512]{1,0:T(8,128)(2,1)S(1)} %get-tuple-element.55.ql, ...), custom_call_target="tpu_custom_call" | custom-call | flops 100000000 | bytes 1970176 | tf_op jit(solution)/shard_map/pallas_call | solution.py:395
  51.0 5.2 %all-to-all-start.2 = ((f32[32,16,128]{2,1,0:T(8,128)}), f32[32,16,128]{2,1,0:T(8,128)S(1)}, u32[]{:S(2)}, u32[]{:S(2)}) async-start(f32[32,16,128]{2,1,0:T(8,128)} %get-tuple-element.68), calls=%async_computation.2 | async-start | bytes 524288 | tf_op jit(solution)/shard_map/all_to_all | solution.py:422
  56.1 0.0 copy-start.6
  56.2 1.0 copy-done.6
  57.2 2.6 %shard_map.108 = (f32[256,256]{1,0:T(8,128)S(1)}, f32[256,128]{1,0:T(8,128)S(1)}, f32[256,512]{1,0:T(8,128)S(1)}) custom-call(f32[32,16,128]{2,1,0:T(8,128)S(1)} %all-to-all-done.1.got, bf16[256,256]{1,0:T(8,128)(2,1)S(1)} %get-tuple-element.58.q, bf16[256,256]{1,0:T(8,128)(2,1)S(1)} %get-tuple-element.50.v, bf16[256,128]{1,0:T(8,128)(2,1)S(1)} %get-tuple-element.49.wq, ...), custom_call_target="tpu_custom_call" | custom-call | flops 1000000000 | bytes 3608576 | tf_op jit(solution)/shard_map/pallas_call | solution.py:395
  59.8 3.7 %all-gather.2 = f32[256,256]{1,0:T(8,128)S(1)} all-gather(f32[128,256]{1,0:T(8,128)S(1)} %shard_map.109), channel_id=4, replica_groups=mesh['dp'=8,'z'=8,'x'=4,'core'=2] {'core'}, dimensions={0}, use_global_device_ids=true | all-gather | bytes 393216 | tf_op jit(solution)/shard_map/all_gather | solution.py:419
  63.5 0.7 shard_map.110
  64.2 2.4 %all-to-all-done.2.got = f32[32,16,128]{2,1,0:T(8,128)S(1)} async-done(((f32[32,16,128]{2,1,0:T(8,128)}), f32[32,16,128]{2,1,0:T(8,128)S(1)}, u32[]{:S(2)}, u32[]{:S(2)}) %all-to-all-start.2) | async-done | bytes 262176 | tf_op jit(solution)/shard_map/all_to_all | solution.py:422
  66.5 1.6 %shard_map.111 = (f32[32,8,128]{2,1,0:T(8,128)}, f32[256,256]{1,0:T(8,128)S(1)}) custom-call(f32[32,16,128]{2,1,0:T(8,128)S(1)} %all-to-all-done.2.got, bf16[256,256]{1,0:T(8,128)(2,1)S(1)} %get-tuple-element.70.k, bf16[256,256]{1,0:T(8,128)(2,1)S(1)} %get-tuple-element.50.v, bf16[256,512]{1,0:T(8,128)(2,1)S(1)} %get-tuple-element.51.kh, ...), custom_call_target="tpu_custom_call" | custom-call | flops 100000000 | bytes 2101248 | tf_op jit(solution)/shard_map/pallas_call | solution.py:395
  68.1 0.0 copy-start.8
  68.1 7.3 %all-to-all-start.3 = ((f32[32,8,128]{2,1,0:T(8,128)}), f32[32,8,128]{2,1,0:T(8,128)S(1)}, u32[]{:S(2)}, u32[]{:S(2)}) async-start(f32[32,8,128]{2,1,0:T(8,128)} %get-tuple-element.77), calls=%async_computation.3 | async-start | bytes 262144 | tf_op jit(solution)/shard_map/all_to_all | solution.py:422
  75.4 0.0 copy-done.8
  75.4 0.4 shard_map.112.whole
  75.9 2.5 %all-gather.3 = f32[256,512]{1,0:T(8,128)S(1)} all-gather(f32[128,512]{1,0:T(8,128)S(1)} %shard_map.113), channel_id=5, replica_groups=mesh['dp'=8,'z'=8,'x'=4,'core'=2] {'core'}, dimensions={0}, use_global_device_ids=true | all-gather | bytes 786432 | tf_op jit(solution)/shard_map/all_gather | solution.py:419
  78.3 0.7 shard_map.114
  79.0 5.7 %all-to-all-done.3.got = f32[32,8,128]{2,1,0:T(8,128)S(1)} async-done(((f32[32,8,128]{2,1,0:T(8,128)}), f32[32,8,128]{2,1,0:T(8,128)S(1)}, u32[]{:S(2)}, u32[]{:S(2)}) %all-to-all-start.3) | async-done | bytes 131104 | tf_op jit(solution)/shard_map/all_to_all | solution.py:422
  84.8 16.8 %all_to_all.30.got = f32[16,8,128]{2,1,0:T(8,128)S(1)} all-to-all(f32[16,8,128]{2,1,0:T(8,128)S(1)} %shard_map.115), channel_id=1, replica_groups=mesh['dp'=8,'z'=8,'x'=4,'core'=2] {'dp','core'}, dimensions={0} | all-to-all | bytes 131072 | tf_op jit(solution)/shard_map/all_to_all | solution.py:490
  101.6 14.8 %all_to_all.31.got = f32[32,16,128]{2,1,0:T(8,128)S(1)} all-to-all(f32[32,16,128]{2,1,0:T(8,128)S(1)} %shard_map.116), channel_id=1, replica_groups=mesh['dp'=8,'z'=8,'x'=4,'core'=2] {'z','x'}, dimensions={0} | all-to-all | bytes 524288 | tf_op jit(solution)/shard_map/all_to_all | solution.py:422
  116.4 0.8 shard_map.117
  (4 shorter events, 0.1 us)
Async XLA Ops:
  2.6 9.1 %copy-start.3 = (bf16[128,512]{1,0:T(8,128)(2,1)S(1)}, bf16[128,512]{1,0:T(8,128)(2,1)}, u32[]{:S(2)}) copy-start(bf16[128,512]{1,0:T(8,128)(2,1)} %get-tuple-element.43.own) | copy-start | bytes 393220
  2.6 9.0 %copy-start.4 = (bf16[256,128]{1,0:T(8,128)(2,1)S(1)}, bf16[256,128]{1,0:T(8,128)(2,1)}, u32[]{:S(2)}) copy-start(bf16[256,128]{1,0:T(8,128)(2,1)} %get-tuple-element.45.wk) | copy-start | bytes 196612
  13.5 7.7 %copy-start = (bf16[1,128,512]{2,1,0:T(8,128)(2,1)S(1)}, bf16[1,128,512]{2,1,0:T(8,128)(2,1)}, u32[]{:S(2)}) copy-start(bf16[1,128,512]{2,1,0:T(8,128)(2,1)} %param.6) | copy-start | bytes 393220
  13.5 7.7 %copy-start.1 = (bf16[1,128,512]{2,1,0:T(8,128)(2,1)S(1)}, bf16[1,128,512]{2,1,0:T(8,128)(2,1)}, u32[]{:S(2)}) copy-start(bf16[1,128,512]{2,1,0:T(8,128)(2,1)} %param.9) | copy-start | bytes 393220
  13.5 7.7 %copy-start.2 = (bf16[8,64,64]{2,1,0:T(8,128)(2,1)S(1)}, bf16[8,64,64]{2,1,0:T(8,128)(2,1)}, u32[]{:S(2)}) copy-start(bf16[8,64,64]{2,1,0:T(8,128)(2,1)} %param.10) | copy-start | bytes 196612
  13.5 19.2 %all-to-all-start = ((f32[32,16,128]{2,1,0:T(8,128)}), f32[32,16,128]{2,1,0:T(8,128)S(1)}, u32[]{:S(2)}, u32[]{:S(2)}) async-start(f32[32,16,128]{2,1,0:T(8,128)} %get-tuple-element.46), calls=%async_computation | async-start | bytes 524288 | tf_op jit(solution)/shard_map/all_to_all | solution.py:422
  34.4 15.1 %all-to-all-start.1 = ((f32[32,16,128]{2,1,0:T(8,128)}), f32[32,16,128]{2,1,0:T(8,128)S(1)}, u32[]{:S(2)}, u32[]{:S(2)}) async-start(f32[32,16,128]{2,1,0:T(8,128)} %get-tuple-element.57), calls=%async_computation.1 | async-start | bytes 524288 | tf_op jit(solution)/shard_map/all_to_all | solution.py:422
  40.9 0.8 copy-start.5
  41.8 0.7 copy-start.7
  51.0 15.6 %all-to-all-start.2 = ((f32[32,16,128]{2,1,0:T(8,128)}), f32[32,16,128]{2,1,0:T(8,128)S(1)}, u32[]{:S(2)}, u32[]{:S(2)}) async-start(f32[32,16,128]{2,1,0:T(8,128)} %get-tuple-element.68), calls=%async_computation.2 | async-start | bytes 524288 | tf_op jit(solution)/shard_map/all_to_all | solution.py:422
  56.1 1.0 copy-start.6
  68.1 7.3 %copy-start.8 = (f32[256,256]{1,0:T(8,128)S(1)}, f32[256,256]{1,0:T(8,128)}, u32[]{:S(2)}) copy-start(f32[256,256]{1,0:T(8,128)} %copy-done.7) | copy-start | bytes 786436
  68.1 16.6 %all-to-all-start.3 = ((f32[32,8,128]{2,1,0:T(8,128)}), f32[32,8,128]{2,1,0:T(8,128)S(1)}, u32[]{:S(2)}, u32[]{:S(2)}) async-start(f32[32,8,128]{2,1,0:T(8,128)} %get-tuple-element.77), calls=%async_computation.3 | async-start | bytes 262144 | tf_op jit(solution)/shard_map/all_to_all | solution.py:422

commit v5 on v4

--- a/solution.py
+++ b/solution.py
@@ -307,7 +307,7 @@
         gk_all[:, w] = gk + (nn(tri_back, later[0]) + nn(tri_back, later[1]))
 
 
-def fifth_kernel(sizes, got, k, v, kh, kl, gkl, gq_map, _, send, dz):
+def fifth_kernel(sizes, got, k, v, kh, kl, gkl, gq_map, send, dz):
     chips = send.shape[0]
     rows = WIDE // chips
     me = chip(sizes)
@@ -345,21 +345,24 @@
         whole[:, WIDE + p * LANES : WIDE + (p + 1) * LANES] = grad
 
 
-def theirs_kernel(whole, send):
-    send[...] = whole[pl.ds(pl.multiple_of((1 - core()) * TOK, TOK), TOK), :]
-
-
-def finish_kernel(whole, got, *outs):
+def theirs_kernel(first, second, send):
+    rows = pl.ds(pl.multiple_of((1 - core()) * TOK, TOK), TOK)
+    send[:, :WIDE] = first[rows, :]
+    send[:, WIDE:] = second[rows, :]
+
+
+def finish_kernel(first, second, got, *outs):
     *outs, token = outs
     token[...] = jnp.zeros_like(token)
-    own = whole[pl.ds(pl.multiple_of(core() * TOK, TOK), TOK), :]
+    rows = pl.ds(pl.multiple_of(core() * TOK, TOK), TOK)
+    own = jnp.concatenate([first[rows, :], second[rows, :]], 1)
     other = got[1 - core()]
-    first = core() == 0
+    zero = core() == 0
     for i, out in enumerate(outs):
         lanes = slice(i * WIDE, (i + 1) * WIDE)
         a, b = own[:, lanes], other[:, lanes]
-        out[:, :WIDE] = jnp.where(first, a, b).astype(BF16)
-        out[:, WIDE:] = jnp.where(first, b, a).astype(BF16)
+        out[:, :WIDE] = jnp.where(zero, a, b).astype(BF16)
+        out[:, WIDE:] = jnp.where(zero, b, a).astype(BF16)
 
 
 def sum_kernel(got, *rest):
@@ -436,11 +439,6 @@
         )
         return own, across(send), wide
 
-    def finish(whole, count):
-        (send,) = call(theirs_kernel, [((TOK, count * WIDE), F32)], whole)
-        out = [((TOK, 2 * WIDE), BF16)] * count + [sums]
-        return call(finish_kernel, out, whole, across(send))
-
     own, got, wk = start(k, v, kmap, 60)
     send, k2, v2, kh, kl = call(
         keys_kernel, [((chips, rows + 8, LANES), F32), small, small, feats, feats], own, got, wk
@@ -468,23 +466,26 @@
         second, g2, qh, ql, numl, den, token,
     )
     third = exchange(send)
-    whole, gq_map, gkl = call(
+    whole_q, gq_map, gkl = call(
         fourth_kernel,
         [flat, ((WIDE, LANES), F32), feats32],
         second, q2, v2, wq, qh, ql, kh, kl, dn, dd, ksum, gql,
         flops=10**9,
     )
-    grad_q, token = finish(whole, 1)
     send, dz = call(
         functools.partial(fifth_kernel, sizes),
         [((chips, rows, LANES), F32), flat],
-        third, k2, v2, kh, kl, gkl, gq_map, token,
+        third, k2, v2, kh, kl, gkl, gq_map,
     )
     got = exchange(send)
     (whole,) = call(
         sixth_kernel, [((BLOCK, 2 * WIDE), F32)], third, wk, kh, kl, gvl, dz, flops=10**9
     )
-    grad_k, grad_v, token = finish(whole, 2)
+    (send,) = call(theirs_kernel, [((TOK, 3 * WIDE), F32)], whole_q, whole)
+    outs = [((TOK, 2 * WIDE), BF16)] * 3
+    grad_q, grad_k, grad_v, token = call(
+        finish_kernel, outs + [sums], whole_q, whole, across(send)
+    )
     others = sizes["dp"] * sizes["core"]
     (send,) = call(sum_kernel, [((others, rows, LANES), F32)], got, token)
     got = lax.all_to_all(send, ("dp", "core"), 0, 0)

time: 118 us -> 117 us (level)
  starting transfers between devices: 24.7 us -> 21.5 us
  blocking collectives: 49.3 us -> 51.6 us
    all_to_all x4, starting transfers between devices: 24.7 us -> 21.5 us  [exchange(): return lax.all_to_all(a, CHIPS, 0, 0)]
    all_to_all x1, blocking collectives: 16.8 us -> 19.6 us  [per_device(): got = lax.all_to_all(send, ('dp', 'core'), 0, 0)]
    all_to_all x4, waiting for transfers between devices: 21.5 us -> 22.6 us  [exchange(): return lax.all_to_all(a, CHIPS, 0, 0)]
    pallas_call x17 -> x15, Pallas kernels: 18.4 us -> 17.7 us  [call(): pl.pallas_call(kernel, out_shape=shapes, in_specs=[pl.BlockSpec(memory_sp...]
    all_gather x4 -> x3, blocking collectives: 17.7 us -> 17.2 us  [across(): return lax.all_gather(a, 'core')]
  transfers between devices with their start and end apart: 4 -> 4, of which waited for: 4 -> 4; matrix products, arithmetic and copies ran while one was open for 0% -> 0% of each run, Pallas kernels for 8% -> 7%
where the time goes in v5:
time: 117 us
  blocking collectives  51.6 us (44%)
  waiting for transfers between devices  22.6 us (19%)
  starting transfers between devices  21.5 us (18%)
  Pallas kernels  17.7 us (15%)
  local copies, waits for them, and re-layouts  2.57 us (2%)
    all_to_all x4, waiting for transfers between devices, exchange(): return lax.all_to_all(a, CHIPS, 0, 0)  22.6 us
    all_to_all x4, starting transfers between devices, exchange(): return lax.all_to_all(a, CHIPS, 0, 0)  21.5 us
    all_to_all x1, blocking collectives, per_device(): got = lax.all_to_all(send, ('dp', 'core'), 0, 0)  19.6 us
    pallas_call x15, Pallas kernels, call(): pl.pallas_call(kernel, out_shape=shapes, in_specs=[pl.BlockSpec(memory_sp...  17.7 us
    all_gather x3, blocking collectives, across(): return lax.all_gather(a, 'core')  17.2 us
    all_to_all x1, blocking collectives, exchange(): return lax.all_to_all(a, CHIPS, 0, 0)  14.8 us
    unnamed x18, local copies, waits for them, and re-layouts  2.57 us
  transfers between devices with their start and end apart: 4, of which 4 were waited for; matrix products, arithmetic and copies ran while one was open for 0% of the time, Pallas kernels for 7%

profile of v5, /device:TPU:1, one launch (start us, length us, event | category | flops | bytes accessed | tf_op | source)
XLA Modules:
  0.0 116.8 jit_solution(18213906164185498882)
XLA Ops:
  0.6 1.9 %shard_map.101 = (f32[128,512]{1,0:T(8,128)}, bf16[128,512]{1,0:T(8,128)(2,1)}, bf16[256,128]{1,0:T(8,128)(2,1)}) custom-call(bf16[128,512]{1,0:T(8,128)(2,1)} %bitcast.18, bf16[128,512]{1,0:T(8,128)(2,1)} %bitcast.19, bf16[512,64]{1,0:T(8,128)(2,1)} %bitcast.20), custom_call_target="tpu_custom_call" | custom-call | flops 100000000 | bytes 786432 | tf_op jit(solution)/shard_map/pallas_call | solution.py:398
  2.6 0.0 copy-start.3
  2.6 0.0 copy-start.4
  2.6 9.0 %all-gather = f32[256,512]{1,0:T(8,128)S(1)} all-gather(f32[128,512]{1,0:T(8,128)} %get-tuple-element.43), channel_id=2, replica_groups=mesh['dp'=8,'z'=8,'x'=4,'core'=2] {'core'}, dimensions={0}, use_global_device_ids=true | all-gather | bytes 786432 | tf_op jit(solution)/shard_map/all_gather | solution.py:422
  11.6 0.0 copy-done.3
  11.6 0.0 copy-done.4
  11.6 1.8 %shard_map.102 = (f32[32,16,128]{2,1,0:T(8,128)}, bf16[256,256]{1,0:T(8,128)(2,1)S(1)}, bf16[256,256]{1,0:T(8,128)(2,1)S(1)}, bf16[256,512]{1,0:T(8,128)(2,1)S(1)}, bf16[256,512]{1,0:T(8,128)(2,1)S(1)}) custom-call(bf16[128,512]{1,0:T(8,128)(2,1)S(1)} %copy-done.3, f32[2,128,512]{2,1,0:T(8,128)S(1)} %bitcast.13, bf16[256,128]{1,0:T(8,128)(2,1)S(1)} %copy-done.4), custom_call_target="tpu_custom_call" | custom-call | flops 100000000 | bytes 1769472 | tf_op jit(solution)/shard_map/pallas_call | solution.py:398
  13.5 0.0 copy-start
  13.5 0.0 copy-start.1
  13.5 0.0 copy-start.2
  13.5 7.6 %all-to-all-start = ((f32[32,16,128]{2,1,0:T(8,128)}), f32[32,16,128]{2,1,0:T(8,128)S(1)}, u32[]{:S(2)}, u32[]{:S(2)}) async-start(f32[32,16,128]{2,1,0:T(8,128)} %get-tuple-element.45), calls=%async_computation | async-start | bytes 524288 | tf_op jit(solution)/shard_map/all_to_all | solution.py:425
  21.1 0.0 copy-done
  21.1 0.0 copy-done.1
  21.1 0.0 copy-done.2
  21.2 0.3 shard_map.103
  21.5 2.5 %all-gather.1 = f32[256,512]{1,0:T(8,128)S(1)} all-gather(f32[128,512]{1,0:T(8,128)S(1)} %get-tuple-element.47), channel_id=3, replica_groups=mesh['dp'=8,'z'=8,'x'=4,'core'=2] {'core'}, dimensions={0}, use_global_device_ids=true | all-gather | bytes 786432 | tf_op jit(solution)/shard_map/all_gather | solution.py:422
  24.0 2.4 %shard_map.104 = (bf16[256,256]{1,0:T(8,128)(2,1)S(1)}, bf16[256,256]{1,0:T(8,128)(2,1)S(1)}, bf16[256,512]{1,0:T(8,128)(2,1)S(1)}, bf16[256,512]{1,0:T(8,128)(2...) custom-call(bf16[128,512]{1,0:T(8,128)(2,1)S(1)} %get-tuple-element.46.own, f32[2,128,512]{2,1,0:T(8,128)S(1)} %bitcast.14, ...), custom_call_target="tpu_custom_call" | custom-call | flops 1000000000 | bytes 2686976 | tf_op jit(solution)/shard_map/pallas_call | solution.py:398
  26.4 6.3 %all-to-all-done.got = f32[32,16,128]{2,1,0:T(8,128)S(1)} async-done(((f32[32,16,128]{2,1,0:T(8,128)}), f32[32,16,128]{2,1,0:T(8,128)S(1)}, u32[]{:S(2)}, u32[]{:S(2)}) %all-to-all-start) | async-done | bytes 262176 | tf_op jit(solution)/shard_map/all_to_all | solution.py:425
  32.7 1.7 %shard_map.105 = (f32[32,16,128]{2,1,0:T(8,128)}, f32[256,256]{1,0:T(8,128)S(1)}, f32[256,256]{1,0:T(8,128)S(1)}, f32[8,128]{1,0:T(8,128)S(1)}) custom-call(f32[32,16,128]{2,1,0:T(8,128)S(1)} %all-to-all-done.got, bf16[256,256]{1,0:T(8,128)(2,1)S(1)} %get-tuple-element.52.g, bf16[256,512]{1,0:T(8,128)(2,1)S(1)} %get-tuple-element.53.qh, ...), custom_call_target="tpu_custom_call" | custom-call | flops 100000000 | bytes 1970176 | tf_op jit(solution)/shard_map/pallas_call | solution.py:398
  34.4 4.6 %all-to-all-start.1 = ((f32[32,16,128]{2,1,0:T(8,128)}), f32[32,16,128]{2,1,0:T(8,128)S(1)}, u32[]{:S(2)}, u32[]{:S(2)}) async-start(f32[32,16,128]{2,1,0:T(8,128)} %get-tuple-element.56), calls=%async_computation.1 | async-start | bytes 524288 | tf_op jit(solution)/shard_map/all_to_all | solution.py:425
  39.0 1.9 %shard_map.106 = (f32[256,512]{1,0:T(8,128)S(1)}, f32[256,256]{1,0:T(8,128)S(1)}, f32[8,128]{1,0:T(8,128)S(1)}) custom-call(bf16[256,256]{1,0:T(8,128)(2,1)S(1)} %get-tuple-element.49.v, bf16[256,512]{1,0:T(8,128)(2,1)S(1)} %get-tuple-element.53.qh, bf16[256,512]{1,0:T(8,128)(2,1)S(1)} %get-tuple-element.54.ql, bf16[256,512]{1,0:T(8,128)(2,1)S(1)} %get-tuple-element.50.kh, ...), custom_call_target="tpu_custom_call" | custom-call | flops 1000000000 | bytes 2232320 | tf_op jit(solution)/shard_map/pallas_call | solution.py:398
  40.9 0.0 copy-start.5
  40.9 0.8 copy-done.5
  41.7 0.0 copy-start.7
  41.7 0.7 copy-done.7
  42.4 7.1 %all-to-all-done.1.got = f32[32,16,128]{2,1,0:T(8,128)S(1)} async-done(((f32[32,16,128]{2,1,0:T(8,128)}), f32[32,16,128]{2,1,0:T(8,128)S(1)}, u32[]{:S(2)}, u32[]{:S(2)}) %all-to-all-start.1) | async-done | bytes 262176 | tf_op jit(solution)/shard_map/all_to_all | solution.py:425
  49.5 1.4 %shard_map.107 = (f32[32,16,128]{2,1,0:T(8,128)}, f32[256,256]{1,0:T(8,128)S(1)}) custom-call(f32[32,16,128]{2,1,0:T(8,128)S(1)} %all-to-all-done.1.got, bf16[256,256]{1,0:T(8,128)(2,1)S(1)} %get-tuple-element.52.g, bf16[256,512]{1,0:T(8,128)(2,1)S(1)} %get-tuple-element.53.qh, bf16[256,512]{1,0:T(8,128)(2,1)S(1)} %get-tuple-element.54.ql, ...), custom_call_target="tpu_custom_call" | custom-call | flops 100000000 | bytes 1970176 | tf_op jit(solution)/shard_map/pallas_call | solution.py:398
  50.9 5.2 %all-to-all-start.2 = ((f32[32,16,128]{2,1,0:T(8,128)}), f32[32,16,128]{2,1,0:T(8,128)S(1)}, u32[]{:S(2)}, u32[]{:S(2)}) async-start(f32[32,16,128]{2,1,0:T(8,128)} %get-tuple-element.66), calls=%async_computation.2 | async-start | bytes 524288 | tf_op jit(solution)/shard_map/all_to_all | solution.py:425
  56.1 0.0 copy-start.6
  56.1 1.0 copy-done.6
  57.1 2.6 %shard_map.108 = (f32[256,256]{1,0:T(8,128)S(1)}, f32[256,128]{1,0:T(8,128)S(1)}, f32[256,512]{1,0:T(8,128)S(1)}) custom-call(f32[32,16,128]{2,1,0:T(8,128)S(1)} %all-to-all-done.1.got, bf16[256,256]{1,0:T(8,128)(2,1)S(1)} %get-tuple-element.57.q, bf16[256,256]{1,0:T(8,128)(2,1)S(1)} %get-tuple-element.49.v, bf16[256,128]{1,0:T(8,128)(2,1)S(1)} %get-tuple-element.48.wq, ...), custom_call_target="tpu_custom_call" | custom-call | flops 1000000000 | bytes 3608576 | tf_op jit(solution)/shard_map/pallas_call | solution.py:398
  59.7 6.8 %all-to-all-done.2.got = f32[32,16,128]{2,1,0:T(8,128)S(1)} async-done(((f32[32,16,128]{2,1,0:T(8,128)}), f32[32,16,128]{2,1,0:T(8,128)S(1)}, u32[]{:S(2)}, u32[]{:S(2)}) %all-to-all-start.2) | async-done | bytes 262176 | tf_op jit(solution)/shard_map/all_to_all | solution.py:425
  66.5 1.6 %shard_map.109 = (f32[32,8,128]{2,1,0:T(8,128)}, f32[256,256]{1,0:T(8,128)S(1)}) custom-call(f32[32,16,128]{2,1,0:T(8,128)S(1)} %all-to-all-done.2.got, bf16[256,256]{1,0:T(8,128)(2,1)S(1)} %get-tuple-element.68.k, bf16[256,256]{1,0:T(8,128)(2,1)S(1)} %get-tuple-element.49.v, bf16[256,512]{1,0:T(8,128)(2,1)S(1)} %get-tuple-element.50.kh, ...), custom_call_target="tpu_custom_call" | custom-call | flops 100000000 | bytes 2097152 | tf_op jit(solution)/shard_map/pallas_call | solution.py:398
  68.0 0.0 copy-start.8
  68.0 4.1 %all-to-all-start.3 = ((f32[32,8,128]{2,1,0:T(8,128)}), f32[32,8,128]{2,1,0:T(8,128)S(1)}, u32[]{:S(2)}, u32[]{:S(2)}) async-start(f32[32,8,128]{2,1,0:T(8,128)} %get-tuple-element.75), calls=%async_computation.3 | async-start | bytes 262144 | tf_op jit(solution)/shard_map/all_to_all | solution.py:425
  72.1 0.0 copy-done.8
  72.1 0.4 shard_map.110.second
  72.6 5.7 %all-gather.2 = f32[256,768]{1,0:T(8,128)S(1)} all-gather(f32[128,768]{1,0:T(8,128)S(1)} %shard_map.111), channel_id=4, replica_groups=mesh['dp'=8,'z'=8,'x'=4,'core'=2] {'core'}, dimensions={0}, use_global_device_ids=true | all-gather | bytes 1179648 | tf_op jit(solution)/shard_map/all_gather | solution.py:422
  78.3 0.8 shard_map.112
  79.1 2.4 %all-to-all-done.3.got = f32[32,8,128]{2,1,0:T(8,128)S(1)} async-done(((f32[32,8,128]{2,1,0:T(8,128)}), f32[32,8,128]{2,1,0:T(8,128)S(1)}, u32[]{:S(2)}, u32[]{:S(2)}) %all-to-all-start.3) | async-done | bytes 131104 | tf_op jit(solution)/shard_map/all_to_all | solution.py:425
  81.6 19.6 %all_to_all.30.got = f32[16,8,128]{2,1,0:T(8,128)S(1)} all-to-all(f32[16,8,128]{2,1,0:T(8,128)S(1)} %shard_map.113), channel_id=1, replica_groups=mesh['dp'=8,'z'=8,'x'=4,'core'=2] {'dp','core'}, dimensions={0} | all-to-all | bytes 131072 | tf_op jit(solution)/shard_map/all_to_all | solution.py:491
  101.1 14.8 %all_to_all.31.got = f32[32,16,128]{2,1,0:T(8,128)S(1)} all-to-all(f32[32,16,128]{2,1,0:T(8,128)S(1)} %shard_map.114), channel_id=1, replica_groups=mesh['dp'=8,'z'=8,'x'=4,'core'=2] {'z','x'}, dimensions={0} | all-to-all | bytes 524288 | tf_op jit(solution)/shard_map/all_to_all | solution.py:425
  116.0 0.8 shard_map.115
  (3 shorter events, 0.1 us)
Async XLA Ops:
  2.6 9.1 %copy-start.3 = (bf16[128,512]{1,0:T(8,128)(2,1)S(1)}, bf16[128,512]{1,0:T(8,128)(2,1)}, u32[]{:S(2)}) copy-start(bf16[128,512]{1,0:T(8,128)(2,1)} %get-tuple-element.42.own) | copy-start | bytes 393220
  2.6 9.0 %copy-start.4 = (bf16[256,128]{1,0:T(8,128)(2,1)S(1)}, bf16[256,128]{1,0:T(8,128)(2,1)}, u32[]{:S(2)}) copy-start(bf16[256,128]{1,0:T(8,128)(2,1)} %get-tuple-element.44.wk) | copy-start | bytes 196612
  13.5 7.7 %copy-start = (bf16[1,128,512]{2,1,0:T(8,128)(2,1)S(1)}, bf16[1,128,512]{2,1,0:T(8,128)(2,1)}, u32[]{:S(2)}) copy-start(bf16[1,128,512]{2,1,0:T(8,128)(2,1)} %param.6) | copy-start | bytes 393220
  13.5 7.7 %copy-start.1 = (bf16[1,128,512]{2,1,0:T(8,128)(2,1)S(1)}, bf16[1,128,512]{2,1,0:T(8,128)(2,1)}, u32[]{:S(2)}) copy-start(bf16[1,128,512]{2,1,0:T(8,128)(2,1)} %param.9) | copy-start | bytes 393220
  13.5 7.7 %copy-start.2 = (bf16[8,64,64]{2,1,0:T(8,128)(2,1)S(1)}, bf16[8,64,64]{2,1,0:T(8,128)(2,1)}, u32[]{:S(2)}) copy-start(bf16[8,64,64]{2,1,0:T(8,128)(2,1)} %param.10) | copy-start | bytes 196612
  13.5 19.2 %all-to-all-start = ((f32[32,16,128]{2,1,0:T(8,128)}), f32[32,16,128]{2,1,0:T(8,128)S(1)}, u32[]{:S(2)}, u32[]{:S(2)}) async-start(f32[32,16,128]{2,1,0:T(8,128)} %get-tuple-element.45), calls=%async_computation | async-start | bytes 524288 | tf_op jit(solution)/shard_map/all_to_all | solution.py:425
  34.4 15.1 %all-to-all-start.1 = ((f32[32,16,128]{2,1,0:T(8,128)}), f32[32,16,128]{2,1,0:T(8,128)S(1)}, u32[]{:S(2)}, u32[]{:S(2)}) async-start(f32[32,16,128]{2,1,0:T(8,128)} %get-tuple-element.56), calls=%async_computation.1 | async-start | bytes 524288 | tf_op jit(solution)/shard_map/all_to_all | solution.py:425
  40.9 0.8 copy-start.5
  41.7 0.7 copy-start.7
  50.9 15.6 %all-to-all-start.2 = ((f32[32,16,128]{2,1,0:T(8,128)}), f32[32,16,128]{2,1,0:T(8,128)S(1)}, u32[]{:S(2)}, u32[]{:S(2)}) async-start(f32[32,16,128]{2,1,0:T(8,128)} %get-tuple-element.66), calls=%async_computation.2 | async-start | bytes 524288 | tf_op jit(solution)/shard_map/all_to_all | solution.py:425
  56.1 1.0 copy-start.6
  68.0 4.1 %copy-start.8 = (f32[256,256]{1,0:T(8,128)S(1)}, f32[256,256]{1,0:T(8,128)}, u32[]{:S(2)}) copy-start(f32[256,256]{1,0:T(8,128)} %copy-done.7) | copy-start | bytes 786436
  68.0 13.5 %all-to-all-start.3 = ((f32[32,8,128]{2,1,0:T(8,128)}), f32[32,8,128]{2,1,0:T(8,128)S(1)}, u32[]{:S(2)}, u32[]{:S(2)}) async-start(f32[32,8,128]{2,1,0:T(8,128)} %get-tuple-element.75), calls=%async_computation.3 | async-start | bytes 262144 | tf_op jit(solution)/shard_map/all_to_all | solution.py:425

commit v6 on v5

--- a/solution.py
+++ b/solution.py
@@ -487,7 +487,7 @@
         finish_kernel, outs + [sums], whole_q, whole, across(send)
     )
     others = sizes["dp"] * sizes["core"]
-    (send,) = call(sum_kernel, [((others, rows, LANES), F32)], got, token)
+    (send,) = call(sum_kernel, [((others, rows, LANES), F32)], got, send)
     got = lax.all_to_all(send, ("dp", "core"), 0, 0)
     (send,) = call(sum_cores_kernel, [((chips, 2 * rows, LANES), F32)], got)
     got = exchange(send)

time: 117 us -> 119 us (1.017)
  blocking collectives: 51.6 us -> 33.4 us
  waiting for transfers between devices: 22.6 us -> 38.7 us
  starting transfers between devices: 21.5 us -> 25.4 us
    all_to_all x4 -> x5, waiting for transfers between devices: 22.6 us -> 38.7 us  [exchange(): return lax.all_to_all(a, CHIPS, 0, 0)]
    all_to_all x1 -> x0, blocking collectives: 14.8 us -> none  [exchange(): return lax.all_to_all(a, CHIPS, 0, 0)]
    all_to_all x4 -> x5, starting transfers between devices: 21.5 us -> 25.4 us  [exchange(): return lax.all_to_all(a, CHIPS, 0, 0)]
    all_gather x3, blocking collectives: 17.2 us -> 13.9 us  [across(): return lax.all_gather(a, 'core')]
  transfers between devices with their start and end apart: 4 -> 5, of which waited for: 4 -> 5; matrix products, arithmetic and copies ran while one was open for 0% -> 0% of each run, Pallas kernels for 7% -> 7%
where the time goes in v6:
time: 119 us
  waiting for transfers between devices  38.7 us (33%)
  blocking collectives  33.4 us (28%)
  starting transfers between devices  25.4 us (21%)
  Pallas kernels  18.5 us (16%)
  local copies, waits for them, and re-layouts  1.87 us (2%)
    all_to_all x5, waiting for transfers between devices, exchange(): return lax.all_to_all(a, CHIPS, 0, 0)  38.7 us
    all_to_all x5, starting transfers between devices, exchange(): return lax.all_to_all(a, CHIPS, 0, 0)  25.4 us
    all_to_all x1, blocking collectives, per_device(): got = lax.all_to_all(send, ('dp', 'core'), 0, 0)  19.5 us
    pallas_call x15, Pallas kernels, call(): pl.pallas_call(kernel, out_shape=shapes, in_specs=[pl.BlockSpec(memory_sp...  18.5 us
    all_gather x3, blocking collectives, across(): return lax.all_gather(a, 'core')  13.9 us
  transfers between devices with their start and end apart: 5, of which 5 were waited for; matrix products, arithmetic and copies ran while one was open for 0% of the time, Pallas kernels for 7%

profile of v6, /device:TPU:1, one launch (start us, length us, event | category | flops | bytes accessed | tf_op | source)
XLA Modules:
  0.0 118.6 jit_solution(10406393584028826815)
XLA Ops:
  0.6 1.9 %shard_map.101 = (f32[128,512]{1,0:T(8,128)}, bf16[128,512]{1,0:T(8,128)(2,1)}, bf16[256,128]{1,0:T(8,128)(2,1)}) custom-call(bf16[128,512]{1,0:T(8,128)(2,1)} %bitcast.18, bf16[128,512]{1,0:T(8,128)(2,1)} %bitcast.19, bf16[512,64]{1,0:T(8,128)(2,1)} %bitcast.20), custom_call_target="tpu_custom_call" | custom-call | flops 100000000 | bytes 786432 | tf_op jit(solution)/shard_map/pallas_call | solution.py:398
  2.6 0.0 copy-start.3
  2.6 0.0 copy-start.4
  2.6 9.0 %all-gather = f32[256,512]{1,0:T(8,128)S(1)} all-gather(f32[128,512]{1,0:T(8,128)} %get-tuple-element.42), channel_id=2, replica_groups=mesh['dp'=8,'z'=8,'x'=4,'core'=2] {'core'}, dimensions={0}, use_global_device_ids=true | all-gather | bytes 786432 | tf_op jit(solution)/shard_map/all_gather | solution.py:422
  11.6 0.0 copy-done.3
  11.6 0.0 copy-done.4
  11.6 1.8 %shard_map.102 = (f32[32,16,128]{2,1,0:T(8,128)}, bf16[256,256]{1,0:T(8,128)(2,1)S(1)}, bf16[256,256]{1,0:T(8,128)(2,1)S(1)}, bf16[256,512]{1,0:T(8,128)(2,1)S(1)}, bf16[256,512]{1,0:T(8,128)(2,1)S(1)}) custom-call(bf16[128,512]{1,0:T(8,128)(2,1)S(1)} %copy-done.3, f32[2,128,512]{2,1,0:T(8,128)S(1)} %bitcast.13, bf16[256,128]{1,0:T(8,128)(2,1)S(1)} %copy-done.4), custom_call_target="tpu_custom_call" | custom-call | flops 100000000 | bytes 1769472 | tf_op jit(solution)/shard_map/pallas_call | solution.py:398
  13.5 0.0 copy-start
  13.5 0.0 copy-start.1
  13.5 0.0 copy-start.2
  13.5 7.6 %all-to-all-start = ((f32[32,16,128]{2,1,0:T(8,128)}), f32[32,16,128]{2,1,0:T(8,128)S(1)}, u32[]{:S(2)}, u32[]{:S(2)}) async-start(f32[32,16,128]{2,1,0:T(8,128)} %get-tuple-element.44), calls=%async_computation | async-start | bytes 524288 | tf_op jit(solution)/shard_map/all_to_all | solution.py:425
  21.1 0.0 copy-done
  21.1 0.0 copy-done.1
  21.2 0.0 copy-done.2
  21.2 0.3 shard_map.103
  21.5 2.5 %all-gather.1 = f32[256,512]{1,0:T(8,128)S(1)} all-gather(f32[128,512]{1,0:T(8,128)S(1)} %get-tuple-element.46), channel_id=3, replica_groups=mesh['dp'=8,'z'=8,'x'=4,'core'=2] {'core'}, dimensions={0}, use_global_device_ids=true | all-gather | bytes 786432 | tf_op jit(solution)/shard_map/all_gather | solution.py:422
  24.0 2.4 %shard_map.104 = (bf16[256,256]{1,0:T(8,128)(2,1)S(1)}, bf16[256,256]{1,0:T(8,128)(2,1)S(1)}, bf16[256,512]{1,0:T(8,128)(2,1)S(1)}, bf16[256,512]{1,0:T(8,128)(2...) custom-call(bf16[128,512]{1,0:T(8,128)(2,1)S(1)} %get-tuple-element.45.own, f32[2,128,512]{2,1,0:T(8,128)S(1)} %bitcast.14, ...), custom_call_target="tpu_custom_call" | custom-call | flops 1000000000 | bytes 2686976 | tf_op jit(solution)/shard_map/pallas_call | solution.py:398
  26.4 6.3 %all-to-all-done.got = f32[32,16,128]{2,1,0:T(8,128)S(1)} async-done(((f32[32,16,128]{2,1,0:T(8,128)}), f32[32,16,128]{2,1,0:T(8,128)S(1)}, u32[]{:S(2)}, u32[]{:S(2)}) %all-to-all-start) | async-done | bytes 262176 | tf_op jit(solution)/shard_map/all_to_all | solution.py:425
  32.7 1.7 %shard_map.105 = (f32[32,16,128]{2,1,0:T(8,128)}, f32[256,256]{1,0:T(8,128)S(1)}, f32[256,256]{1,0:T(8,128)S(1)}, f32[8,128]{1,0:T(8,128)S(1)}) custom-call(f32[32,16,128]{2,1,0:T(8,128)S(1)} %all-to-all-done.got, bf16[256,256]{1,0:T(8,128)(2,1)S(1)} %get-tuple-element.51.g, bf16[256,512]{1,0:T(8,128)(2,1)S(1)} %get-tuple-element.52.qh, ...), custom_call_target="tpu_custom_call" | custom-call | flops 100000000 | bytes 1970176 | tf_op jit(solution)/shard_map/pallas_call | solution.py:398
  34.4 4.6 %all-to-all-start.1 = ((f32[32,16,128]{2,1,0:T(8,128)}), f32[32,16,128]{2,1,0:T(8,128)S(1)}, u32[]{:S(2)}, u32[]{:S(2)}) async-start(f32[32,16,128]{2,1,0:T(8,128)} %get-tuple-element.55), calls=%async_computation.1 | async-start | bytes 524288 | tf_op jit(solution)/shard_map/all_to_all | solution.py:425
  39.0 1.9 %shard_map.106 = (f32[256,512]{1,0:T(8,128)S(1)}, f32[256,256]{1,0:T(8,128)S(1)}, f32[8,128]{1,0:T(8,128)S(1)}) custom-call(bf16[256,256]{1,0:T(8,128)(2,1)S(1)} %get-tuple-element.48.v, bf16[256,512]{1,0:T(8,128)(2,1)S(1)} %get-tuple-element.52.qh, bf16[256,512]{1,0:T(8,128)(2,1)S(1)} %get-tuple-element.53.ql, bf16[256,512]{1,0:T(8,128)(2,1)S(1)} %get-tuple-element.49.kh, ...), custom_call_target="tpu_custom_call" | custom-call | flops 1000000000 | bytes 2232320 | tf_op jit(solution)/shard_map/pallas_call | solution.py:398
  40.9 0.0 copy-start.5
  40.9 0.8 copy-done.5
  41.7 0.0 copy-start.7
  41.7 7.8 %all-to-all-done.1.got = f32[32,16,128]{2,1,0:T(8,128)S(1)} async-done(((f32[32,16,128]{2,1,0:T(8,128)}), f32[32,16,128]{2,1,0:T(8,128)S(1)}, u32[]{:S(2)}, u32[]{:S(2)}) %all-to-all-start.1) | async-done | bytes 262176 | tf_op jit(solution)/shard_map/all_to_all | solution.py:425
  49.5 1.4 %shard_map.107 = (f32[32,16,128]{2,1,0:T(8,128)}, f32[256,256]{1,0:T(8,128)S(1)}) custom-call(f32[32,16,128]{2,1,0:T(8,128)S(1)} %all-to-all-done.1.got, bf16[256,256]{1,0:T(8,128)(2,1)S(1)} %get-tuple-element.51.g, bf16[256,512]{1,0:T(8,128)(2,1)S(1)} %get-tuple-element.52.qh, bf16[256,512]{1,0:T(8,128)(2,1)S(1)} %get-tuple-element.53.ql, ...), custom_call_target="tpu_custom_call" | custom-call | flops 100000000 | bytes 1970176 | tf_op jit(solution)/shard_map/pallas_call | solution.py:398
  50.9 0.0 copy-done.7
  50.9 5.2 %all-to-all-start.2 = ((f32[32,16,128]{2,1,0:T(8,128)}), f32[32,16,128]{2,1,0:T(8,128)S(1)}, u32[]{:S(2)}, u32[]{:S(2)}) async-start(f32[32,16,128]{2,1,0:T(8,128)} %get-tuple-element.65), calls=%async_computation.2 | async-start | bytes 524288 | tf_op jit(solution)/shard_map/all_to_all | solution.py:425
  56.1 0.0 copy-start.6
  56.1 1.0 copy-done.6
  57.2 2.6 %shard_map.108 = (f32[256,256]{1,0:T(8,128)S(1)}, f32[256,128]{1,0:T(8,128)S(1)}, f32[256,512]{1,0:T(8,128)S(1)}) custom-call(f32[32,16,128]{2,1,0:T(8,128)S(1)} %all-to-all-done.1.got, bf16[256,256]{1,0:T(8,128)(2,1)S(1)} %get-tuple-element.56.q, bf16[256,256]{1,0:T(8,128)(2,1)S(1)} %get-tuple-element.48.v, bf16[256,128]{1,0:T(8,128)(2,1)S(1)} %get-tuple-element.47.wq, ...), custom_call_target="tpu_custom_call" | custom-call | flops 1000000000 | bytes 3608576 | tf_op jit(solution)/shard_map/pallas_call | solution.py:398
  59.7 6.8 %all-to-all-done.2.got = f32[32,16,128]{2,1,0:T(8,128)S(1)} async-done(((f32[32,16,128]{2,1,0:T(8,128)}), f32[32,16,128]{2,1,0:T(8,128)S(1)}, u32[]{:S(2)}, u32[]{:S(2)}) %all-to-all-start.2) | async-done | bytes 262176 | tf_op jit(solution)/shard_map/all_to_all | solution.py:425
  66.5 1.6 %shard_map.109 = (f32[32,8,128]{2,1,0:T(8,128)}, f32[256,256]{1,0:T(8,128)S(1)}) custom-call(f32[32,16,128]{2,1,0:T(8,128)S(1)} %all-to-all-done.2.got, bf16[256,256]{1,0:T(8,128)(2,1)S(1)} %get-tuple-element.67.k, bf16[256,256]{1,0:T(8,128)(2,1)S(1)} %get-tuple-element.48.v, bf16[256,512]{1,0:T(8,128)(2,1)S(1)} %get-tuple-element.49.kh, ...), custom_call_target="tpu_custom_call" | custom-call | flops 100000000 | bytes 2097152 | tf_op jit(solution)/shard_map/pallas_call | solution.py:398
  68.1 0.0 copy-start.8
  68.1 4.1 %all-to-all-start.3 = ((f32[32,8,128]{2,1,0:T(8,128)}), f32[32,8,128]{2,1,0:T(8,128)S(1)}, u32[]{:S(2)}, u32[]{:S(2)}) async-start(f32[32,8,128]{2,1,0:T(8,128)} %get-tuple-element.74), calls=%async_computation.3 | async-start | bytes 262144 | tf_op jit(solution)/shard_map/all_to_all | solution.py:425
  72.2 0.0 copy-done.8
  72.2 0.4 shard_map.110.second
  72.7 8.9 %all-to-all-done.3.got = f32[32,8,128]{2,1,0:T(8,128)S(1)} async-done(((f32[32,8,128]{2,1,0:T(8,128)}), f32[32,8,128]{2,1,0:T(8,128)S(1)}, u32[]{:S(2)}, u32[]{:S(2)}) %all-to-all-start.3) | async-done | bytes 131104 | tf_op jit(solution)/shard_map/all_to_all | solution.py:425
  81.6 19.5 %all_to_all.30.got = f32[16,8,128]{2,1,0:T(8,128)S(1)} all-to-all(f32[16,8,128]{2,1,0:T(8,128)S(1)} %shard_map.113), channel_id=1, replica_groups=mesh['dp'=8,'z'=8,'x'=4,'core'=2] {'dp','core'}, dimensions={0} | all-to-all | bytes 131072 | tf_op jit(solution)/shard_map/all_to_all | solution.py:491
  101.1 0.7 shard_map.114
  101.9 3.9 %all-to-all-start.5 = ((f32[32,16,128]{2,1,0:T(8,128)}), f32[32,16,128]{2,1,0:T(8,128)S(1)}, u32[]{:S(2)}, u32[]{:S(2)}) async-start(f32[32,16,128]{2,1,0:T(8,128)} %shard_map.114), calls=%async_computation.5 | async-start | bytes 524288 | tf_op jit(solution)/shard_map/all_to_all | solution.py:425
  105.7 2.4 %all-gather.2 = f32[256,768]{1,0:T(8,128)S(1)} all-gather(f32[128,768]{1,0:T(8,128)S(1)} %shard_map.111.rest_0_), channel_id=4, replica_groups=mesh['dp'=8,'z'=8,'x'=4,'core'=2] {'core'}, dimensions={0}, use_global_device_ids=true | all-gather | bytes 1179648 | tf_op jit(solution)/shard_map/all_gather | solution.py:422
  108.1 0.8 shard_map.112
  108.9 8.9 %all-to-all-done.5.got = f32[32,16,128]{2,1,0:T(8,128)S(1)} async-done(((f32[32,16,128]{2,1,0:T(8,128)}), f32[32,16,128]{2,1,0:T(8,128)S(1)}, u32[]{:S(2)}, u32[]{:S(2)}) %all-to-all-start.5) | async-done | bytes 262176 | tf_op jit(solution)/shard_map/all_to_all | solution.py:425
  117.8 0.8 shard_map.115
  (2 shorter events, 0.1 us)
Async XLA Ops:
  2.6 9.1 %copy-start.3 = (bf16[128,512]{1,0:T(8,128)(2,1)S(1)}, bf16[128,512]{1,0:T(8,128)(2,1)}, u32[]{:S(2)}) copy-start(bf16[128,512]{1,0:T(8,128)(2,1)} %get-tuple-element.41.own) | copy-start | bytes 393220
  2.6 9.0 %copy-start.4 = (bf16[256,128]{1,0:T(8,128)(2,1)S(1)}, bf16[256,128]{1,0:T(8,128)(2,1)}, u32[]{:S(2)}) copy-start(bf16[256,128]{1,0:T(8,128)(2,1)} %get-tuple-element.43.wk) | copy-start | bytes 196612
  13.5 7.7 %copy-start = (bf16[1,128,512]{2,1,0:T(8,128)(2,1)S(1)}, bf16[1,128,512]{2,1,0:T(8,128)(2,1)}, u32[]{:S(2)}) copy-start(bf16[1,128,512]{2,1,0:T(8,128)(2,1)} %param.6) | copy-start | bytes 393220
  13.5 7.7 %copy-start.1 = (bf16[1,128,512]{2,1,0:T(8,128)(2,1)S(1)}, bf16[1,128,512]{2,1,0:T(8,128)(2,1)}, u32[]{:S(2)}) copy-start(bf16[1,128,512]{2,1,0:T(8,128)(2,1)} %param.9) | copy-start | bytes 393220
  13.5 7.7 %copy-start.2 = (bf16[8,64,64]{2,1,0:T(8,128)(2,1)S(1)}, bf16[8,64,64]{2,1,0:T(8,128)(2,1)}, u32[]{:S(2)}) copy-start(bf16[8,64,64]{2,1,0:T(8,128)(2,1)} %param.10) | copy-start | bytes 196612
  13.5 19.2 %all-to-all-start = ((f32[32,16,128]{2,1,0:T(8,128)}), f32[32,16,128]{2,1,0:T(8,128)S(1)}, u32[]{:S(2)}, u32[]{:S(2)}) async-start(f32[32,16,128]{2,1,0:T(8,128)} %get-tuple-element.44), calls=%async_computation | async-start | bytes 524288 | tf_op jit(solution)/shard_map/all_to_all | solution.py:425
  34.4 15.1 %all-to-all-start.1 = ((f32[32,16,128]{2,1,0:T(8,128)}), f32[32,16,128]{2,1,0:T(8,128)S(1)}, u32[]{:S(2)}, u32[]{:S(2)}) async-start(f32[32,16,128]{2,1,0:T(8,128)} %get-tuple-element.55), calls=%async_computation.1 | async-start | bytes 524288 | tf_op jit(solution)/shard_map/all_to_all | solution.py:425
  40.9 0.8 copy-start.5
  41.7 9.2 %copy-start.7 = (f32[256,256]{1,0:T(8,128)}, f32[256,256]{1,0:T(8,128)S(1)}, u32[]{:S(2)}) copy-start(f32[256,256]{1,0:T(8,128)S(1)} %get-tuple-element.66.gvl) | copy-start | bytes 786436
  50.9 15.6 %all-to-all-start.2 = ((f32[32,16,128]{2,1,0:T(8,128)}), f32[32,16,128]{2,1,0:T(8,128)S(1)}, u32[]{:S(2)}, u32[]{:S(2)}) async-start(f32[32,16,128]{2,1,0:T(8,128)} %get-tuple-element.65), calls=%async_computation.2 | async-start | bytes 524288 | tf_op jit(solution)/shard_map/all_to_all | solution.py:425
  56.1 1.0 copy-start.6
  68.1 4.1 %copy-start.8 = (f32[256,256]{1,0:T(8,128)S(1)}, f32[256,256]{1,0:T(8,128)}, u32[]{:S(2)}) copy-start(f32[256,256]{1,0:T(8,128)} %copy-done.7) | copy-start | bytes 786436
  68.1 13.5 %all-to-all-start.3 = ((f32[32,8,128]{2,1,0:T(8,128)}), f32[32,8,128]{2,1,0:T(8,128)S(1)}, u32[]{:S(2)}, u32[]{:S(2)}) async-start(f32[32,8,128]{2,1,0:T(8,128)} %get-tuple-element.74), calls=%async_computation.3 | async-start | bytes 262144 | tf_op jit(solution)/shard_map/all_to_all | solution.py:425
  101.9 16.0 %all-to-all-start.5 = ((f32[32,16,128]{2,1,0:T(8,128)}), f32[32,16,128]{2,1,0:T(8,128)S(1)}, u32[]{:S(2)}, u32[]{:S(2)}) async-start(f32[32,16,128]{2,1,0:T(8,128)} %shard_map.114), calls=%async_computation.5 | async-start | bytes 524288 | tf_op jit(solution)/shard_map/all_to_all | solution.py:425

commit v7 on v6

--- a/solution.py
+++ b/solution.py
@@ -334,7 +334,7 @@
     send[...] = jnp.concatenate(out, 0).reshape(chips, rows, LANES)
 
 
-def sixth_kernel(got, wk, kh, kl, gvl, dz, whole):
+def sixth_kernel(got, wk, kh, kl, gvl, dz, _, whole):
     rows = WIDE // got.shape[0]
     later = got[:, :rows, :].reshape(WIDE, LANES)
     for p in range(PAIRS):
@@ -373,7 +373,7 @@
     send[...] = jnp.broadcast_to(total[None], send.shape)
 
 
-def sum_cores_kernel(got, send):
+def sum_cores_kernel(got, _, send):
     acc = [got[0], got[1]]
     for m in range(2, got.shape[0]):
         acc[m % 2] = acc[m % 2] + got[m]
@@ -478,18 +478,21 @@
         third, k2, v2, kh, kl, gkl, gq_map,
     )
     got = exchange(send)
+    others = sizes["dp"] * sizes["core"]
+    (partial,) = call(sum_kernel, [((others, rows, LANES), F32)], got)
     (whole,) = call(
-        sixth_kernel, [((BLOCK, 2 * WIDE), F32)], third, wk, kh, kl, gvl, dz, flops=10**9
+        sixth_kernel,
+        [((BLOCK, 2 * WIDE), F32)],
+        third, wk, kh, kl, gvl, dz, partial,
+        flops=10**9,
     )
     (send,) = call(theirs_kernel, [((TOK, 3 * WIDE), F32)], whole_q, whole)
     outs = [((TOK, 2 * WIDE), BF16)] * 3
     grad_q, grad_k, grad_v, token = call(
         finish_kernel, outs + [sums], whole_q, whole, across(send)
     )
-    others = sizes["dp"] * sizes["core"]
-    (send,) = call(sum_kernel, [((others, rows, LANES), F32)], got, send)
-    got = lax.all_to_all(send, ("dp", "core"), 0, 0)
-    (send,) = call(sum_cores_kernel, [((chips, 2 * rows, LANES), F32)], got)
+    got = lax.all_to_all(partial, ("dp", "core"), 0, 0)
+    (send,) = call(sum_cores_kernel, [((chips, 2 * rows, LANES), F32)], got, token)
     got = exchange(send)
     scale = float(BLOCK * chips * sizes["dp"]) ** (-0.5)
     heads = ((8, HALF, HALF), BF16)

time: 119 us -> 117 us (0.983)
  waiting for transfers between devices: 38.7 us -> 23.5 us
  blocking collectives: 33.4 us -> 41.8 us
  starting transfers between devices: 25.4 us -> 29 us
    all_to_all x5 -> x3, waiting for transfers between devices: 38.7 us -> 20.2 us  [exchange(): return lax.all_to_all(a, CHIPS, 0, 0)]
    all_to_all x0 -> x1, starting transfers between devices: none -> 11.6 us  [per_device(): got = lax.all_to_all(partial, ('dp', 'core'), 0, 0)]
    all_to_all x1 -> x2, blocking collectives: 19.5 us -> 27.9 us  [exchange(): return lax.all_to_all(a, CHIPS, 0, 0)]
    all_to_all x5 -> x3, starting transfers between devices: 25.4 us -> 17.4 us  [exchange(): return lax.all_to_all(a, CHIPS, 0, 0)]
    all_to_all x0 -> x1, waiting for transfers between devices: none -> 3.29 us  [per_device(): got = lax.all_to_all(partial, ('dp', 'core'), 0, 0)]
  transfers between devices with their start and end apart: 5 -> 4, of which waited for: 5 -> 4; matrix products, arithmetic and copies ran while one was open for 0% -> 0% of each run, Pallas kernels for 7% -> 8%
where the time goes in v7:
time: 117 us; the launch traced here: 116 us
  blocking collectives  41.8 us (36%)
  starting transfers between devices  29 us (25%)
  waiting for transfers between devices  23.5 us (20%)
  Pallas kernels  18.6 us (16%)
  local copies, waits for them, and re-layouts  2.57 us (2%)
    all_to_all x2, blocking collectives, exchange(): return lax.all_to_all(a, CHIPS, 0, 0)  27.9 us
    all_to_all x3, waiting for transfers between devices, exchange(): return lax.all_to_all(a, CHIPS, 0, 0)  20.2 us
    pallas_call x15, Pallas kernels, call(): pl.pallas_call(kernel, out_shape=shapes, in_specs=[pl.BlockSpec(memory_sp...  18.6 us
    all_to_all x3, starting transfers between devices, exchange(): return lax.all_to_all(a, CHIPS, 0, 0)  17.4 us
    all_gather x3, blocking collectives, across(): return lax.all_gather(a, 'core')  13.9 us
    all_to_all x1, starting transfers between devices, per_device(): got = lax.all_to_all(partial, ('dp', 'core'), 0, 0)  11.6 us
    all_to_all x1, waiting for transfers between devices, per_device(): got = lax.all_to_all(partial, ('dp', 'core'), 0, 0)  3.29 us
    unnamed x18, local copies, waits for them, and re-layouts  2.57 us
  transfers between devices with their start and end apart: 4, of which 4 were waited for; matrix products, arithmetic and copies ran while one was open for 0% of the time, Pallas kernels for 8%

profile of v7, /device:TPU:1, one launch (start us, length us, event | category | flops | bytes accessed | tf_op | source)
XLA Modules:
  0.0 116.3 jit_solution(16855091149197391747)
XLA Ops:
  0.6 1.9 %shard_map.101 = (f32[128,512]{1,0:T(8,128)}, bf16[128,512]{1,0:T(8,128)(2,1)}, bf16[256,128]{1,0:T(8,128)(2,1)}) custom-call(bf16[128,512]{1,0:T(8,128)(2,1)} %bitcast.18, bf16[128,512]{1,0:T(8,128)(2,1)} %bitcast.19, bf16[512,64]{1,0:T(8,128)(2,1)} %bitcast.20), custom_call_target="tpu_custom_call" | custom-call | flops 100000000 | bytes 786432 | tf_op jit(solution)/shard_map/pallas_call | solution.py:398
  2.6 0.0 copy-start.3
  2.6 0.0 copy-start.4
  2.6 9.0 %all-gather = f32[256,512]{1,0:T(8,128)S(1)} all-gather(f32[128,512]{1,0:T(8,128)} %get-tuple-element.43), channel_id=2, replica_groups=mesh['dp'=8,'z'=8,'x'=4,'core'=2] {'core'}, dimensions={0}, use_global_device_ids=true | all-gather | bytes 786432 | tf_op jit(solution)/shard_map/all_gather | solution.py:422
  11.6 0.0 copy-done.3
  11.6 0.0 copy-done.4
  11.6 1.8 %shard_map.102 = (f32[32,16,128]{2,1,0:T(8,128)}, bf16[256,256]{1,0:T(8,128)(2,1)S(1)}, bf16[256,256]{1,0:T(8,128)(2,1)S(1)}, bf16[256,512]{1,0:T(8,128)(2,1)S(1)}, bf16[256,512]{1,0:T(8,128)(2,1)S(1)}) custom-call(bf16[128,512]{1,0:T(8,128)(2,1)S(1)} %copy-done.3, f32[2,128,512]{2,1,0:T(8,128)S(1)} %bitcast.13, bf16[256,128]{1,0:T(8,128)(2,1)S(1)} %copy-done.4), custom_call_target="tpu_custom_call" | custom-call | flops 100000000 | bytes 1769472 | tf_op jit(solution)/shard_map/pallas_call | solution.py:398
  13.5 0.0 copy-start
  13.5 0.0 copy-start.1
  13.5 0.0 copy-start.2
  13.5 7.6 %all-to-all-start = ((f32[32,16,128]{2,1,0:T(8,128)}), f32[32,16,128]{2,1,0:T(8,128)S(1)}, u32[]{:S(2)}, u32[]{:S(2)}) async-start(f32[32,16,128]{2,1,0:T(8,128)} %get-tuple-element.45), calls=%async_computation | async-start | bytes 524288 | tf_op jit(solution)/shard_map/all_to_all | solution.py:425
  21.1 0.0 copy-done
  21.1 0.0 copy-done.1
  21.1 0.0 copy-done.2
  21.2 0.3 shard_map.103
  21.5 2.5 %all-gather.1 = f32[256,512]{1,0:T(8,128)S(1)} all-gather(f32[128,512]{1,0:T(8,128)S(1)} %get-tuple-element.47), channel_id=3, replica_groups=mesh['dp'=8,'z'=8,'x'=4,'core'=2] {'core'}, dimensions={0}, use_global_device_ids=true | all-gather | bytes 786432 | tf_op jit(solution)/shard_map/all_gather | solution.py:422
  24.0 2.4 %shard_map.104 = (bf16[256,256]{1,0:T(8,128)(2,1)S(1)}, bf16[256,256]{1,0:T(8,128)(2,1)S(1)}, bf16[256,512]{1,0:T(8,128)(2,1)S(1)}, bf16[256,512]{1,0:T(8,128)(2...) custom-call(bf16[128,512]{1,0:T(8,128)(2,1)S(1)} %get-tuple-element.46.own, f32[2,128,512]{2,1,0:T(8,128)S(1)} %bitcast.14, ...), custom_call_target="tpu_custom_call" | custom-call | flops 1000000000 | bytes 2686976 | tf_op jit(solution)/shard_map/pallas_call | solution.py:398
  26.4 6.3 %all-to-all-done.got = f32[32,16,128]{2,1,0:T(8,128)S(1)} async-done(((f32[32,16,128]{2,1,0:T(8,128)}), f32[32,16,128]{2,1,0:T(8,128)S(1)}, u32[]{:S(2)}, u32[]{:S(2)}) %all-to-all-start) | async-done | bytes 262176 | tf_op jit(solution)/shard_map/all_to_all | solution.py:425
  32.7 1.7 %shard_map.105 = (f32[32,16,128]{2,1,0:T(8,128)}, f32[256,256]{1,0:T(8,128)S(1)}, f32[256,256]{1,0:T(8,128)S(1)}, f32[8,128]{1,0:T(8,128)S(1)}) custom-call(f32[32,16,128]{2,1,0:T(8,128)S(1)} %all-to-all-done.got, bf16[256,256]{1,0:T(8,128)(2,1)S(1)} %get-tuple-element.52.g, bf16[256,512]{1,0:T(8,128)(2,1)S(1)} %get-tuple-element.53.qh, ...), custom_call_target="tpu_custom_call" | custom-call | flops 100000000 | bytes 1970176 | tf_op jit(solution)/shard_map/pallas_call | solution.py:398
  34.4 4.6 %all-to-all-start.1 = ((f32[32,16,128]{2,1,0:T(8,128)}), f32[32,16,128]{2,1,0:T(8,128)S(1)}, u32[]{:S(2)}, u32[]{:S(2)}) async-start(f32[32,16,128]{2,1,0:T(8,128)} %get-tuple-element.56), calls=%async_computation.1 | async-start | bytes 524288 | tf_op jit(solution)/shard_map/all_to_all | solution.py:425
  39.0 1.9 %shard_map.106 = (f32[256,512]{1,0:T(8,128)S(1)}, f32[256,256]{1,0:T(8,128)S(1)}, f32[8,128]{1,0:T(8,128)S(1)}) custom-call(bf16[256,256]{1,0:T(8,128)(2,1)S(1)} %get-tuple-element.49.v, bf16[256,512]{1,0:T(8,128)(2,1)S(1)} %get-tuple-element.53.qh, bf16[256,512]{1,0:T(8,128)(2,1)S(1)} %get-tuple-element.54.ql, bf16[256,512]{1,0:T(8,128)(2,1)S(1)} %get-tuple-element.50.kh, ...), custom_call_target="tpu_custom_call" | custom-call | flops 1000000000 | bytes 2232320 | tf_op jit(solution)/shard_map/pallas_call | solution.py:398
  40.9 0.0 copy-start.5
  40.9 0.8 copy-done.5
  41.7 0.0 copy-start.7
  41.7 0.7 copy-done.7
  42.4 7.1 %all-to-all-done.1.got = f32[32,16,128]{2,1,0:T(8,128)S(1)} async-done(((f32[32,16,128]{2,1,0:T(8,128)}), f32[32,16,128]{2,1,0:T(8,128)S(1)}, u32[]{:S(2)}, u32[]{:S(2)}) %all-to-all-start.1) | async-done | bytes 262176 | tf_op jit(solution)/shard_map/all_to_all | solution.py:425
  49.5 1.4 %shard_map.107 = (f32[32,16,128]{2,1,0:T(8,128)}, f32[256,256]{1,0:T(8,128)S(1)}) custom-call(f32[32,16,128]{2,1,0:T(8,128)S(1)} %all-to-all-done.1.got, bf16[256,256]{1,0:T(8,128)(2,1)S(1)} %get-tuple-element.52.g, bf16[256,512]{1,0:T(8,128)(2,1)S(1)} %get-tuple-element.53.qh, bf16[256,512]{1,0:T(8,128)(2,1)S(1)} %get-tuple-element.54.ql, ...), custom_call_target="tpu_custom_call" | custom-call | flops 100000000 | bytes 1970176 | tf_op jit(solution)/shard_map/pallas_call | solution.py:398
  50.9 5.2 %all-to-all-start.2 = ((f32[32,16,128]{2,1,0:T(8,128)}), f32[32,16,128]{2,1,0:T(8,128)S(1)}, u32[]{:S(2)}, u32[]{:S(2)}) async-start(f32[32,16,128]{2,1,0:T(8,128)} %get-tuple-element.66), calls=%async_computation.2 | async-start | bytes 524288 | tf_op jit(solution)/shard_map/all_to_all | solution.py:425
  56.1 0.0 copy-start.6
  56.1 1.0 copy-done.6
  57.1 2.6 %shard_map.108 = (f32[256,256]{1,0:T(8,128)S(1)}, f32[256,128]{1,0:T(8,128)S(1)}, f32[256,512]{1,0:T(8,128)S(1)}) custom-call(f32[32,16,128]{2,1,0:T(8,128)S(1)} %all-to-all-done.1.got, bf16[256,256]{1,0:T(8,128)(2,1)S(1)} %get-tuple-element.57.q, bf16[256,256]{1,0:T(8,128)(2,1)S(1)} %get-tuple-element.49.v, bf16[256,128]{1,0:T(8,128)(2,1)S(1)} %get-tuple-element.48.wq, ...), custom_call_target="tpu_custom_call" | custom-call | flops 1000000000 | bytes 3608576 | tf_op jit(solution)/shard_map/pallas_call | solution.py:398
  59.7 6.8 %all-to-all-done.2.got = f32[32,16,128]{2,1,0:T(8,128)S(1)} async-done(((f32[32,16,128]{2,1,0:T(8,128)}), f32[32,16,128]{2,1,0:T(8,128)S(1)}, u32[]{:S(2)}, u32[]{:S(2)}) %all-to-all-start.2) | async-done | bytes 262176 | tf_op jit(solution)/shard_map/all_to_all | solution.py:425
  66.5 0.9 shard_map.109
  67.4 13.1 %all_to_all.30.got = f32[32,8,128]{2,1,0:T(8,128)S(1)} all-to-all(f32[32,8,128]{2,1,0:T(8,128)S(1)} %get-tuple-element.72), channel_id=1, replica_groups=mesh['dp'=8,'z'=8,'x'=4,'core'=2] {'z','x'}, dimensions={0} | all-to-all | bytes 262144 | tf_op jit(solution)/shard_map/all_to_all | solution.py:425
  80.5 0.0 copy-start.8
  80.5 0.7 shard_map.110._
  81.1 11.6 %all-to-all-start.4 = ((f32[16,8,128]{2,1,0:T(8,128)}), f32[16,8,128]{2,1,0:T(8,128)S(1)}, u32[]{:S(2)}, u32[]{:S(2)}) async-start(f32[16,8,128]{2,1,0:T(8,128)} %shard_map.110._), calls=%async_computation.4 | async-start | bytes 131072 | tf_op jit(solution)/shard_map/all_to_all | solution.py:494
  92.8 0.0 copy-done.8
  92.8 1.3 %shard_map.111.second = f32[256,512]{1,0:T(8,128)S(1)} custom-call(f32[32,16,128]{2,1,0:T(8,128)S(1)} %all-to-all-done.2.got, bf16[256,128]{1,0:T(8,128)(2,1)S(1)} %copy-done.4, bf16[256,512]{1,0:T(8,128)(2,1)S(1)} %get-tuple-element.50.kh, bf16[256,512]{1,0:T(8,128)(2,1)S(1)} %get-tuple-element.51.kl, f32[256,256]{1,0:T(8,128)S(1)} %copy-done.8, ...), custom_call_target="tpu_custom_call" | custom-call | flops 1000000000 | bytes 1966080 | tf_op jit(solution)/shard_map/pallas_call | solution.py:398
  94.2 2.4 %all-gather.2 = f32[256,768]{1,0:T(8,128)S(1)} all-gather(f32[128,768]{1,0:T(8,128)S(1)} %shard_map.112), channel_id=4, replica_groups=mesh['dp'=8,'z'=8,'x'=4,'core'=2] {'core'}, dimensions={0}, use_global_device_ids=true | all-gather | bytes 1179648 | tf_op jit(solution)/shard_map/all_gather | solution.py:422
  96.5 0.8 shard_map.113
  97.3 3.3 %all-to-all-done.4.got = f32[16,8,128]{2,1,0:T(8,128)S(1)} async-done(((f32[16,8,128]{2,1,0:T(8,128)}), f32[16,8,128]{2,1,0:T(8,128)S(1)}, u32[]{:S(2)}, u32[]{:S(2)}) %all-to-all-start.4) | async-done | bytes 65568 | tf_op jit(solution)/shard_map/all_to_all | solution.py:494
  100.6 14.8 %all_to_all.31.got = f32[32,16,128]{2,1,0:T(8,128)S(1)} all-to-all(f32[32,16,128]{2,1,0:T(8,128)S(1)} %shard_map.114), channel_id=1, replica_groups=mesh['dp'=8,'z'=8,'x'=4,'core'=2] {'z','x'}, dimensions={0} | all-to-all | bytes 524288 | tf_op jit(solution)/shard_map/all_to_all | solution.py:425
  115.5 0.8 shard_map.115
  (2 shorter events, 0.1 us)
Async XLA Ops:
  2.6 9.1 %copy-start.3 = (bf16[128,512]{1,0:T(8,128)(2,1)S(1)}, bf16[128,512]{1,0:T(8,128)(2,1)}, u32[]{:S(2)}) copy-start(bf16[128,512]{1,0:T(8,128)(2,1)} %get-tuple-element.42.own) | copy-start | bytes 393220
  2.6 9.0 %copy-start.4 = (bf16[256,128]{1,0:T(8,128)(2,1)S(1)}, bf16[256,128]{1,0:T(8,128)(2,1)}, u32[]{:S(2)}) copy-start(bf16[256,128]{1,0:T(8,128)(2,1)} %get-tuple-element.44.wk) | copy-start | bytes 196612
  13.5 7.7 %copy-start = (bf16[1,128,512]{2,1,0:T(8,128)(2,1)S(1)}, bf16[1,128,512]{2,1,0:T(8,128)(2,1)}, u32[]{:S(2)}) copy-start(bf16[1,128,512]{2,1,0:T(8,128)(2,1)} %param.6) | copy-start | bytes 393220
  13.5 7.7 %copy-start.1 = (bf16[1,128,512]{2,1,0:T(8,128)(2,1)S(1)}, bf16[1,128,512]{2,1,0:T(8,128)(2,1)}, u32[]{:S(2)}) copy-start(bf16[1,128,512]{2,1,0:T(8,128)(2,1)} %param.9) | copy-start | bytes 393220
  13.5 7.7 %copy-start.2 = (bf16[8,64,64]{2,1,0:T(8,128)(2,1)S(1)}, bf16[8,64,64]{2,1,0:T(8,128)(2,1)}, u32[]{:S(2)}) copy-start(bf16[8,64,64]{2,1,0:T(8,128)(2,1)} %param.10) | copy-start | bytes 196612
  13.5 19.2 %all-to-all-start = ((f32[32,16,128]{2,1,0:T(8,128)}), f32[32,16,128]{2,1,0:T(8,128)S(1)}, u32[]{:S(2)}, u32[]{:S(2)}) async-start(f32[32,16,128]{2,1,0:T(8,128)} %get-tuple-element.45), calls=%async_computation | async-start | bytes 524288 | tf_op jit(solution)/shard_map/all_to_all | solution.py:425
  34.4 15.1 %all-to-all-start.1 = ((f32[32,16,128]{2,1,0:T(8,128)}), f32[32,16,128]{2,1,0:T(8,128)S(1)}, u32[]{:S(2)}, u32[]{:S(2)}) async-start(f32[32,16,128]{2,1,0:T(8,128)} %get-tuple-element.56), calls=%async_computation.1 | async-start | bytes 524288 | tf_op jit(solution)/shard_map/all_to_all | solution.py:425
  40.9 0.8 copy-start.5
  41.7 0.7 copy-start.7
  50.9 15.6 %all-to-all-start.2 = ((f32[32,16,128]{2,1,0:T(8,128)}), f32[32,16,128]{2,1,0:T(8,128)S(1)}, u32[]{:S(2)}, u32[]{:S(2)}) async-start(f32[32,16,128]{2,1,0:T(8,128)} %get-tuple-element.66), calls=%async_computation.2 | async-start | bytes 524288 | tf_op jit(solution)/shard_map/all_to_all | solution.py:425
  56.1 1.0 copy-start.6
  80.5 12.3 %copy-start.8 = (f32[256,256]{1,0:T(8,128)S(1)}, f32[256,256]{1,0:T(8,128)}, u32[]{:S(2)}) copy-start(f32[256,256]{1,0:T(8,128)} %copy-done.7) | copy-start | bytes 786436
  81.1 19.5 %all-to-all-start.4 = ((f32[16,8,128]{2,1,0:T(8,128)}), f32[16,8,128]{2,1,0:T(8,128)S(1)}, u32[]{:S(2)}, u32[]{:S(2)}) async-start(f32[16,8,128]{2,1,0:T(8,128)} %shard_map.110._), calls=%async_computation.4 | async-start | bytes 131072 | tf_op jit(solution)/shard_map/all_to_all | solution.py:494
